TPU v7x, 32 devices: a whole 2x2x4 slice. The times are simulated.
32 devices in a mesh: fsdp: 8 (over y, x, core), seq: 4 (over z).
Axes of the slice: x: 2, y: 2, z: 4, core: 2. Of those that a mesh axis runs over, the one named last changes fastest.
Arguments:
- frames: bfloat16 [16, 1500, 768], P('fsdp', 'seq'), may hold values from -6 to 6
- cotangent: bfloat16 [16, 1500, 768], P('fsdp', 'seq'), may hold values from -6 to 6
- valid_slots: int32 [16], P('fsdp'), may hold values 0 or 1
- first_gain: bfloat16 [768], P('fsdp'), may hold values from 0.25 to 1.75
- first_shift: bfloat16 [768], P('fsdp'), may hold values from -3 to 3
- query_weight: bfloat16 [768, 768], P('fsdp'), may hold values from -0.21875 to 0.21875
- query_bias: bfloat16 [768], P('fsdp'), may hold values from -3 to 3
- key_weight: bfloat16 [768, 768], P('fsdp'), may hold values from -0.21875 to 0.21875
- value_weight: bfloat16 [768, 768], P('fsdp'), may hold values from -0.21875 to 0.21875
- value_bias: bfloat16 [768], P('fsdp'), may hold values from -3 to 3
- output_weight: bfloat16 [768, 768], P('fsdp'), may hold values from -6 to 6
- output_bias: bfloat16 [768], P('fsdp'), may hold values from -3 to 3
- second_gain: bfloat16 [768], P('fsdp'), may hold values from 0.25 to 1.75
- second_shift: bfloat16 [768], P('fsdp'), may hold values from -3 to 3
- inner_weight: bfloat16 [768, 3072], P('fsdp'), may hold values from -0.21875 to 0.21875
- inner_bias: bfloat16 [3072], P('fsdp'), may hold values from -3 to 3
- outer_weight: bfloat16 [3072, 768], P('fsdp'), may hold values from -0.21875 to 0.21875
- outer_bias: bfloat16 [768], P('fsdp'), may hold values from -3 to 3
Outputs:
- outputs: bfloat16 [16, 1500, 768], P('fsdp', 'seq')
- input_grad: bfloat16 [16, 1500, 768], P('fsdp', 'seq')
- grad_first_gain: float32 [768], P('fsdp')
- grad_first_shift: float32 [768], P('fsdp')
- grad_query_weight: float32 [768, 768], P('fsdp')
- grad_query_bias: float32 [768], P('fsdp')
- grad_key_weight: float32 [768, 768], P('fsdp')
- grad_value_weight: float32 [768, 768], P('fsdp')
- grad_value_bias: float32 [768], P('fsdp')
- grad_output_weight: float32 [768, 768], P('fsdp')
- grad_output_bias: float32 [768], P('fsdp')
- grad_second_gain: float32 [768], P('fsdp')
- grad_second_shift: float32 [768], P('fsdp')
- grad_inner_weight: float32 [768, 3072], P('fsdp')
- grad_inner_bias: float32 [3072], P('fsdp')
- grad_outer_weight: float32 [3072, 768], P('fsdp')
- grad_outer_bias: float32 [768], P('fsdp')
All inputs are finite; a program needn't handle non-finite values. No bound on the sum of `valid_slots` on one device may be relied on, other than what follows from the above.
Results may differ from a plain program's by a relative error of at most 0.012.
The roundings to bfloat16 on the way count: a program that leaves them out, or rounds other values in their place, can miss the bound.
Values may be sent and summed in bfloat16 or wider, within the bound.
A program may use at most 256 MiB of HBM per device.

v0:
```python
import math

import jax
import jax.numpy as jnp
from jax import lax
from jax.sharding import PartitionSpec as P

H = 12
HD = 64


epsilon = 1e-05


def product(left, right):
    return jnp.dot(left, right, preferred_element_type=jnp.float32)


def left_product(left, right):
    return lax.dot_general(
        left, right, (((0,), (0,)), ((), ())), preferred_element_type=jnp.float32
    )


def right_product(left, right):
    return lax.dot_general(
        left, right, (((1,), (1,)), ((), ())), preferred_element_type=jnp.float32
    )


def normalize(rows):
    center = rows - jnp.mean(rows, -1, keepdims=True)
    scale_inv = lax.rsqrt(jnp.mean(center * center, -1, keepdims=True) + epsilon)
    return (center * scale_inv, scale_inv)


def norm_back(grad_norm, gain, normal, scale_inv):
    tilted = grad_norm * gain
    first_mean = jnp.mean(tilted, -1, keepdims=True)
    cross_mean = jnp.mean(tilted * normal, -1, keepdims=True)
    return scale_inv * (tilted - first_mean - normal * cross_mean)


def gelu_slope(value):
    return 0.5 * (1.0 + lax.erf(value * (1.0 / math.sqrt(2.0)))) + value * jnp.exp(
        -0.5 * value * value
    ) * (1.0 / math.sqrt(2.0 * math.pi))


def per_device(
    frames,
    cotangent,
    valid_slots,
    first_gain,
    first_shift,
    query_weight,
    query_bias,
    key_weight,
    value_weight,
    value_bias,
    output_weight,
    output_bias,
    second_gain,
    second_shift,
    inner_weight,
    inner_bias,
    outer_weight,
    outer_bias,
):
    groups = lax.axis_size("seq")
    slots, local, width = frames.shape
    heads_dev = H // groups
    length = local * groups
    rows = slots * local
    factor = HD ** (-0.5)
    attn_fwd = (
        lax.all_gather(first_gain, "fsdp", axis=0, tiled=True),
        lax.all_gather(first_shift, "fsdp", axis=0, tiled=True),
        lax.all_gather(query_weight, "fsdp", axis=0, tiled=True),
        lax.all_gather(query_bias, "fsdp", axis=0, tiled=True),
        lax.all_gather(key_weight, "fsdp", axis=0, tiled=True),
        lax.all_gather(value_weight, "fsdp", axis=0, tiled=True),
        lax.all_gather(value_bias, "fsdp", axis=0, tiled=True),
        lax.all_gather(output_weight, "fsdp", axis=0, tiled=True),
        lax.all_gather(output_bias, "fsdp", axis=0, tiled=True),
    )
    feed_fwd = (
        lax.all_gather(second_gain, "fsdp", axis=0, tiled=True),
        lax.all_gather(second_shift, "fsdp", axis=0, tiled=True),
        lax.all_gather(inner_weight, "fsdp", axis=0, tiled=True),
        lax.all_gather(inner_bias, "fsdp", axis=0, tiled=True),
        lax.all_gather(outer_weight, "fsdp", axis=0, tiled=True),
        lax.all_gather(outer_bias, "fsdp", axis=0, tiled=True),
    )
    (
        gain_one,
        shift_one,
        query_full,
        qbias_full,
        key_full,
        value_full,
        vbias_full,
        output_full,
        obias_full,
    ) = attn_fwd
    gain_two, shift_two, inner_full, ibias_full, outer_full, ubias_full = feed_fwd
    inputs = frames.astype(jnp.float32).reshape(rows, width)
    keep_rows = jnp.repeat(valid_slots.astype(jnp.float32), local)[:, None]
    hat_one, inv_one = normalize(inputs)
    normed1 = (hat_one * gain_one.astype(jnp.float32) + shift_one.astype(jnp.float32)).astype(
        jnp.bfloat16
    )
    query = (product(normed1, query_full) + qbias_full.astype(jnp.float32)).astype(jnp.bfloat16)
    keys = product(normed1, key_full).astype(jnp.bfloat16)
    values = (product(normed1, value_full) + vbias_full.astype(jnp.float32)).astype(jnp.bfloat16)

    def to_heads(block):
        return block.reshape(slots, local, groups, heads_dev * HD)

    def to_frames(block):
        return block.reshape(slots, length, 1, heads_dev * HD)

    head_q, head_k, head_v = (
        lax.all_to_all(to_heads(query), "seq", split_axis=2, concat_axis=1, tiled=True),
        lax.all_to_all(to_heads(keys), "seq", split_axis=2, concat_axis=1, tiled=True),
        lax.all_to_all(to_heads(values), "seq", split_axis=2, concat_axis=1, tiled=True),
    )
    head_q = head_q.reshape(slots, length, heads_dev, HD)
    head_k = head_k.reshape(slots, length, heads_dev, HD)
    head_v = head_v.reshape(slots, length, heads_dev, HD)

    def attend(item):
        slot_q, slot_k, slot_v = item
        scores = (
            jnp.einsum("qhd,khd->hqk", slot_q, slot_k, preferred_element_type=jnp.float32) * factor
        )
        peak = jnp.max(scores, -1, keepdims=True)
        expo = jnp.exp(scores - peak)
        total = jnp.sum(expo, -1, keepdims=True)
        probs = (expo / total).astype(jnp.bfloat16)
        mixed_slot = jnp.einsum(
            "hqk,khd->qhd", probs, slot_v, preferred_element_type=jnp.float32
        ).astype(jnp.bfloat16)
        return (mixed_slot, (peak + jnp.log(total))[..., 0])

    mixed_heads, log_total = lax.map(attend, (head_q, head_k, head_v))
    mixed = lax.all_to_all(
        to_frames(mixed_heads), "seq", split_axis=1, concat_axis=2, tiled=True
    ).reshape(rows, width)
    resid = inputs + product(mixed, output_full) + obias_full.astype(jnp.float32)
    hat_two, inv_two = normalize(resid)
    normed2 = (hat_two * gain_two.astype(jnp.float32) + shift_two.astype(jnp.float32)).astype(
        jnp.bfloat16
    )
    inner = product(normed2, inner_full) + ibias_full.astype(jnp.float32)
    active = jax.nn.gelu(inner, approximate=False).astype(jnp.bfloat16)
    result = (resid + product(active, outer_full) + ubias_full.astype(jnp.float32)) * keep_rows
    outputs = result.astype(jnp.bfloat16).reshape(slots, local, width)
    attn_back = (
        lax.all_gather(first_gain, "fsdp", axis=0, tiled=True),
        lax.all_gather(first_shift, "fsdp", axis=0, tiled=True),
        lax.all_gather(query_weight, "fsdp", axis=0, tiled=True),
        lax.all_gather(query_bias, "fsdp", axis=0, tiled=True),
        lax.all_gather(key_weight, "fsdp", axis=0, tiled=True),
        lax.all_gather(value_weight, "fsdp", axis=0, tiled=True),
        lax.all_gather(value_bias, "fsdp", axis=0, tiled=True),
        lax.all_gather(output_weight, "fsdp", axis=0, tiled=True),
        lax.all_gather(output_bias, "fsdp", axis=0, tiled=True),
    )
    feed_back = (
        lax.all_gather(second_gain, "fsdp", axis=0, tiled=True),
        lax.all_gather(second_shift, "fsdp", axis=0, tiled=True),
        lax.all_gather(inner_weight, "fsdp", axis=0, tiled=True),
        lax.all_gather(inner_bias, "fsdp", axis=0, tiled=True),
        lax.all_gather(outer_weight, "fsdp", axis=0, tiled=True),
        lax.all_gather(outer_bias, "fsdp", axis=0, tiled=True),
    )
    back_gain_one, back_query, back_key, back_value, back_output = (
        attn_back[0],
        attn_back[2],
        attn_back[4],
        attn_back[5],
        attn_back[7],
    )
    back_gain_two, back_inner, back_outer = (feed_back[0], feed_back[2], feed_back[4])
    grad_out = cotangent.astype(jnp.float32).reshape(rows, width) * keep_rows
    grad_out_low = grad_out.astype(jnp.bfloat16)
    grad_outer_weight = left_product(active, grad_out_low)
    grad_outer_bias = jnp.sum(grad_out, 0)
    grad_inner = (right_product(grad_out_low, back_outer) * gelu_slope(inner)).astype(jnp.bfloat16)
    grad_inner_weight = left_product(normed2, grad_inner)
    grad_inner_bias = jnp.sum(grad_inner.astype(jnp.float32), 0)
    grad_normed2 = right_product(grad_inner, back_inner)
    grad_second_gain = jnp.sum(grad_normed2 * hat_two, 0)
    grad_second_shift = jnp.sum(grad_normed2, 0)
    grad_resid = grad_out + norm_back(
        grad_normed2, back_gain_two.astype(jnp.float32), hat_two, inv_two
    )
    grad_branch = grad_resid.astype(jnp.bfloat16)
    grad_output_weight = left_product(mixed, grad_branch)
    grad_output_bias = jnp.sum(grad_branch.astype(jnp.float32), 0)
    grad_mixed = right_product(grad_branch, back_output).astype(jnp.bfloat16)
    grad_heads = lax.all_to_all(
        to_heads(grad_mixed), "seq", split_axis=2, concat_axis=1, tiled=True
    )
    grad_heads = grad_heads.reshape(slots, length, heads_dev, HD)

    def attend_back(item):
        slot_q, slot_k, slot_v, slot_g, slot_lse = item
        scores = (
            jnp.einsum("qhd,khd->hqk", slot_q, slot_k, preferred_element_type=jnp.float32) * factor
        )
        probs = jnp.exp(scores - slot_lse[..., None])
        grad_v = jnp.einsum(
            "hqk,qhd->khd", probs.astype(jnp.bfloat16), slot_g, preferred_element_type=jnp.float32
        ).astype(jnp.bfloat16)
        grad_p = jnp.einsum("qhd,khd->hqk", slot_g, slot_v, preferred_element_type=jnp.float32)
        centre = jnp.sum(probs * grad_p, -1, keepdims=True)
        grad_s = (probs * (grad_p - centre)).astype(jnp.bfloat16)
        grad_q = (
            jnp.einsum("hqk,khd->qhd", grad_s, slot_k, preferred_element_type=jnp.float32) * factor
        ).astype(jnp.bfloat16)
        grad_k = (
            jnp.einsum("hqk,qhd->khd", grad_s, slot_q, preferred_element_type=jnp.float32) * factor
        ).astype(jnp.bfloat16)
        return (grad_q, grad_k, grad_v)

    heads_gq, heads_gk, heads_gv = lax.map(
        attend_back, (head_q, head_k, head_v, grad_heads, log_total)
    )
    frame_gq, frame_gk, frame_gv = (
        lax.all_to_all(to_frames(heads_gq), "seq", split_axis=1, concat_axis=2, tiled=True),
        lax.all_to_all(to_frames(heads_gk), "seq", split_axis=1, concat_axis=2, tiled=True),
        lax.all_to_all(to_frames(heads_gv), "seq", split_axis=1, concat_axis=2, tiled=True),
    )
    frame_gq = frame_gq.reshape(rows, width)
    frame_gk = frame_gk.reshape(rows, width)
    frame_gv = frame_gv.reshape(rows, width)
    grad_query_weight = left_product(normed1, frame_gq)
    grad_query_bias = jnp.sum(frame_gq.astype(jnp.float32), 0)
    grad_key_weight = left_product(normed1, frame_gk)
    grad_value_weight = left_product(normed1, frame_gv)
    grad_value_bias = jnp.sum(frame_gv.astype(jnp.float32), 0)
    grad_normed1 = (
        right_product(frame_gq, back_query)
        + right_product(frame_gk, back_key)
        + right_product(frame_gv, back_value)
    )
    grad_first_gain = jnp.sum(grad_normed1 * hat_one, 0)
    grad_first_shift = jnp.sum(grad_normed1, 0)
    input_grad = grad_resid + norm_back(
        grad_normed1, back_gain_one.astype(jnp.float32), hat_one, inv_one
    )
    input_grad = input_grad.astype(jnp.bfloat16).reshape(slots, local, width)
    gradients = (
        grad_first_gain,
        grad_first_shift,
        grad_query_weight,
        grad_query_bias,
        grad_key_weight,
        grad_value_weight,
        grad_value_bias,
        grad_output_weight,
        grad_output_bias,
        grad_second_gain,
        grad_second_shift,
        grad_inner_weight,
        grad_inner_bias,
        grad_outer_weight,
        grad_outer_bias,
    )
    summed = lax.psum(
        (
            gradients[0],
            gradients[1],
            gradients[2],
            gradients[3],
            gradients[4],
            gradients[5],
            gradients[6],
            gradients[7],
            gradients[8],
            gradients[9],
            gradients[10],
            gradients[11],
            gradients[12],
            gradients[13],
            gradients[14],
        ),
        "seq",
    )
    shards = (
        lax.psum_scatter(summed[0], "fsdp", scatter_dimension=0, tiled=True),
        lax.psum_scatter(summed[1], "fsdp", scatter_dimension=0, tiled=True),
        lax.psum_scatter(summed[2], "fsdp", scatter_dimension=0, tiled=True),
        lax.psum_scatter(summed[3], "fsdp", scatter_dimension=0, tiled=True),
        lax.psum_scatter(summed[4], "fsdp", scatter_dimension=0, tiled=True),
        lax.psum_scatter(summed[5], "fsdp", scatter_dimension=0, tiled=True),
        lax.psum_scatter(summed[6], "fsdp", scatter_dimension=0, tiled=True),
        lax.psum_scatter(summed[7], "fsdp", scatter_dimension=0, tiled=True),
        lax.psum_scatter(summed[8], "fsdp", scatter_dimension=0, tiled=True),
        lax.psum_scatter(summed[9], "fsdp", scatter_dimension=0, tiled=True),
        lax.psum_scatter(summed[10], "fsdp", scatter_dimension=0, tiled=True),
        lax.psum_scatter(summed[11], "fsdp", scatter_dimension=0, tiled=True),
        lax.psum_scatter(summed[12], "fsdp", scatter_dimension=0, tiled=True),
        lax.psum_scatter(summed[13], "fsdp", scatter_dimension=0, tiled=True),
        lax.psum_scatter(summed[14], "fsdp", scatter_dimension=0, tiled=True),
    )
    return (outputs, input_grad) + tuple(shards)


def solution(mesh):
    return jax.shard_map(
        per_device,
        mesh=mesh,
        in_specs=(
            P("fsdp", "seq", None),
            P("fsdp", "seq", None),
            P("fsdp"),
            P("fsdp"),
            P("fsdp"),
            P("fsdp", None),
            P("fsdp"),
            P("fsdp", None),
            P("fsdp", None),
            P("fsdp"),
            P("fsdp", None),
            P("fsdp"),
            P("fsdp"),
            P("fsdp"),
            P("fsdp", None),
            P("fsdp"),
            P("fsdp", None),
            P("fsdp"),
        ),
        out_specs=(
            P("fsdp", "seq", None),
            P("fsdp", "seq", None),
            P("fsdp"),
            P("fsdp"),
            P("fsdp", None),
            P("fsdp"),
            P("fsdp", None),
            P("fsdp", None),
            P("fsdp"),
            P("fsdp", None),
            P("fsdp"),
            P("fsdp"),
            P("fsdp"),
            P("fsdp", None),
            P("fsdp"),
            P("fsdp", None),
            P("fsdp"),
        ),
        check_vma=False,
    )
```

profile of v0, /device:TPU:0, one launch (start us, length us, event | category | flops | bytes accessed | tf_op | source)
XLA Modules:
  0.0 1094.1 jit_solution(10326943066400094859)
XLA Ops:
  21.2 26.2 %all-reduce.20 = (bf16[768]{0:T(1024)(128)(2,1)S(1)}, bf16[768]{0:T(1024)(128)(2,1)S(1)}, bf16[768]{0:T(1024)(128)(2,1)S(1)}, bf16[768]{0:T(1024)(128)(2,1)S(1)}...) all-reduce(bf16[768]{0:T(1024)(128)(2,1)S(1)} %dynamic-update-slice, ...), channel_id=1, replica_groups=mesh['fsdp'=8,'seq'=4] {'fsdp'}, use_global_device_ids=true, to_apply=%add.1 | all-reduce | flops 6144 | bytes 24576
  69.8 19.6 %all-to-all-done = bf16[2,375,4,192]{1,0,3,2:T(2,128)(2,1)S(1)} async-done(((bf16[2,375,4,192]{1,0,3,2:T(2,128)(2,1)}), bf16[2,375,4,192]{1,0,3,2:T(2,128)(2,1)S(1)}, u32[]{:S(2)}, u32[]{:S(2)}) %all-to-all-start) | async-done | bytes 1152032 | tf_op jit(solution)/shard_map/all_to_all | solution.py:126
  100.5 20.0 %all-to-all-done.1 = bf16[2,375,4,192]{1,0,3,2:T(2,128)(2,1)S(1)} async-done(((bf16[2,375,4,192]{1,0,3,2:T(2,128)(2,1)}), bf16[2,375,4,192]{1,0,3,2:T(2,128)(2,1)S(1)}, u32[]{:S(2)}, u32[]{:S(2)}) %all-to-all-start.1) | async-done | bytes 1152032 | tf_op jit(solution)/shard_map/all_to_all | solution.py:124
  134.4 18.4 %all-to-all-done.2 = bf16[2,375,4,192]{1,0,3,2:T(2,128)(2,1)} async-done(((bf16[2,375,4,192]{1,0,3,2:T(2,128)(2,1)}), bf16[2,375,4,192]{1,0,3,2:T(2,128)(2,1)}, u32[]{:S(2)}, u32[]{:S(2)}) %all-to-all-start.2) | async-done | bytes 1152032 | tf_op jit(solution)/shard_map/all_to_all | solution.py:125
  159.8 72.4 %while.26 = (s32[]{:T(128)}, bf16[2,1500,3,64]{1,3,2,0:T(8,128)(2,1)}, f32[2,3,1500]{2,1,0:T(4,128)}, bf16[2,1500,3,64]{1,3,2,0:T(8,128)(2,1)S(1)}, bf16[2,1500,...) while((s32[]{:T(128)}, bf16[2,1500,3,64]{1,3,2,0:T(8,128)(2,1)}, ...), condition=%wide.region_5.6_spmd, body=%wide.region_2.5_spmd.sunk | while | flops 1789033472 | bytes 84247392 | solution.py:146
  159.8 11.5 %multiply_reduce_fusion.13 = (f32[3,1500]{1,0:T(4,128)S(1)}, f32[3,1500,1500]{1,2,0:T(8,128)}) fusion(bf16[2,1500,3,64]{1,3,2,0:T(8,128)(2,1)S(1)} %get-tuple-element.413, s32[]{:T(128)} %get-tuple-element.401, bf16[2,1500,3,64]{1,3,2,0:T(8,128)(2,1)S(1)} %get-tuple-element.412), kind=kOutput, calls=%fused_computation.2.clone.1 | convolution fusion | flops 877495488 | bytes 28198672 | tf_op jit(solution)/shard_map/while/body/eval_jaxpr/qhd,khd->hqk/dot_general | solution.py:135
  171.3 11.8 %fusion.129 = f32[3,1500]{1,0:T(4,128)S(1)} fusion(f32[3,1500,1500]{1,2,0:T(8,128)} %get-tuple-element.381, f32[3,1500]{1,0:T(4,128)S(1)} %get-tuple-element.382), kind=kLoop, calls=%fused_computation.3.clone.1 | loop fusion | flops 20245500 | bytes 27036000 | tf_op jit(solution)/shard_map/while/body/eval_jaxpr/reduce_sum | solution.py:139
  183.7 12.3 %fusion.130 = bf16[2,1500,3,64]{1,3,2,0:T(8,128)(2,1)} fusion(bf16[2,1500,3,64]{1,3,2,0:T(8,128)(2,1)} %get-tuple-element.402, s32[]{:T(128)} %get-tuple-element.401, f32[3,1500,1500]{1,2,0:T(8,128)} %get-tuple-element.381, f32[3,1500]{1,0:T(4,128)S(1)} %fusion.129, f32[3,1500]{1,0:T(4,128)S(1)} %get-tuple-element.382, ...), kind=kOutput, calls=%fused_computation.7.clone.1 | convolution fusion | flops 891288000 | bytes 28951552 | tf_op jit(solution)/shard_map/while/body/eval_jaxpr/hqk,khd->qhd/dot_general | solution.py:141
  196.1 11.3 %multiply_reduce_fusion.13 = (f32[3,1500]{1,0:T(4,128)S(1)}, f32[3,1500,1500]{1,2,0:T(8,128)}) fusion(bf16[2,1500,3,64]{1,3,2,0:T(8,128)(2,1)S(1)} %get-tuple-element.413, s32[]{:T(128)} %get-tuple-element.401, bf16[2,1500,3,64]{1,3,2,0:T(8,128)(2,1)S(1)} %get-tuple-element.412), kind=kOutput, calls=%fused_computation.2.clone.1 | convolution fusion | flops 877495488 | bytes 28198672 | tf_op jit(solution)/shard_map/while/body/eval_jaxpr/qhd,khd->hqk/dot_general | solution.py:135
  207.4 11.8 %fusion.129 = f32[3,1500]{1,0:T(4,128)S(1)} fusion(f32[3,1500,1500]{1,2,0:T(8,128)} %get-tuple-element.381, f32[3,1500]{1,0:T(4,128)S(1)} %get-tuple-element.382), kind=kLoop, calls=%fused_computation.3.clone.1 | loop fusion | flops 20245500 | bytes 27036000 | tf_op jit(solution)/shard_map/while/body/eval_jaxpr/reduce_sum | solution.py:139
  219.8 12.3 %fusion.130 = bf16[2,1500,3,64]{1,3,2,0:T(8,128)(2,1)} fusion(bf16[2,1500,3,64]{1,3,2,0:T(8,128)(2,1)} %get-tuple-element.402, s32[]{:T(128)} %get-tuple-element.401, f32[3,1500,1500]{1,2,0:T(8,128)} %get-tuple-element.381, f32[3,1500]{1,0:T(4,128)S(1)} %fusion.129, f32[3,1500]{1,0:T(4,128)S(1)} %get-tuple-element.382, ...), kind=kOutput, calls=%fused_computation.7.clone.1 | convolution fusion | flops 891288000 | bytes 28951552 | tf_op jit(solution)/shard_map/while/body/eval_jaxpr/hqk,khd->qhd/dot_general | solution.py:141
  257.2 20.3 %all-to-all-done.3 = bf16[2,1500,1,192]{3,0,2,1:T(2,128)(2,1)} async-done(((bf16[2,1500,1,192]{3,0,2,1:T(2,128)(2,1)}), bf16[2,1500,1,192]{3,0,2,1:T(2,128)(2,1)}, u32[]{:S(2)}, u32[]{:S(2)}) %all-to-all-start.3) | async-done | bytes 1152032 | tf_op jit(solution)/shard_map/all_to_all | solution.py:147
  292.0 26.9 %fusion.54 = (bf16[750,3072]{1,0:T(8,128)(2,1)}, f32[750,3072]{1,0:T(8,128)}) fusion(f32[3072]{0:T(1024)S(1)} %bitcast.196, bf16[768,3072]{1,0:T(8,128)(2,1)} %all-gather.16.cloned.1.call-done, f32[750,768]{1,0:T(8,128)} %copy-done.7, f32[768]{0:T(1024)S(1)} %convert_element_type.139, f32[768]{0:T(1024)S(1)} %convert_element_type.138, ...), kind=kOutput, calls=%fused_computation.60 | convolution fusion | flops 3693888000 | bytes 20871024 | tf_op jit(solution)/shard_map/dot_general | solution.py:16
  348.8 24.1 %all-to-all-done.4 = bf16[2,375,4,192]{1,0,3,2:T(2,128)(2,1)S(1)} async-done(((bf16[2,375,4,192]{1,0,3,2:T(2,128)(2,1)}), bf16[2,375,4,192]{1,0,3,2:T(2,128)(2,1)S(1)}, u32[]{:S(2)}, u32[]{:S(2)}) %all-to-all-start.4) | async-done | bytes 1152032 | tf_op jit(solution)/shard_map/all_to_all | solution.py:203
  378.1 183.5 %while.27 = (s32[]{:T(128)}, bf16[2,1500,3,64]{1,3,2,0:T(8,128)(2,1)}, bf16[2,1500,3,64]{1,3,2,0:T(8,128)(2,1)}, bf16[2,1500,3,64]{1,3,2,0:T(8,128)(2,1)}, bf16[...) while((s32[]{:T(128)}, ...), condition=%wide.region_12.13_spmd, body=%wide.region_10.12_spmd.sunk | while | flops 4375435264 | bytes 219881280 | solution.py:228
  378.2 12.7 %fusion.139 = f32[3,1500,1500]{1,2,0:T(8,128)} fusion(bf16[2,1500,3,64]{1,3,2,0:T(8,128)(2,1)} %get-tuple-element.443, s32[]{:T(128)} %get-tuple-element.425, bf16[2,1500,3,64]{1,3,2,0:T(8,128)(2,1)S(1)} %get-tuple-element.442), kind=kOutput, calls=%fused_computation.35.clone.1 | convolution fusion | flops 864000000 | bytes 28180672 | tf_op jit(solution)/shard_map/while/body/eval_jaxpr/qhd,khd->hqk/dot_general | solution.py:217
  392.3 22.5 %multiply_reduce_fusion.14 = (f32[3,1500]{1,0:T(4,128)}, f32[3,1500,1500]{1,2,0:T(8,128)}) fusion(f32[3,1500,1500]{1,2,0:T(8,128)} %fusion.139, f32[3,1500]{1,0:T(4,128)} %dynamic-slice_bitcast_fusion.2, bf16[2,1500,3,64]{1,3,2,0:T(8,128)(2,1)S(1)} %get-tuple-element.439, s32[]{:T(128)} %get-tuple-element.425, ...), kind=kOutput, calls=%fused_computation.20.clone.1 | convolution fusion | flops 890995520 | bytes 55944976 | tf_op jit(solution)/shard_map/while/body/eval_jaxpr/qhd,khd->hqk/dot_general | solution.py:211
  414.8 23.7 %multiply_convert_fusion.6 = bf16[3,1500,1500]{1,2,0:T(8,128)(2,1)} fusion(f32[3,1500,1500]{1,2,0:T(8,128)} %get-tuple-element.392, f32[3,1500,1500]{1,2,0:T(8,128)} %fusion.139, f32[3,1500]{1,0:T(4,128)} %get-tuple-element.393), kind=kLoop, calls=%fused_computation.19.clone.1 | loop fusion | flops 20250000 | bytes 67518000 | tf_op jit(solution)/shard_map/while/body/eval_jaxpr/convert_element_type | solution.py:219
  456.2 13.8 %fusion.142 = bf16[2,1500,3,64]{1,3,2,0:T(8,128)(2,1)} fusion(bf16[2,1500,3,64]{1,3,2,0:T(8,128)(2,1)} %get-tuple-element.428, s32[]{:T(128)} %get-tuple-element.425, f32[3,1500,1500]{1,2,0:T(8,128)} %get-tuple-element.392, bf16[2,1500,3,64]{1,3,2,0:T(8,128)(2,1)S(1)} %get-tuple-element.442), kind=kOutput, calls=%fused_computation.30.clone.1 | convolution fusion | flops 871038016 | bytes 28902400 | tf_op jit(solution)/shard_map/while/body/eval_jaxpr/hqk,qhd->khd/dot_general | solution.py:214
  470.0 12.5 %fusion.139 = f32[3,1500,1500]{1,2,0:T(8,128)} fusion(bf16[2,1500,3,64]{1,3,2,0:T(8,128)(2,1)} %get-tuple-element.443, s32[]{:T(128)} %get-tuple-element.425, bf16[2,1500,3,64]{1,3,2,0:T(8,128)(2,1)S(1)} %get-tuple-element.442), kind=kOutput, calls=%fused_computation.35.clone.1 | convolution fusion | flops 864000000 | bytes 28180672 | tf_op jit(solution)/shard_map/while/body/eval_jaxpr/qhd,khd->hqk/dot_general | solution.py:217
  483.8 22.4 %multiply_reduce_fusion.14 = (f32[3,1500]{1,0:T(4,128)}, f32[3,1500,1500]{1,2,0:T(8,128)}) fusion(f32[3,1500,1500]{1,2,0:T(8,128)} %fusion.139, f32[3,1500]{1,0:T(4,128)} %dynamic-slice_bitcast_fusion.2, bf16[2,1500,3,64]{1,3,2,0:T(8,128)(2,1)S(1)} %get-tuple-element.439, s32[]{:T(128)} %get-tuple-element.425, ...), kind=kOutput, calls=%fused_computation.20.clone.1 | convolution fusion | flops 890995520 | bytes 55944976 | tf_op jit(solution)/shard_map/while/body/eval_jaxpr/qhd,khd->hqk/dot_general | solution.py:211
  506.2 23.7 %multiply_convert_fusion.6 = bf16[3,1500,1500]{1,2,0:T(8,128)(2,1)} fusion(f32[3,1500,1500]{1,2,0:T(8,128)} %get-tuple-element.392, f32[3,1500,1500]{1,2,0:T(8,128)} %fusion.139, f32[3,1500]{1,0:T(4,128)} %get-tuple-element.393), kind=kLoop, calls=%fused_computation.19.clone.1 | loop fusion | flops 20250000 | bytes 67518000 | tf_op jit(solution)/shard_map/while/body/eval_jaxpr/convert_element_type | solution.py:219
  547.6 13.8 %fusion.142 = bf16[2,1500,3,64]{1,3,2,0:T(8,128)(2,1)} fusion(bf16[2,1500,3,64]{1,3,2,0:T(8,128)(2,1)} %get-tuple-element.428, s32[]{:T(128)} %get-tuple-element.425, f32[3,1500,1500]{1,2,0:T(8,128)} %get-tuple-element.392, bf16[2,1500,3,64]{1,3,2,0:T(8,128)(2,1)S(1)} %get-tuple-element.442), kind=kOutput, calls=%fused_computation.30.clone.1 | convolution fusion | flops 871038016 | bytes 28902400 | tf_op jit(solution)/shard_map/while/body/eval_jaxpr/hqk,qhd->khd/dot_general | solution.py:214
  573.8 32.0 %all-to-all-done.7 = bf16[2,1500,1,192]{3,0,2,1:T(2,128)(2,1)S(1)} async-done(((bf16[2,1500,1,192]{3,0,2,1:T(2,128)(2,1)}), bf16[2,1500,1,192]{3,0,2,1:T(2,128)(2,1)S(1)}, u32[]{:S(2)}, u32[]{:S(2)}) %all-to-all-start.7) | async-done | bytes 1152032 | tf_op jit(solution)/shard_map/all_to_all | solution.py:234
  625.0 38.9 %all_to_all.120 = bf16[2,1500,1,192]{3,0,2,1:T(2,128)(2,1)} all-to-all(bf16[2,1500,1,192]{3,0,2,1:T(2,128)(2,1)S(1)} %copy.169), channel_id=1, replica_groups=mesh['fsdp'=8,'seq'=4] {'seq'}, dimensions={1} | all-to-all | bytes 2304000 | tf_op jit(solution)/shard_map/all_to_all | solution.py:232
  682.6 39.0 %all_to_all.121 = bf16[2,1500,1,192]{3,0,2,1:T(2,128)(2,1)} all-to-all(bf16[2,1500,1,192]{3,0,2,1:T(2,128)(2,1)S(1)} %copy.172), channel_id=1, replica_groups=mesh['fsdp'=8,'seq'=4] {'seq'}, dimensions={1} | all-to-all | bytes 2304000 | tf_op jit(solution)/shard_map/all_to_all | solution.py:233
  762.6 16.9 %reduce-scatter.9.cloned.1.call-done = f32[96,768]{1,0:T(8,128)} async-done(((f32[768,768]{1,0:T(8,128)}), f32[96,768]{1,0:T(8,128)}) %reduce-scatter.9.cloned.1.call-update) | async-done | bytes 294928 | tf_op jit(solution)/shard_map/reduce_scatter | solution.py:297
  779.5 80.0 %reduce-scatter.15.cloned.1.call-done = f32[96,3072]{1,0:T(8,128)} async-done(((f32[768,3072]{1,0:T(8,128)}), f32[96,3072]{1,0:T(8,128)}) %reduce-scatter.15.cloned.1.call-update) | async-done | bytes 1179664 | tf_op jit(solution)/shard_map/reduce_scatter | solution.py:304
  859.5 79.9 %reduce-scatter.17.cloned.1.call-done = f32[384,768]{1,0:T(8,128)} async-done(((f32[3072,768]{1,0:T(8,128)}), f32[384,768]{1,0:T(8,128)}) %reduce-scatter.17.cloned.1.call-update) | async-done | bytes 1179664 | tf_op jit(solution)/shard_map/reduce_scatter | solution.py:306
  963.8 25.3 %all-reduce.17 = (f32[768]{0:T(1024)S(1)}, f32[768]{0:T(1024)S(1)}, f32[768]{0:T(1024)S(1)}, f32[768]{0:T(1024)S(1)}, f32[768]{0:T(1024)S(1)}, /*index=5*/f32[76...) all-reduce(f32[768]{0:T(1024)S(1)} %get-tuple-element.208, ...), channel_id=2, replica_groups=mesh['fsdp'=8,'seq'=4] {'fsdp'}, use_global_device_ids=true, to_apply=%region_17.18.clone | all-reduce | flops 9216 | bytes 73728
  994.7 13.5 %all-reduce.18 = (f32[96]{0:T(128)}, f32[96]{0:T(128)}, f32[96]{0:T(128)}, f32[96]{0:T(128)}, f32[96]{0:T(128)}, /*index=5*/f32[96]{0:T(128)}, f32[96]{0:T(128)}, f32[384]{0:T(512)}, f32[96]{0:T(128)}) all-reduce(f32[96]{0:T(128)S(1)} %dynamic-slice.9, f32[96]{0:T(128)S(1)} %dynamic-slice.11, ...), channel_id=1, replica_groups=mesh['fsdp'=8,'seq'=4] {'seq'}, use_global_device_ids=true, to_apply=%region_16.17 | all-reduce | flops 1152 | bytes 9216 | tf_op jit(solution)/shard_map/psum | solution.py:272
  1008.2 70.1 %all-reduce.23.cloned.1.call-done = (f32[96,768]{1,0:T(8,128)}, f32[96,768]{1,0:T(8,128)}, f32[96,768]{1,0:T(8,128)}, f32[96,768]{1,0:T(8,128)}, f32[96,3072]{1,0:T(8,128)}, /*index=5*/f32[384,768]{1,0:T(8,128)}) async-done(((f32[96,768]{1,0:T(8,128)}, f32[96,768]{1,0:T(8,128)}, f32[96,768]{1,0:T(8,128)}, f32[96,768]{1,0:T(8,128)}, f32[96,3072]{1,0:T(8,128)}, /*index=5*/f32[384,768]{1,0:T(8,128)}), ...) | async-done | bytes 3538960 | tf_op jit(solution)/shard_map/psum | solution.py:272
  (344 shorter events, 309.1 us)
Async XLA Ops:
  7.2 43.4 %all-gather.8.cloned.1.call-start = ((), (), s32[]{:S(2)}) async-start(), calls=%async_computation.14 | async-start | bytes 1327104 | tf_op jit(solution)/shard_map/all_gather | solution.py:82
  7.9 56.8 %all-gather.10.cloned.1.call-start = ((), (), s32[]{:S(2)}) async-start(), calls=%async_computation.15 | async-start | bytes 1327104 | tf_op jit(solution)/shard_map/all_gather | solution.py:79
  11.1 9.7 copy-start.76
  11.1 9.9 copy-start.77
  59.0 30.3 %all-to-all-start = ((bf16[2,375,4,192]{1,0,3,2:T(2,128)(2,1)}), bf16[2,375,4,192]{1,0,3,2:T(2,128)(2,1)S(1)}, u32[]{:S(2)}, u32[]{:S(2)}) async-start(bf16[2,375,4,192]{1,0,3,2:T(2,128)(2,1)} %reshape.267), calls=%async_computation | async-start | bytes 2359296 | tf_op jit(solution)/shard_map/all_to_all | solution.py:126
  64.0 29.5 %all-gather.12.cloned.1.call-start = ((), (), s32[]{:S(2)}) async-start(), calls=%async_computation.16 | async-start | bytes 1327104 | tf_op jit(solution)/shard_map/all_gather | solution.py:81
  67.8 25.7 %copy-start.36 = (bf16[750,768]{1,0:T(8,128)(2,1)S(1)}, bf16[750,768]{1,0:T(8,128)(2,1)}, u32[]{:S(2)}) copy-start(bf16[750,768]{1,0:T(8,128)(2,1)} %copy-done.34) | copy-start | bytes 3456004
  89.3 31.1 %all-to-all-start.1 = ((bf16[2,375,4,192]{1,0,3,2:T(2,128)(2,1)}), bf16[2,375,4,192]{1,0,3,2:T(2,128)(2,1)S(1)}, u32[]{:S(2)}, u32[]{:S(2)}) async-start(bf16[2,375,4,192]{1,0,3,2:T(2,128)(2,1)} %reshape.269), calls=%async_computation.1 | async-start | bytes 2359296 | tf_op jit(solution)/shard_map/all_to_all | solution.py:124
  92.9 194.3 %all-gather.14.cloned.1.call-start = ((), (), s32[]{:S(2)}) async-start(), calls=%async_computation.17 | async-start | bytes 1327104 | tf_op jit(solution)/shard_map/all_gather | solution.py:84
  120.4 32.4 %all-to-all-start.2 = ((bf16[2,375,4,192]{1,0,3,2:T(2,128)(2,1)}), bf16[2,375,4,192]{1,0,3,2:T(2,128)(2,1)}, u32[]{:S(2)}, u32[]{:S(2)}) async-start(bf16[2,375,4,192]{1,0,3,2:T(2,128)(2,1)} %reshape.271), calls=%async_computation.2 | async-start | bytes 2359296 | tf_op jit(solution)/shard_map/all_to_all | solution.py:125
  124.7 167.2 %all-gather.16.cloned.1.call-start = ((), (), s32[]{:S(2)}) async-start(), calls=%async_computation.18 | async-start | bytes 5308416 | tf_op jit(solution)/shard_map/all_gather | solution.py:90
  237.4 40.2 %all-to-all-start.3 = ((bf16[2,1500,1,192]{3,0,2,1:T(2,128)(2,1)}), bf16[2,1500,1,192]{3,0,2,1:T(2,128)(2,1)}, u32[]{:S(2)}, u32[]{:S(2)}) async-start(bf16[2,1500,1,192]{3,0,2,1:T(2,128)(2,1)} %copy.163), calls=%async_computation.3 | async-start | bytes 3072000 | tf_op jit(solution)/shard_map/all_to_all | solution.py:147
  241.9 77.1 %all-gather.18.cloned.1.call-start = ((), (), s32[]{:S(2)}) async-start(), calls=%async_computation.19 | async-start | bytes 5308416 | tf_op jit(solution)/shard_map/all_gather | solution.py:92
  242.5 91.9 %copy-start.39 = (f32[768]{0:T(1024)}, f32[768]{0:T(1024)S(1)}, u32[]{:S(2)}) copy-start(f32[768]{0:T(1024)S(1)} %convert_element_type.138) | copy-start | bytes 9220
  242.5 49.5 %copy-start.43 = (f32[768]{0:T(1024)}, f32[768]{0:T(1024)S(1)}, u32[]{:S(2)}) copy-start(f32[768]{0:T(1024)S(1)} %convert_element_type.139) | copy-start | bytes 9220
  254.0 80.4 %copy-start.53 = (f32[750]{0:T(1024)}, f32[750]{0:T(1024)S(1)}, u32[]{:S(2)}) copy-start(f32[750]{0:T(1024)S(1)} %mul.195) | copy-start | bytes 9004
  290.2 44.3 %copy-start.37 = (f32[750]{0:T(1024)}, f32[750]{0:T(1024)S(1)}, u32[]{:S(2)}) copy-start(f32[750]{0:T(1024)S(1)} %broadcast_multiply_fusion.5) | copy-start | bytes 9004
  291.9 42.5 %copy-start.41 = (f32[750]{0:T(1024)}, f32[750]{0:T(1024)S(1)}, u32[]{:S(2)}) copy-start(f32[750]{0:T(1024)S(1)} %add_rsqrt_fusion.1) | copy-start | bytes 9004
  292.0 27.0 %copy-start.15 = (f32[750,768]{1,0:T(8,128)S(1)}, f32[750,768]{1,0:T(8,128)}, u32[]{:S(2)}) copy-start(f32[750,768]{1,0:T(8,128)} %reshape.276) | copy-start | bytes 6912004
  319.0 10.6 copy-start.8
  319.0 10.6 copy-start.67
  341.4 31.5 %all-to-all-start.4 = ((bf16[2,375,4,192]{1,0,3,2:T(2,128)(2,1)}), bf16[2,375,4,192]{1,0,3,2:T(2,128)(2,1)S(1)}, u32[]{:S(2)}, u32[]{:S(2)}) async-start(bf16[2,375,4,192]{1,0,3,2:T(2,128)(2,1)} %reshape.277), calls=%async_computation.4 | async-start | bytes 2359296 | tf_op jit(solution)/shard_map/all_to_all | solution.py:203
  344.9 417.6 %reduce-scatter.13.cloned.1.call-start = ((), (), s32[]{:S(2)}) async-start(), calls=%async_computation.23 | async-start | bytes 2654208 | tf_op jit(solution)/shard_map/reduce_scatter | solution.py:300
  414.8 23.7 %copy-start.21 = (bf16[2,1500,3,64]{1,3,2,0:T(8,128)(2,1)S(1)}, bf16[2,1500,3,64]{1,3,2,0:T(8,128)(2,1)}, u32[]{:S(2)}) copy-start(bf16[2,1500,3,64]{1,3,2,0:T(8,128)(2,1)} %get-tuple-element.427) | copy-start | bytes 3456004 | tf_op jit(solution)/shard_map/while
  506.2 23.7 %copy-start.21 = (bf16[2,1500,3,64]{1,3,2,0:T(8,128)(2,1)S(1)}, bf16[2,1500,3,64]{1,3,2,0:T(8,128)(2,1)}, u32[]{:S(2)}) copy-start(bf16[2,1500,3,64]{1,3,2,0:T(8,128)(2,1)} %get-tuple-element.427) | copy-start | bytes 3456004 | tf_op jit(solution)/shard_map/while
  566.6 39.2 %all-to-all-start.7 = ((bf16[2,1500,1,192]{3,0,2,1:T(2,128)(2,1)}), bf16[2,1500,1,192]{3,0,2,1:T(2,128)(2,1)S(1)}, u32[]{:S(2)}, u32[]{:S(2)}) async-start(bf16[2,1500,1,192]{3,0,2,1:T(2,128)(2,1)} %copy.175), calls=%async_computation.7 | async-start | bytes 3072000 | tf_op jit(solution)/shard_map/all_to_all | solution.py:234
  570.2 192.4 %reduce-scatter.11.cloned.1.call-start = ((), (), s32[]{:S(2)}) async-start(), calls=%async_computation.22 | async-start | bytes 2654208 | tf_op jit(solution)/shard_map/reduce_scatter | solution.py:298
  620.9 141.7 %reduce-scatter.7.cloned.1.call-start = ((), (), s32[]{:S(2)}) async-start(), calls=%async_computation.20 | async-start | bytes 2654208 | tf_op jit(solution)/shard_map/reduce_scatter | solution.py:295
  678.4 101.0 %reduce-scatter.9.cloned.1.call-start = ((), (), s32[]{:S(2)}) async-start(), calls=%async_computation.21 | async-start | bytes 2654208 | tf_op jit(solution)/shard_map/reduce_scatter | solution.py:297
  736.1 123.4 %reduce-scatter.15.cloned.1.call-start = ((), (), s32[]{:S(2)}) async-start(), calls=%async_computation.24 | async-start | bytes 10616832 | tf_op jit(solution)/shard_map/reduce_scatter | solution.py:304
  746.7 192.7 %reduce-scatter.17.cloned.1.call-start = ((), (), s32[]{:S(2)}) async-start(), calls=%async_computation.25 | async-start | bytes 10616832 | tf_op jit(solution)/shard_map/reduce_scatter | solution.py:306
  758.3 320.0 %all-reduce.23.cloned.1.call-start = ((), (), s32[]{:S(2)}) async-start(), calls=%async_computation.26 | async-start | bytes 7077888 | tf_op jit(solution)/shard_map/psum | solution.py:272
  (67 other events, 296.8 us)
Sparse Core Ops, SparseCore 0:
  9.9 26.8 all-gather.7
  38.7 24.1 all-gather.9
  66.7 23.6 all-gather.11
  95.3 26.1 all-gather.13
  127.1 42.1 all-gather.15
  244.3 42.0 all-gather.17
  349.1 45.6 reduce-scatter.12
  621.0 43.2 reduce-scatter.10
  678.6 43.2 reduce-scatter.6
  736.2 43.2 reduce-scatter.8
  783.0 76.4 reduce-scatter.14
  862.9 76.4 reduce-scatter.16
  942.2 136.0 all-reduce.22
where the time goes:
time: 1100 us; the launch traced here: 1090 us
  waiting for transfers between devices  385 us (35%)
  matrix products  288 us (26%)
  blocking collectives  153 us (14%)
  local copies, waits for them, and re-layouts  133 us (12%)
  other arithmetic  91.8 us (8%)
  starting transfers between devices  25.4 us (2%)
  between operations  17.2 us (2%)
    reduce_scatter x1, waiting for transfers between devices, per_device(): lax.psum_scatter(summed[11], 'fsdp', scatter_dimension=0, tiled=True)  80 us
    reduce_scatter x1, waiting for transfers between devices, per_device(): lax.psum_scatter(summed[13], 'fsdp', scatter_dimension=0, tiled=True)  79.9 us
    psum x1, waiting for transfers between devices, per_device(): lax.psum((gradients[0], gradients[1], gradients[2], gradients[3], gradien...  70.1 us
    unnamed x2, blocking collectives  51.5 us
    dot_general x6, matrix products, product(): return jnp.dot(left, right, preferred_element_type=jnp.float32)  47.4 us
    convert_element_type x2, other arithmetic, attend_back(): grad_s = (probs * (grad_p - centre)).astype(jnp.bfloat16)  47.4 us
    dot_general x2, matrix products, attend_back(): jnp.einsum('qhd,khd->hqk', slot_q, slot_k, preferred_element_type=jnp.flo...  44.9 us
    all_to_all x1, blocking collectives, per_device(): lax.all_to_all(to_frames(heads_gk), 'seq', split_axis=1, concat_axis=2, t...  39 us
  transfers between devices with their start and end apart: 19, of which 10 were waited for; matrix products, arithmetic and copies ran while one was open for 43% of the time, Pallas kernels for 0%

commit v1 on v0

v1 whole, which is shorter than its diff:
```python
import math

import jax
import jax.numpy as jnp
from jax import lax
from jax.experimental import pallas as pl
from jax.experimental.pallas import tpu as pltpu
from jax.sharding import PartitionSpec as P

H = 12
HD = 64
EPS = 1e-05
MESH = pl.DeviceIdType.MESH
F32 = jnp.float32
BF16 = jnp.bfloat16
ANY = pl.BlockSpec(memory_space=pl.ANY)
VMEM = pl.BlockSpec(memory_space=pltpu.VMEM)
LIMIT = 60 << 20
QB = 256


def nn(a, b):
    return lax.dot_general(a, b, (((1,), (0,)), ((), ())), preferred_element_type=F32)


def nt(a, b):
    return lax.dot_general(a, b, (((1,), (1,)), ((), ())), preferred_element_type=F32)


def tn(a, b):
    return lax.dot_general(a, b, (((0,), (0,)), ((), ())), preferred_element_type=F32)


def normalize(rows):
    center = rows - jnp.mean(rows, -1, keepdims=True)
    inv = lax.rsqrt(jnp.mean(center * center, -1, keepdims=True) + EPS)
    return center * inv, inv


def norm_back(grad, gain, hat, inv):
    tilted = grad * gain
    first = jnp.mean(tilted, -1, keepdims=True)
    cross = jnp.mean(tilted * hat, -1, keepdims=True)
    return inv * (tilted - first - hat * cross)


def where_am_i():
    f = lax.axis_index("fsdp")
    z = lax.axis_index("seq")
    return f, z, f // 2, f % 2


def meet(peers):
    barrier = pltpu.get_barrier_semaphore()
    for peer in peers:
        pl.semaphore_signal(barrier, inc=1, device_id=peer, device_id_type=MESH)
    pl.semaphore_wait(barrier, len(peers))


def column_peers(seq):
    f, z, m, c = where_am_i()
    peers = []
    for dc in range(2):
        for dz in range(seq):
            if dc or dz:
                peers.append((m * 2 + (c + dc) % 2, (z + dz) % seq))
    return peers


class Ship:
    def __init__(self, src, dst, send, recv, target):
        f, z, _, _ = where_am_i()
        self.here = jnp.logical_and(target[0] == f, target[1] == z)
        self.local = pltpu.make_async_copy(src, dst, recv)
        self.remote = pltpu.make_async_remote_copy(
            src, dst, send, recv, device_id=target, device_id_type=MESH
        )

    def start(self):
        pl.when(self.here)(self.local.start)
        pl.when(jnp.logical_not(self.here))(self.remote.start)

    def wait_send(self):
        pl.when(jnp.logical_not(self.here))(self.remote.wait_send)


def remote(src, dst, send, recv, target):
    return pltpu.make_async_remote_copy(
        src, dst, send, recv, device_id=target, device_id_type=MESH
    )


class Gather:
    def __init__(self, send_ref, full_ref, send_sem, recv_sem, pass_send, pass_recv, seq):
        f, z, m, c = where_am_i()
        self.ships = []
        for i in range(2):
            for h in range(2):
                slot = 2 * c + i
                self.ships.append(
                    Ship(
                        send_ref.at[i, h],
                        full_ref.at[z, h],
                        send_sem.at[i, h],
                        recv_sem.at[z],
                        (m * 2 + h, slot),
                    )
                )
        other = (m * 2 + 1 - c, z)
        self.arrivals = [
            remote(send_ref.at[0, 0], full_ref.at[k, c], send_sem.at[0, 0], recv_sem.at[k], other)
            for k in range(seq)
        ]
        self.passes = [
            remote(full_ref.at[k, c], full_ref.at[k, c], pass_send.at[k], pass_recv.at[k], other)
            for k in range(seq)
        ]
        self.handed = [
            remote(
                full_ref.at[k, c], full_ref.at[k, 1 - c], pass_send.at[k], pass_recv.at[k], other
            )
            for k in range(seq)
        ]

    def start(self):
        for ship in self.ships:
            ship.start()

    def hand_on(self, k):
        self.arrivals[k].wait_recv()
        self.passes[k].start()

    def ready(self, k):
        self.handed[k].wait_recv()

    def finish(self):
        for ship in self.ships:
            ship.wait_send()
        for item in self.passes:
            item.wait_send()


GATHER_SEMS = lambda seq: [
    pltpu.SemaphoreType.DMA((2, 2)),
    pltpu.SemaphoreType.DMA((seq,)),
    pltpu.SemaphoreType.DMA((seq,)),
    pltpu.SemaphoreType.DMA((seq,)),
]


class Return:
    def __init__(self, own_ref, back_ref, send_sem, recv_sem, seq):
        f, z, m, c = where_am_i()
        home = z // 2
        self.ships = [
            Ship(
                own_ref.at[k],
                back_ref.at[z % 2, c],
                send_sem.at[k],
                recv_sem.at[z % 2, c],
                (m * 2 + home, k),
            )
            for k in range(seq)
        ]
        self.arrivals = [
            remote(
                own_ref.at[0],
                back_ref.at[i, h],
                send_sem.at[0],
                recv_sem.at[i, h],
                (m * 2 + 1 - c, z),
            )
            for i in range(2)
            for h in range(2)
        ]

    def start(self):
        for ship in self.ships:
            ship.start()

    def finish(self):
        for ship in self.ships:
            ship.wait_send()
        for item in self.arrivals:
            item.wait_recv()


RETURN_SEMS = lambda seq: [pltpu.SemaphoreType.DMA((seq,)), pltpu.SemaphoreType.DMA((2, 2))]


def own_lanes(parity):
    lane = lax.broadcasted_iota(jnp.int32, (1, 128), 1)
    return (lane // HD) == parity, lane == HD * (1 - parity)


def project_kernel(
    seq, x_send, wqkv, vecs, x_full, n1_out, q_out, k_out, v_out, ssem, rsem, psend, precv, xv, lsem
):
    f, z, m, c = where_am_i()
    meet(column_peers(seq))
    gather = Gather(x_send, x_full, ssem, rsem, psend, precv, seq)
    gather.start()
    half = xv.shape[1]
    width = q_out.shape[1]
    for k in range(seq):
        gather.hand_on(k)
    gain = vecs[0:1, :]
    shift = vecs[1:2, :]
    cols = pl.ds(pl.multiple_of(c * width, 128), width)
    qb = vecs[2:3, cols]
    vb = vecs[3:4, cols]

    for k in range(seq):
        gather.ready(k)
        copy = pltpu.make_async_copy(x_full.at[k], xv, lsem)
        copy.start()
        copy.wait()
        rows = pl.ds(k * 2 * half, 2 * half)
        hat, _ = normalize(xv[...].reshape(2 * half, -1).astype(F32))
        normed = (hat * gain + shift).astype(BF16)
        n1_out[rows, :] = normed
        qkv = nn(normed, wqkv[...])
        q_out[rows, :] = (qkv[:, :width] + qb).astype(BF16)
        k_out[rows, :] = qkv[:, width : 2 * width].astype(BF16)
        v_out[rows, :] = (qkv[:, 2 * width :] + vb).astype(BF16)
    gather.finish()


def project(x_send, wqkv, vecs, seq):
    _, _, half, width = x_send.shape
    rows = seq * 2 * half
    mine = wqkv.shape[1] // 3
    return pl.pallas_call(
        lambda *refs: project_kernel(seq, *refs),
        in_specs=[ANY, VMEM, VMEM],
        out_specs=[ANY, VMEM, VMEM, VMEM, VMEM],
        out_shape=[
            jax.ShapeDtypeStruct((seq, 2, half, width), BF16),
            jax.ShapeDtypeStruct((rows, width), BF16),
        ]
        + [jax.ShapeDtypeStruct((rows, mine), BF16)] * 3,
        scratch_shapes=GATHER_SEMS(seq)
        + [pltpu.VMEM((2, half, width), BF16), pltpu.SemaphoreType.DMA],
        compiler_params=pltpu.CompilerParams(
            collective_id=0, has_side_effects=True, vmem_limit_bytes=LIMIT
        ),
        name="project",
    )(x_send, wqkv, vecs)


def attend_kernel(
    seq, local, heads, cot_send, q, k, v, e_out, o_out, linv_out, mixed_out, cot_full,
    ssem, rsem, psend, precv, stage, ka, va, msend, mrecv, mlocal,
):
    f, z, m, c = where_am_i()
    h = pl.program_id(0)
    pair = h // 2
    parity = h % 2
    rows = q.shape[0]
    gather = Gather(cot_send, cot_full, ssem, rsem, psend, precv, seq)
    other = (m * 2 + 1 - c, z)

    @pl.when(h == 0)
    def _():
        meet(column_peers(seq))
        gather.start()

    mine, first = own_lanes(parity)
    place = lax.broadcasted_iota(jnp.int32, (rows, 1), 0) % (rows // seq)
    bar = jnp.where(place < local, 0.0, -1e38).astype(F32)
    ka[...] = jnp.where(mine, k[...].astype(F32), jnp.where(first, bar, 0.0)).astype(BF16)
    va[...] = jnp.where(mine, v[...].astype(F32), jnp.where(first, 1.0, 0.0)).astype(BF16)
    factor = HD ** (-0.5) * math.log2(math.e)
    for i in range(rows // QB):
        sl = slice(i * QB, (i + 1) * QB)
        qa = jnp.where(mine, q[sl, :].astype(F32), jnp.where(first, 1.0, 0.0)).astype(BF16)
        scores = nt(qa, ka[...])
        peak = jnp.max(scores, -1, keepdims=True)
        expo = jnp.exp2((scores - peak) * factor).astype(BF16)
        e_out[0, sl, :] = expo
        raw = nn(expo, va[...])
        total = jnp.sum(jnp.where(first, raw, 0.0), -1, keepdims=True)
        inv = 1.0 / total
        res = raw * inv

        @pl.when(parity == 0)
        def _():
            o_out[sl, :] = res
            linv_out[sl, :] = jnp.broadcast_to(inv, res.shape)

        @pl.when(parity == 1)
        def _():
            both = jnp.where(mine, res, o_out[sl, :])
            o_out[sl, :] = both
            linv_out[sl, :] = jnp.where(mine, inv, linv_out[sl, :])
            stage[pair, sl, :] = both.astype(BF16)

    def mixed_copies(p):
        return (
            pltpu.make_async_copy(stage.at[p], mixed_out.at[c, p], mlocal.at[p]),
            remote(stage.at[p], mixed_out.at[c, p], msend.at[p], mrecv.at[p], other),
            remote(stage.at[p], mixed_out.at[1 - c, p], msend.at[p], mrecv.at[p], other),
        )

    @pl.when(parity == 1)
    def _():
        here, there, _ = mixed_copies(pair)
        here.start()
        there.start()

    @pl.when(h == heads - 2)
    def _():
        for item in range(seq):
            gather.hand_on(item)

    @pl.when(h == heads - 1)
    def _():
        for item in range(seq):
            gather.ready(item)
        gather.finish()
        for p in range(heads // 2):
            here, there, back = mixed_copies(p)
            here.wait()
            there.wait_send()
            back.wait_recv()


def attend(cot_send, q, k, v, local, seq):
    rows, mine = q.shape
    heads = mine // HD
    _, _, half, width = cot_send.shape
    pairs = heads // 2
    by_pair = pl.BlockSpec((rows, 128), lambda h: (0, h // 2))
    return pl.pallas_call(
        lambda *refs: attend_kernel(seq, local, heads, *refs),
        grid=(heads,),
        in_specs=[ANY, by_pair, by_pair, by_pair],
        out_specs=[
            pl.BlockSpec((1, rows, rows), lambda h: (h, 0, 0)),
            by_pair,
            by_pair,
            ANY,
            ANY,
        ],
        out_shape=[
            jax.ShapeDtypeStruct((heads, rows, rows), BF16),
            jax.ShapeDtypeStruct((rows, mine), F32),
            jax.ShapeDtypeStruct((rows, mine), F32),
            jax.ShapeDtypeStruct((2, pairs, rows, 128), BF16),
            jax.ShapeDtypeStruct((seq, 2, half, width), BF16),
        ],
        scratch_shapes=GATHER_SEMS(seq)
        + [
            pltpu.VMEM((pairs, rows, 128), BF16),
            pltpu.VMEM((rows, 128), BF16),
            pltpu.VMEM((rows, 128), BF16),
            pltpu.SemaphoreType.DMA((pairs,)),
            pltpu.SemaphoreType.DMA((pairs,)),
            pltpu.SemaphoreType.DMA((pairs,)),
        ],
        compiler_params=pltpu.CompilerParams(
            collective_id=1, has_side_effects=True, vmem_limit_bytes=LIMIT
        ),
        name="attend",
    )(cot_send, q, k, v)


def gelu_parts(u):
    x = jnp.abs(u) * (1.0 / math.sqrt(2.0))
    t = 1.0 / (1.0 + 0.3275911 * x)
    poly = t * (
        0.254829592
        + t * (-0.284496736 + t * (1.421413741 + t * (-1.453152027 + t * 1.061405429)))
    )
    expo = jnp.exp(-x * x)
    tail = 0.5 * poly * expo
    phi = jnp.where(u >= 0, 1.0 - tail, tail)
    return phi, u * expo * (1.0 / math.sqrt(2.0 * math.pi))


def dense_kernel(
    seq, x, mixed, cot, wo, wi, wu, vecs, ibias,
    out_own, gres_own, gm_out, gwo_out, gwi_out, gwu_out, gvec_out, gib_out,
    n2, hat2, inv2, keep, gown, pstage, precv, gstage, grecv, psem, prsem, gsem, grsem,
):
    f, z, m, c = where_am_i()
    other = (m * 2 + 1 - c, z)
    meet([other])
    half = x.shape[2]
    chunk = 2 * half
    width = x.shape[3]
    mine = gm_out.shape[1]
    obias, gain, shift, ubias = vecs[4:5, :], vecs[5:6, :], vecs[6:7, :], vecs[7:8, :]
    gvec_out[...] = jnp.zeros_like(gvec_out)
    gib_out[...] = jnp.zeros_like(gib_out)
    gwo_out[...] = jnp.zeros_like(gwo_out)
    gwi_out[...] = jnp.zeros_like(gwi_out)
    gwu_out[...] = jnp.zeros_like(gwu_out)

    def p_copy(i):
        return remote(pstage.at[i], precv.at[i], psem.at[i], prsem.at[i], other)

    def g_copy(i):
        return remote(gstage.at[i], grecv.at[i], gsem.at[i], grsem.at[i], other)

    def mixed_rows(i):
        rows = pl.ds(i * chunk, chunk)
        return jnp.concatenate(
            [mixed[a, p, rows, :] for a in range(2) for p in range(mixed.shape[1])], axis=1
        )

    def first(i, _):
        rows = pl.ds(i * chunk, chunk)
        resid = (
            x[i].reshape(chunk, width).astype(F32) + nn(mixed_rows(i), wo[...]) + obias
        )
        hat, inv = normalize(resid)
        normed = (hat * gain + shift).astype(BF16)
        n2[rows, :] = normed
        hat2[rows, :] = hat
        inv2[rows, :] = jnp.broadcast_to(inv, (chunk, 128))
        inner = nn(normed, wi[...]) + ibias[...]
        phi, bump = gelu_parts(inner)
        active = (inner * phi).astype(BF16)
        slope = phi + bump
        pout = nn(active, wu[...])
        full = resid + ubias

        @pl.when(c == 0)
        def _():
            keep[i] = full[:half] + pout[:half]
            pstage[i] = pout[half:]

        @pl.when(c == 1)
        def _():
            keep[i] = full[half:] + pout[half:]
            pstage[i] = pout[:half]

        p_copy(i).start()
        g = cot[i].reshape(chunk, width)
        gi = (nt(g, wu[...]) * slope).astype(BF16)
        gn2 = nt(gi, wi[...])
        gown[i] = gn2
        gstage[i] = gn2.astype(gstage.dtype)
        g_copy(i).start()
        gwu_out[...] += tn(active, g)
        gwi_out[...] += tn(normed, gi)
        gib_out[...] += jnp.sum(gi.astype(F32), 0, keepdims=True)
        gvec_out[0:1, :] += jnp.sum(g.astype(F32), 0, keepdims=True)
        return 0

    def second(i, _):
        rows = pl.ds(i * chunk, chunk)
        g_copy(i).wait_recv()
        gn2 = gown[i] + grecv[i].astype(F32)
        hat = hat2[rows, :]
        gvec_out[1:2, :] += jnp.sum(gn2 * hat, 0, keepdims=True)
        gvec_out[2:3, :] += jnp.sum(gn2, 0, keepdims=True)
        g = cot[i].reshape(chunk, width).astype(F32)
        gres = g + norm_back(gn2, gain, hat, inv2[rows, 0:1])
        branch = gres.astype(BF16)
        gvec_out[3:4, :] += jnp.sum(branch.astype(F32), 0, keepdims=True)
        wrows = pl.ds(pl.multiple_of(c * mine, 128), mine)
        gm_out[rows, :] = nt(branch, wo[wrows, :]).astype(BF16)
        mix = mixed_rows(i)

        @pl.when(c == 0)
        def _():
            gres_own[i] = gres[:half]
            gwo_out[...] += tn(mix, branch[:, :mine])

        @pl.when(c == 1)
        def _():
            gres_own[i] = gres[half:]
            gwo_out[...] += tn(mix, branch[:, mine:])

        p_copy(i).wait_recv()
        out_own[i] = (keep[i] + precv[i]).astype(BF16)
        return 0

    lax.fori_loop(0, seq, first, 0)
    lax.fori_loop(0, seq, second, 0)

    def last(i, _):
        p_copy(i).wait_send()
        g_copy(i).wait_send()
        return 0

    lax.fori_loop(0, seq, last, 0)


def dense(x, mixed, cot, wo, wi, wu, vecs, ibias):
    seq, _, half, width = x.shape
    rows = seq * 2 * half
    hidden = wi.shape[1]
    mine = width // 2
    return pl.pallas_call(
        lambda *refs: dense_kernel(seq, *refs),
        in_specs=[VMEM] * 8,
        out_specs=[VMEM] * 8,
        out_shape=[
            jax.ShapeDtypeStruct((seq, half, width), BF16),
            jax.ShapeDtypeStruct((seq, half, width), F32),
            jax.ShapeDtypeStruct((rows, mine), BF16),
            jax.ShapeDtypeStruct((width, mine), F32),
            jax.ShapeDtypeStruct((width, hidden), F32),
            jax.ShapeDtypeStruct((hidden, width), F32),
            jax.ShapeDtypeStruct((8, width), F32),
            jax.ShapeDtypeStruct((1, hidden), F32),
        ],
        scratch_shapes=[
            pltpu.VMEM((rows, width), BF16),
            pltpu.VMEM((rows, width), F32),
            pltpu.VMEM((rows, 128), F32),
            pltpu.VMEM((seq, half, width), F32),
            pltpu.VMEM((seq, 2 * half, width), F32),
            pltpu.VMEM((seq, half, width), F32),
            pltpu.VMEM((seq, half, width), F32),
            pltpu.VMEM((seq, 2 * half, width), BF16),
            pltpu.VMEM((seq, 2 * half, width), BF16),
            pltpu.SemaphoreType.DMA((seq,)),
            pltpu.SemaphoreType.DMA((seq,)),
            pltpu.SemaphoreType.DMA((seq,)),
            pltpu.SemaphoreType.DMA((seq,)),
        ],
        compiler_params=pltpu.CompilerParams(
            collective_id=2, has_side_effects=True, vmem_limit_bytes=LIMIT
        ),
        name="dense",
    )(x, mixed, cot, wo, wi, wu, vecs, ibias)


def attend_back_kernel(
    seq, heads, out_own, q, k, v, gm, o, linv, e, gq_out, gk_out, gv_out, out_back,
    ssem, rsem, do, dot_, qt, va, km, dqs, dvt, dkt,
):
    h = pl.program_id(0)
    parity = h % 2
    rows = q.shape[0]
    back = Return(out_own, out_back, ssem, rsem, seq)

    @pl.when(h == 0)
    def _():
        meet(column_peers(seq))
        back.start()

    mine, first = own_lanes(parity)
    third = HD ** (-0.5)
    scaled = (gm[...].astype(F32) * linv[...]).astype(BF16).astype(F32)
    scaled = jnp.where(mine, scaled, 0.0)
    delta = jnp.sum(scaled * o[...], -1, keepdims=True)
    high = delta.astype(BF16).astype(F32)
    middle = (delta - high).astype(BF16).astype(F32)
    low = delta - high - middle
    lane = lax.broadcasted_iota(jnp.int32, (1, 128), 1)
    base = HD * (1 - parity)
    do[...] = (
        scaled
        - jnp.where(lane == base, high, 0.0)
        - jnp.where(lane == base + 1, middle, 0.0)
        - jnp.where(lane == base + 2, low, 0.0)
    ).astype(BF16)
    ones = jnp.logical_and(lane >= base, lane < base + 3)
    va[...] = jnp.where(mine, v[...].astype(F32), jnp.where(ones, 1.0, 0.0)).astype(BF16)
    km[...] = jnp.where(mine, k[...].astype(F32), 0.0).astype(BF16)
    dot_[...] = do[...].T
    qt[...] = q[...].T
    sub = pl.ds(pl.multiple_of(parity * HD, HD), HD)
    for i in range(rows // QB):
        sl = slice(i * QB, (i + 1) * QB)
        p = e[0, sl, :]
        dp = nt(do[sl, :], va[...])
        ds = (p.astype(F32) * dp).astype(BF16)
        dq = nn(ds, km[...])

        @pl.when(parity == 0)
        def _():
            dqs[sl, :] = dq

        @pl.when(parity == 1)
        def _():
            gq_out[sl, :] = ((dqs[sl, :] + dq) * third).astype(BF16)

        a = nn(dot_[sub, sl], p)
        b = nn(qt[sub, sl], ds)
        if i == 0:
            dvt[sub, :] = a
            dkt[sub, :] = b
        else:
            dvt[sub, :] += a
            dkt[sub, :] += b

    @pl.when(parity == 1)
    def _():
        gv_out[...] = dvt[...].T.astype(BF16)
        gk_out[...] = (dkt[...] * third).T.astype(BF16)

    @pl.when(h == heads - 1)
    def _():
        back.finish()


def attend_back(out_own, q, k, v, gm, o, linv, e):
    rows, mine = q.shape
    heads = mine // HD
    seq, half, width = out_own.shape
    by_pair = pl.BlockSpec((rows, 128), lambda h: (0, h // 2))
    return pl.pallas_call(
        lambda *refs: attend_back_kernel(seq, heads, *refs),
        grid=(heads,),
        in_specs=[ANY] + [by_pair] * 6 + [pl.BlockSpec((1, rows, rows), lambda h: (h, 0, 0))],
        out_specs=[by_pair] * 3 + [ANY],
        out_shape=[jax.ShapeDtypeStruct((rows, mine), BF16)] * 3
        + [jax.ShapeDtypeStruct((2, 2, half, width), BF16)],
        scratch_shapes=RETURN_SEMS(seq)
        + [
            pltpu.VMEM((rows, 128), BF16),
            pltpu.VMEM((128, rows), BF16),
            pltpu.VMEM((128, rows), BF16),
            pltpu.VMEM((rows, 128), BF16),
            pltpu.VMEM((rows, 128), BF16),
            pltpu.VMEM((rows, 128), F32),
            pltpu.VMEM((128, rows), F32),
            pltpu.VMEM((128, rows), F32),
        ],
        compiler_params=pltpu.CompilerParams(
            collective_id=3, has_side_effects=True, vmem_limit_bytes=LIMIT
        ),
        name="attend_back",
    )(out_own, q, k, v, gm, o, linv, e)


def project_back_kernel(
    seq, x, n1, gq, gk, gv, gres, wqkv, vecs, gw_out, gvec_out, ig_back,
    gown, gstage, grecv, ig_own, gsem, grsem, ssem, rsem,
):
    f, z, m, c = where_am_i()
    other = (m * 2 + 1 - c, z)
    meet(column_peers(seq))
    half = x.shape[2]
    chunk = 2 * half
    width = x.shape[3]
    mine = gq.shape[1]
    gain = vecs[0:1, :]

    def g_copy(i):
        return remote(gstage.at[i], grecv.at[i], gsem.at[i], grsem.at[i], other)

    def grads(i):
        rows = pl.ds(i * chunk, chunk)
        return jnp.concatenate([gq[rows, :], gk[rows, :], gv[rows, :]], axis=1)

    gw_out[...] = jnp.zeros_like(gw_out)
    gvec_out[...] = jnp.zeros_like(gvec_out)

    def first(i, _):
        gn1 = nt(grads(i), wqkv[...])

        @pl.when(c == 0)
        def _():
            gown[i] = gn1[:half]
            gstage[i] = gn1[half:]

        @pl.when(c == 1)
        def _():
            gown[i] = gn1[half:]
            gstage[i] = gn1[:half]

        g_copy(i).start()
        return 0

    def second(i, _):
        g_copy(i).wait_recv()
        gn1 = gown[i] + grecv[i]
        hat, inv = normalize(x[i, c].astype(F32))
        gvec_out[0:1, :] += jnp.sum(gn1 * hat, 0, keepdims=True)
        gvec_out[1:2, :] += jnp.sum(gn1, 0, keepdims=True)
        ig_own[i] = (gres[i] + norm_back(gn1, gain, hat, inv)).astype(BF16)
        return 0

    lax.fori_loop(0, seq, first, 0)
    lax.fori_loop(0, seq, second, 0)
    back = Return(ig_own, ig_back, ssem, rsem, seq)
    back.start()

    def third(i, _):
        rows = pl.ds(i * chunk, chunk)
        g = grads(i)
        gw_out[...] += tn(n1[rows, :], g)
        gvec_out[2:3, :mine] += jnp.sum(g[:, :mine].astype(F32), 0, keepdims=True)
        gvec_out[3:4, :mine] += jnp.sum(g[:, 2 * mine :].astype(F32), 0, keepdims=True)
        return 0

    lax.fori_loop(0, seq, third, 0)

    def last(i, _):
        g_copy(i).wait_send()
        return 0

    lax.fori_loop(0, seq, last, 0)
    back.finish()


def project_back(x, n1, gq, gk, gv, gres, wqkv, vecs):
    seq, _, half, width = x.shape
    return pl.pallas_call(
        lambda *refs: project_back_kernel(seq, *refs),
        in_specs=[VMEM] * 8,
        out_specs=[VMEM, VMEM, ANY],
        out_shape=[
            jax.ShapeDtypeStruct(wqkv.shape, F32),
            jax.ShapeDtypeStruct((8, width), F32),
            jax.ShapeDtypeStruct((2, 2, half, width), BF16),
        ],
        scratch_shapes=[
            pltpu.VMEM((seq, half, width), F32),
            pltpu.VMEM((seq, half, width), F32),
            pltpu.VMEM((seq, half, width), F32),
            pltpu.VMEM((seq, half, width), BF16),
            pltpu.SemaphoreType.DMA((seq,)),
            pltpu.SemaphoreType.DMA((seq,)),
        ]
        + RETURN_SEMS(seq),
        compiler_params=pltpu.CompilerParams(
            collective_id=4, has_side_effects=True, vmem_limit_bytes=LIMIT
        ),
        name="project_back",
    )(x, n1, gq, gk, gv, gres, wqkv, vecs)


def per_device(
    frames,
    cotangent,
    valid_slots,
    first_gain,
    first_shift,
    query_weight,
    query_bias,
    key_weight,
    value_weight,
    value_bias,
    output_weight,
    output_bias,
    second_gain,
    second_shift,
    inner_weight,
    inner_bias,
    outer_weight,
    outer_bias,
):
    seq = lax.axis_size("seq")
    n_f = lax.axis_size("fsdp")
    f = lax.axis_index("fsdp")
    c = f % 2
    slots, local, width = frames.shape
    chunk = -(-local // 128) * 128
    half = chunk // 2
    mine = width // 2
    hidden = n_f * inner_bias.shape[0]
    piece = hidden // n_f

    def gathered(value):
        return lax.all_gather(value, "fsdp", axis=0, tiled=True)

    def my_columns(value):
        return lax.dynamic_slice_in_dim(value, c * mine, mine, axis=1)

    keep = valid_slots.astype(BF16)[:, None, None]
    pad = ((0, 0), (0, chunk - local), (0, 0))
    x_send = jnp.pad(frames, pad).reshape(slots, 2, half, width)
    cot_send = jnp.pad(cotangent * keep, pad).reshape(slots, 2, half, width)
    wqkv = jnp.concatenate(
        [my_columns(gathered(w)) for w in (query_weight, key_weight, value_weight)], axis=1
    )
    wo = gathered(output_weight)
    wi = gathered(inner_weight).reshape(width, n_f // 2, 2, piece)
    wi = lax.dynamic_index_in_dim(wi, c, 2, keepdims=False).reshape(width, hidden // 2)
    wu = gathered(outer_weight).reshape(n_f // 2, 2, piece, width)
    wu = lax.dynamic_index_in_dim(wu, c, 1, keepdims=False).reshape(hidden // 2, width)
    small = jnp.stack(
        [
            first_gain,
            first_shift,
            query_bias,
            value_bias,
            output_bias,
            second_gain,
            second_shift,
            outer_bias,
        ]
    )
    vecs = lax.all_gather(small, "fsdp", axis=1, tiled=True).astype(F32)
    ibias = gathered(inner_bias).astype(F32).reshape(n_f // 2, 2, piece)
    ibias = lax.dynamic_index_in_dim(ibias, c, 1, keepdims=False).reshape(1, hidden // 2)

    x, n1, q, k, v = project(x_send, wqkv, vecs, seq)
    e, o, linv, mixed, cot = attend(cot_send, q, k, v, local, seq)
    out_own, gres, gm, gwo, gwi, gwu, gvec_b, gib = dense(x, mixed, cot, wo, wi, wu, vecs, ibias)
    gq, gk, gv, out_back = attend_back(out_own, q, k, v, gm, o, linv, e)
    gw, gvec_a, ig_back = project_back(x, n1, gq, gk, gv, gres, wqkv, vecs)

    keep32 = valid_slots.astype(F32)[:, None, None]
    outputs = (out_back.reshape(slots, chunk, width)[:, :local].astype(F32) * keep32).astype(BF16)
    input_grad = ig_back.reshape(slots, chunk, width)[:, :local]

    def both_columns(value):
        wide = jnp.zeros((value.shape[0], 2 * mine), F32)
        return lax.dynamic_update_slice_in_dim(wide, value, c * mine, axis=1)

    def both_blocks(value, axis):
        shape = list(value.shape)
        shape[axis : axis + 1] = [n_f // 2, 1, piece]
        full = list(shape)
        full[axis + 1] = 2
        wide = jnp.zeros(full, F32)
        wide = lax.dynamic_update_slice_in_dim(wide, value.reshape(shape), c, axis=axis + 1)
        shape = list(value.shape)
        shape[axis] = hidden
        return wide.reshape(shape)

    def reduced(value):
        return lax.psum_scatter(
            lax.psum(value, "seq"), "fsdp", scatter_dimension=0, tiled=True
        )

    grads = dict(
        first_gain=gvec_a[0],
        first_shift=gvec_a[1],
        query_weight=both_columns(gw[:, :mine]),
        query_bias=both_columns(gvec_a[2:3, :mine])[0],
        key_weight=both_columns(gw[:, mine : 2 * mine]),
        value_weight=both_columns(gw[:, 2 * mine :]),
        value_bias=both_columns(gvec_a[3:4, :mine])[0],
        output_weight=both_columns(gwo),
        output_bias=0.5 * gvec_b[3],
        second_gain=0.5 * gvec_b[1],
        second_shift=0.5 * gvec_b[2],
        inner_weight=both_blocks(gwi, 1),
        inner_bias=both_blocks(gib, 1)[0],
        outer_weight=both_blocks(gwu, 0),
        outer_bias=0.5 * gvec_b[0],
    )
    return (outputs, input_grad) + tuple(reduced(value) for value in grads.values())


def solution(mesh):
    rows = P("fsdp", "seq", None)
    vector, matrix = P("fsdp"), P("fsdp", None)
    weights = (
        vector,
        vector,
        matrix,
        vector,
        matrix,
        matrix,
        vector,
        matrix,
        vector,
        vector,
        vector,
        matrix,
        vector,
        matrix,
        vector,
    )
    return jax.shard_map(
        per_device,
        mesh=mesh,
        in_specs=(rows, rows, vector) + weights,
        out_specs=(rows, rows) + weights,
        check_vma=False,
    )
```

time: 1100 us -> 861 us (0.78)
  matrix products: 288 us -> 0 us
  Pallas kernels: 0 us -> 219 us
  blocking collectives: 153 us -> 57.7 us
  other arithmetic: 91.8 us -> 4.53 us
  local copies, waits for them, and re-layouts: 133 us -> 183 us
  starting transfers between devices: 25.4 us -> 0.52 us
  waiting for transfers between devices: 385 us -> 368 us
    dot_general x32 -> x0, matrix products: 288 us -> none  [the longest x6 47.4 us: product(): return jnp.dot(left, right, preferred_element_type=jnp.float32)]
    pallas_call x0 -> x5, Pallas kernels: none -> 219 us  [the longest x1 55 us: dense(): pl.pallas_call(lambda *refs: dense_kernel(seq, *refs), in_specs=[VMEM] *...]
    all_to_all x6 -> x0, waiting for transfers between devices: 134 us -> none  [the longest x1 32 us: per_device(): lax.all_to_all(to_frames(heads_gv), 'seq', split_axis=1, concat_axis=2, t...]
    dynamic_update_slice x0 -> x9, local copies, waits for them, and re-layouts: none -> 89.4 us  [the longest x3 84.8 us: both_blocks(): lax.dynamic_update_slice_in_dim(wide, value.reshape(shape), c, axis=axis...]
    all_to_all x2 -> x0, blocking collectives: 77.9 us -> none  [the longest x1 39 us: per_device(): lax.all_to_all(to_frames(heads_gk), 'seq', split_axis=1, concat_axis=2, t...]
    convert_element_type x15 -> x2, other arithmetic: 53.4 us -> 1.97 us  [the longest x1 1.96 us: per_device(): (out_back.reshape(slots, chunk, width)[:, :local].astype(F32) * keep32).a...]
    all_gather x6, waiting for transfers between devices: 0.1 us -> 51 us  [gathered(): return lax.all_gather(value, 'fsdp', axis=0, tiled=True)]
    reduce_scatter x6, waiting for transfers between devices: 177 us -> 222 us  [reduced(): lax.psum_scatter(lax.psum(value, 'seq'), 'fsdp', scatter_dimension=0, til...]
  transfers between devices with their start and end apart: 19 -> 13, of which waited for: 10 -> 8; matrix products, arithmetic and copies ran while one was open for 43% -> 20% of each run, Pallas kernels for 0% -> 10%
where the time goes in v1:
time: 861 us; the launch traced here: 849 us
  waiting for transfers between devices  368 us (43%)
  Pallas kernels  219 us (25%)
  local copies, waits for them, and re-layouts  183 us (21%)
  blocking collectives  57.7 us (7%)
  between operations  16.2 us (2%)
    reduce_scatter x6, waiting for transfers between devices, reduced(): lax.psum_scatter(lax.psum(value, 'seq'), 'fsdp', scatter_dimension=0, til...  222 us
    psum x1, waiting for transfers between devices, reduced(): lax.psum(value, 'seq')  91.5 us
    dynamic_update_slice x3, local copies, waits for them, and re-layouts, both_blocks(): lax.dynamic_update_slice_in_dim(wide, value.reshape(shape), c, axis=axis...  84.8 us
    pallas_call x1, Pallas kernels, dense(): pl.pallas_call(lambda *refs: dense_kernel(seq, *refs), in_specs=[VMEM] *...  55 us
    all_gather x6, waiting for transfers between devices, gathered(): return lax.all_gather(value, 'fsdp', axis=0, tiled=True)  51 us
    pallas_call x1, Pallas kernels, attend(): pl.pallas_call(lambda *refs: attend_kernel(seq, local, heads, *refs), gri...  49.7 us
    pallas_call x1, Pallas kernels, attend_back(): pl.pallas_call(lambda *refs: attend_back_kernel(seq, heads, *refs), grid=...  42.6 us
    pallas_call x1, Pallas kernels, project(): pl.pallas_call(lambda *refs: project_kernel(seq, *refs), in_specs=[ANY, V...  36.9 us
  transfers between devices with their start and end apart: 13, of which 8 were waited for; matrix products, arithmetic and copies ran while one was open for 20% of the time, Pallas kernels for 10%

profile of v1, /device:TPU:0, one launch (start us, length us, event | category | flops | bytes accessed | tf_op | source)
XLA Modules:
  0.0 848.9 jit_solution(64142282700411466)
XLA Ops:
  11.6 10.3 %all-gather = bf16[8,96,8]{1,2,0:T(8,128)(2,1)S(1)} all-gather(bf16[1,96,8]{1,2,0:T(8,128)(2,1)S(1)} %bitcast.46), channel_id=1, replica_groups=mesh['fsdp'=8,'seq'=4] {'fsdp'}, dimensions={0}, use_global_device_ids=true | all-gather | bytes 13824 | tf_op jit(solution)/shard_map/all_gather | solution.py:792
  26.0 8.9 %all-gather.1 = bf16[8,1,384]{2,1,0:T(2,128)(2,1)S(1)} all-gather(bf16[1,1,384]{2,1,0:T(2,128)(2,1)S(1)} %reshape.119), channel_id=1, replica_groups=mesh['fsdp'=8,'seq'=4] {'fsdp'}, dimensions={0}, use_global_device_ids=true | all-gather | bytes 6912 | tf_op jit(solution)/shard_map/all_gather | solution.py:763
  38.0 24.8 %all-gather.11.cloned.1.call-done = bf16[768,768]{1,0:T(8,128)(2,1)} async-done(((bf16[96,768]{1,0:T(8,128)(2,1)}), bf16[768,768]{1,0:T(8,128)(2,1)}) %all-gather.11.cloned.1.call-update) | async-done | bytes 1179664 | tf_op jit(solution)/shard_map/all_gather | solution.py:763
  64.0 24.9 %all-gather.9.cloned.1.call-done = bf16[768,768]{1,0:T(8,128)(2,1)} async-done(((bf16[96,768]{1,0:T(8,128)(2,1)}), bf16[768,768]{1,0:T(8,128)(2,1)}) %all-gather.9.cloned.1.call-update) | async-done | bytes 1179664 | tf_op jit(solution)/shard_map/all_gather | solution.py:763
  91.4 36.9 %project.1 = (bf16[4,2,192,768]{3,2,1,0:T(8,128)(2,1)}, bf16[1536,768]{1,0:T(8,128)(2,1)}, bf16[1536,384]{1,0:T(8,128)(2,1)}, bf16[1536,384]{1,0:T(8,128)(2,1)}, bf16[1536,384]{1,0:T(8,128)(2,1)}) custom-call(bf16[2,2,192,768]{3,2,1,0:T(8,128)(2,1)} %bitcast.38, bf16[768,1152]{1,0:T(8,128)(2,1)} %pad_maximum_fusion.refs_1_.refs_6_, f32[8,768]{1,0:T(8,128)} %bitcast.42), custom_call_target="tpu_custom_call" | custom-call | tf_op jit(solution)/shard_map/project/pallas_call | solution.py:233
  128.3 49.7 %attend.1 = (bf16[6,1536,1536]{2,1,0:T(8,128)(2,1)}, f32[1536,384]{1,0:T(8,128)}, f32[1536,384]{1,0:T(8,128)}, bf16[2,3,1536,128]{3,2,1,0:T(8,128)(2,1)}, bf16[4,2,192,768]{3,2,1,0:T(8,128)(2,1)}) custom-call(bf16[2,2,192,768]{3,2,1,0:T(8,128)(2,1)} %bitcast.37, bf16[1536,384]{1,0:T(8,128)(2,1)} %get-tuple-element.43.refs_1_, ...), custom_call_target="tpu_custom_call" | custom-call | tf_op jit(solution)/shard_map/attend/pallas_call | solution.py:334
  178.0 11.6 %reshape.101 = bf16[768,4,2,384]{3,2,1,0:T(2,128)(2,1)} reshape(bf16[768,3072]{1,0:T(8,128)(2,1)} %all-gather.17.cloned.1.call-done) | data formatting | bytes 9437184 | tf_op jit(solution)/shard_map/reshape | solution.py:776
  189.6 16.3 %dynamic-slice_reduce_fusion = bf16[768,4,384]{2,1,0:T(4,128)(2,1)S(1)} fusion(bf16[768,4,2,384]{3,2,1,0:T(2,128)(2,1)} %reshape.101, s32[]{:T(128)S(6)} %select_n.19), kind=kLoop, calls=%fused_computation | loop fusion | bytes 4718596 | tf_op jit(solution)/shard_map/jit(dynamic_index_in_dim)/dynamic_slice | solution.py:777
  206.0 1.8 copy.71
  207.8 3.3 constant_dynamic-slice_fusion.1
  211.1 55.0 %dense.1 = (bf16[4,192,768]{2,1,0:T(8,128)(2,1)}, f32[4,192,768]{2,1,0:T(8,128)}, bf16[1536,384]{1,0:T(8,128)(2,1)}, f32[768,384]{1,0:T(8,128)}, f32[768,1536]{1...) custom-call(bf16[4,2,192,768]{3,2,1,0:T(8,128)(2,1)} %get-tuple-element.42.refs_0_, ...), custom_call_target="tpu_custom_call" | custom-call | tf_op jit(solution)/shard_map/dense/pallas_call | solution.py:497
  266.1 42.6 %attend_back.1 = (bf16[1536,384]{1,0:T(8,128)(2,1)}, bf16[1536,384]{1,0:T(8,128)(2,1)}, bf16[1536,384]{1,0:T(8,128)(2,1)}, bf16[2,2,192,768]{3,2,1,0:T(8,128)(2,1)}) custom-call(bf16[4,192,768]{2,1,0:T(8,128)(2,1)} %get-tuple-element.48.refs_0_, bf16[1536,384]{1,0:T(8,128)(2,1)} %get-tuple-element.43.refs_1_, bf16[1536,384]{1,0:T(8,128)(2,1)} %get-tuple-element.44.refs_2_, ...), custom_call_target="tpu_custom_call" | custom-call | tf_op jit(solution)/shard_map/attend_back/pallas_call | solution.py:608
  308.7 35.2 %project_back.1 = (f32[768,1152]{1,0:T(8,128)}, f32[8,768]{1,0:T(8,128)}, bf16[2,2,192,768]{3,2,1,0:T(8,128)(2,1)}) custom-call(bf16[4,2,192,768]{3,2,1,0:T(8,128)(2,1)} %get-tuple-element.42.refs_0_, bf16[1536,768]{1,0:T(8,128)(2,1)} %get-tuple-element.54.refs_1_, bf16[1536,384]{1,0:T(8,128)(2,1)} %get-tuple-element.55.refs_2_, ...), custom_call_target="tpu_custom_call" | custom-call | tf_op jit(solution)/shard_map/project_back/pallas_call | solution.py:706
  355.2 8.5 %reshape.134 = f32[768,4,1,384]{3,2,1,0:T(1,128)} reshape(f32[768,1536]{1,0:T(8,128)} %get-tuple-element.64) | data formatting | bytes 9437184 | tf_op jit(solution)/shard_map/reshape | solution.py:816
  363.7 6.1 broadcast_in_dim.11
  369.8 82.2 %dynamic_update_slice.35 = f32[768,4,2,384]{3,2,1,0:T(2,128)} dynamic-update-slice(f32[768,4,2,384]{3,2,1,0:T(2,128)} %broadcast_in_dim.11, f32[768,4,1,384]{3,2,1,0:T(1,128)} %reshape.134, s32[]{:T(128)} %constant.25.clone.1, s32[]{:T(128)} %constant.25.clone.1, s32[]{:T(128)S(6)} %select_n.19, s32[]{:T(128)} %constant.25.clone.1) | dynamic-update-slice | bytes 9437188 | tf_op jit(solution)/shard_map/dynamic_update_slice | solution.py:816
  452.0 13.0 %reshape.111 = f32[768,3072]{1,0:T(8,128)} reshape(f32[768,4,2,384]{3,2,1,0:T(2,128)} %dynamic_update_slice.35) | data formatting | bytes 18874368 | tf_op jit(solution)/shard_map/reshape | solution.py:819
  465.1 4.6 broadcast_in_dim.13
  469.7 2.6 constant_dynamic-update-slice_fusion
  472.4 15.6 %reduce-scatter.11.cloned.1.call-done = f32[96,768]{1,0:T(8,128)} async-done(((f32[768,768]{1,0:T(8,128)}), f32[96,768]{1,0:T(8,128)}) %reduce-scatter.11.cloned.1.call-update) | async-done | bytes 294928 | tf_op jit(solution)/shard_map/reduce_scatter | solution.py:822
  488.1 46.1 %reduce-scatter.13.cloned.1.call-done = f32[96,768]{1,0:T(8,128)} async-done(((f32[768,768]{1,0:T(8,128)}), f32[96,768]{1,0:T(8,128)}) %reduce-scatter.13.cloned.1.call-update) | async-done | bytes 294928 | tf_op jit(solution)/shard_map/reduce_scatter | solution.py:822
  534.1 80.0 %reduce-scatter.15.cloned.1.call-done = f32[96,3072]{1,0:T(8,128)} async-done(((f32[768,3072]{1,0:T(8,128)}), f32[96,3072]{1,0:T(8,128)}) %reduce-scatter.15.cloned.1.call-update) | async-done | bytes 1179664 | tf_op jit(solution)/shard_map/reduce_scatter | solution.py:822
  614.2 79.9 %reduce-scatter.17.cloned.1.call-done = f32[384,768]{1,0:T(8,128)} async-done(((f32[3072,768]{1,0:T(8,128)}), f32[384,768]{1,0:T(8,128)}) %reduce-scatter.17.cloned.1.call-update) | async-done | bytes 1179664 | tf_op jit(solution)/shard_map/reduce_scatter | solution.py:822
  696.2 1.9 copy.68
  700.3 24.8 %all-reduce.11 = (f32[768]{0:T(1024)S(1)}, f32[768]{0:T(1024)S(1)}, f32[768]{0:T(1024)S(1)}, f32[768]{0:T(1024)S(1)}, f32[768]{0:T(1024)S(1)}, /*index=5*/f32[76...) all-reduce(f32[768]{0:T(1024)S(1)} %get-tuple-element.74, ...), channel_id=2, replica_groups=mesh['fsdp'=8,'seq'=4] {'fsdp'}, use_global_device_ids=true, to_apply=%region_1.2.clone | all-reduce | flops 9216 | bytes 73728
  725.8 13.7 %all-reduce.12 = (f32[96]{0:T(128)}, f32[96]{0:T(128)}, f32[96]{0:T(128)}, f32[96]{0:T(128)}, f32[96]{0:T(128)}, /*index=5*/f32[96]{0:T(128)}, f32[96]{0:T(128)}, f32[384]{0:T(512)}, f32[96]{0:T(128)}) all-reduce(f32[96]{0:T(128)S(1)} %dynamic-slice.1, f32[96]{0:T(128)S(1)} %dynamic-slice.3, ...), channel_id=1, replica_groups=mesh['fsdp'=8,'seq'=4] {'seq'}, use_global_device_ids=true, to_apply=%region_0.1 | all-reduce | flops 1152 | bytes 9216 | tf_op jit(solution)/shard_map/psum | solution.py:823
  739.5 2.0 multiply_convert_fusion
  741.4 91.5 %all-reduce.16.cloned.1.call-done = (f32[96,768]{1,0:T(8,128)}, f32[96,768]{1,0:T(8,128)}, f32[96,768]{1,0:T(8,128)}, f32[96,768]{1,0:T(8,128)}, f32[96,3072]{1,0:T(8,128)}, /*index=5*/f32[384,768]{1,0:T(8,128)}) async-done(((f32[96,768]{1,0:T(8,128)}, f32[96,768]{1,0:T(8,128)}, f32[96,768]{1,0:T(8,128)}, f32[96,768]{1,0:T(8,128)}, f32[96,3072]{1,0:T(8,128)}, /*index=5*/f32[384,768]{1,0:T(8,128)}), ...) | async-done | bytes 3538960 | tf_op jit(solution)/shard_map/psum | solution.py:823
  832.9 1.8 copy.88
  834.8 1.7 copy.89
  836.5 1.7 copy.90
  838.2 1.7 copy.91
  (134 shorter events, 31.9 us)
Async XLA Ops:
  7.2 4.1 copy-start.7
  7.2 4.3 copy-start.14
  7.2 4.3 copy-start.15
  7.2 4.3 copy-start.16
  7.2 4.3 copy-start.17
  7.2 4.3 copy-start.18
  7.3 4.3 copy-start.19
  7.3 4.3 copy-start.20
  7.3 4.3 copy-start.21
  7.3 15.3 %copy-start.22 = (s32[2]{0:T(128)S(1)}, s32[2]{0:T(128)}, u32[]{:S(2)}) copy-start(s32[2]{0:T(128)} %param.20) | copy-start | bytes 28
  7.3 15.3 %copy-start.8 = (bf16[2,375,768]{2,0,1:T(2,128)(2,1)S(1)}, bf16[2,375,768]{2,0,1:T(2,128)(2,1)}, u32[]{:S(2)}) copy-start(bf16[2,375,768]{2,0,1:T(2,128)(2,1)} %param.19) | copy-start | bytes 3456004
  7.3 29.6 %all-gather.13.cloned.1.call-start = ((), (), s32[]{:S(2)}) async-start(), calls=%async_computation.8 | async-start | bytes 1327104 | tf_op jit(solution)/shard_map/all_gather | solution.py:763
  8.0 54.8 %all-gather.11.cloned.1.call-start = ((), (), s32[]{:S(2)}) async-start(), calls=%async_computation.7 | async-start | bytes 1327104 | tf_op jit(solution)/shard_map/all_gather | solution.py:763
  8.8 80.0 %all-gather.9.cloned.1.call-start = ((), (), s32[]{:S(2)}) async-start(), calls=%async_computation.6 | async-start | bytes 1327104 | tf_op jit(solution)/shard_map/all_gather | solution.py:763
  9.5 168.5 %all-gather.17.cloned.1.call-start = ((), (), s32[]{:S(2)}) async-start(), calls=%async_computation.10 | async-start | bytes 5308416 | tf_op jit(solution)/shard_map/all_gather | solution.py:763
  10.1 197.7 %all-gather.19.cloned.1.call-start = ((), (), s32[]{:S(2)}) async-start(), calls=%async_computation.11 | async-start | bytes 5308416 | tf_op jit(solution)/shard_map/all_gather | solution.py:763
  10.7 200.4 %all-gather.15.cloned.1.call-start = ((), (), s32[]{:S(2)}) async-start(), calls=%async_computation.9 | async-start | bytes 1327104 | tf_op jit(solution)/shard_map/all_gather | solution.py:763
  11.3 461.2 %reduce-scatter.7.cloned.1.call-start = ((), (), s32[]{:S(2)}) async-start(), calls=%async_computation.12 | async-start | bytes 2654208 | tf_op jit(solution)/shard_map/reduce_scatter | solution.py:822
  23.8 2.2 copy-start.13
  346.9 125.6 %reduce-scatter.9.cloned.1.call-start = ((), (), s32[]{:S(2)}) async-start(), calls=%async_computation.13 | async-start | bytes 2654208 | tf_op jit(solution)/shard_map/reduce_scatter | solution.py:822
  349.9 138.1 %reduce-scatter.11.cloned.1.call-start = ((), (), s32[]{:S(2)}) async-start(), calls=%async_computation.14 | async-start | bytes 2654208 | tf_op jit(solution)/shard_map/reduce_scatter | solution.py:822
  353.0 181.1 %reduce-scatter.13.cloned.1.call-start = ((), (), s32[]{:S(2)}) async-start(), calls=%async_computation.15 | async-start | bytes 2654208 | tf_op jit(solution)/shard_map/reduce_scatter | solution.py:822
  355.2 259.0 %reduce-scatter.15.cloned.1.call-start = ((), (), s32[]{:S(2)}) async-start(), calls=%async_computation.16 | async-start | bytes 10616832 | tf_op jit(solution)/shard_map/reduce_scatter | solution.py:822
  465.0 4.7 slice-start
  465.0 229.0 %reduce-scatter.17.cloned.1.call-start = ((), (), s32[]{:S(2)}) async-start(), calls=%async_computation.17 | async-start | bytes 10616832 | tf_op jit(solution)/shard_map/reduce_scatter | solution.py:822
  465.1 4.6 slice-start.1
  472.3 221.7 %copy-start.23 = (u32[32]{0:T(128)S(1)}, u32[32]{0:T(128)}, u32[]{:S(2)}) copy-start(u32[32]{0:T(128)} %constant.57) | copy-start | bytes 388
  472.3 223.6 %copy-start.9 = (bf16[2,2,192,768]{3,2,1,0:T(8,128)(2,1)S(1)}, bf16[2,2,192,768]{3,2,1,0:T(8,128)(2,1)}, u32[]{:S(2)}) copy-start(bf16[2,2,192,768]{3,2,1,0:T(8,128)(2,1)} %get-tuple-element.53) | copy-start | bytes 3538948
  472.3 360.6 %all-reduce.16.cloned.1.call-start = ((), (), s32[]{:S(2)}) async-start(), calls=%async_computation.18 | async-start | bytes 7077888 | tf_op jit(solution)/shard_map/psum | solution.py:823
  696.1 4.2 copy-start.11
  832.9 6.9 copy-start.6
  832.9 7.9 copy-start.5
  (7 other events, 11.9 us)
Sparse Core Ops, SparseCore 0:
  10.0 26.7 all-gather.12
  38.7 24.0 all-gather.10
  64.7 24.0 all-gather.8
  90.5 38.9 all-gather.16
  131.2 39.3 all-gather.18
  172.4 23.5 all-gather.14
  347.0 48.9 reduce-scatter.6
  399.7 42.4 reduce-scatter.8
  445.5 42.4 reduce-scatter.10
  491.6 42.4 reduce-scatter.12
  537.6 76.4 reduce-scatter.14
  617.5 76.4 reduce-scatter.16
  696.9 136.0 all-reduce.15

commit v2 on v1

--- a/solution.py
+++ b/solution.py
@@ -15,7 +15,7 @@
 BF16 = jnp.bfloat16
 ANY = pl.BlockSpec(memory_space=pl.ANY)
 VMEM = pl.BlockSpec(memory_space=pltpu.VMEM)
-LIMIT = 60 << 20
+LIMIT = 62 << 20
 QB = 256
 
 
@@ -188,28 +188,293 @@
 RETURN_SEMS = lambda seq: [pltpu.SemaphoreType.DMA((seq,)), pltpu.SemaphoreType.DMA((2, 2))]
 
 
+class Spread:
+    def __init__(self, source, full_ref, send_sem, recv_sem, local_sem, stride):
+        f, z, m, c = where_am_i()
+        n_f = lax.axis_size("fsdp")
+        steps = n_f // stride
+        slot = f if stride == 1 else m
+        self.local = pltpu.make_async_copy(source(f), full_ref.at[slot], local_sem)
+        self.sends = []
+        self.arrivals = []
+        for d in range(1, steps):
+            to = (f + d * stride) % n_f
+            back = (f + n_f - d * stride) % n_f
+            self.sends.append(
+                remote(source(to), full_ref.at[slot], send_sem.at[d], recv_sem.at[d], (to, z))
+            )
+            place = back if stride == 1 else back // 2
+            self.arrivals.append(
+                remote(source(f), full_ref.at[place], send_sem.at[d], recv_sem.at[d], (to, z))
+            )
+
+    def start(self):
+        self.local.start()
+        for item in self.sends:
+            item.start()
+
+    def ready(self):
+        self.local.wait()
+        for item in self.arrivals:
+            item.wait_recv()
+
+    def finish(self):
+        for item in self.sends:
+            item.wait_send()
+
+
+def spread_sems(steps):
+    return [
+        pltpu.SemaphoreType.DMA((steps,)),
+        pltpu.SemaphoreType.DMA((steps,)),
+        pltpu.SemaphoreType.DMA,
+    ]
+
+
+def fsdp_peers():
+    f, z, _, _ = where_am_i()
+    n_f = lax.axis_size("fsdp")
+    return [((f + d) % n_f, z) for d in range(1, n_f)]
+
+
+def all_peers(seq):
+    f, z, m, c = where_am_i()
+    other = m * 2 + 1 - c
+    peers = fsdp_peers()
+    for d in range(1, seq):
+        peers.append((f, (z + d) % seq))
+        peers.append((other, (z + d) % seq))
+    return peers
+
+
+class Scatter:
+    def __init__(self, parts_ref, got_ref, send_sem, recv_sem):
+        f, z, m, c = where_am_i()
+        n_m = lax.axis_size("fsdp") // 2
+        self.copies = []
+        for d in range(1, n_m):
+            to = (m + d) % n_m
+            self.copies.append(
+                remote(
+                    parts_ref.at[to],
+                    got_ref.at[d - 1],
+                    send_sem.at[d],
+                    recv_sem.at[d],
+                    (to * 2 + c, z),
+                )
+            )
+
+    def start(self):
+        for item in self.copies:
+            item.start()
+
+    def ready(self):
+        for item in self.copies:
+            item.wait_recv()
+
+    def finish(self):
+        for item in self.copies:
+            item.wait_send()
+
+
+def scatter_sems():
+    n_m = lax.axis_size("fsdp") // 2
+    return [pltpu.SemaphoreType.DMA((n_m,)), pltpu.SemaphoreType.DMA((n_m,))]
+
+
+class Across:
+    def __init__(self, own_ref, mate_ref, end_ref, sems):
+        f, z, _, _ = where_am_i()
+        self.own, self.mate, self.end = own_ref, mate_ref, end_ref
+        self.edge = jnp.logical_or(z == 0, z == 3)
+        self.inner = jnp.logical_not(self.edge)
+        beside = jnp.where(z < 2, 1 - z, 5 - z)
+        across = 3 - z
+        self.up = remote(own_ref, end_ref, sems.at[0], sems.at[1], (f, beside))
+        self.swap = remote(own_ref, mate_ref, sems.at[2], sems.at[3], (f, across))
+        self.down = remote(own_ref, mate_ref, sems.at[4], sems.at[5], (f, beside))
+
+    def rise(self):
+        pl.when(self.edge)(self.up.start)
+
+    def exchange(self):
+        @pl.when(self.inner)
+        def _():
+            self.up.wait_recv()
+            total = self.own[...].astype(F32) + self.end[...].astype(F32)
+            self.own[...] = total.astype(self.own.dtype)
+            self.swap.start()
+
+    def settle(self):
+        @pl.when(self.inner)
+        def _():
+            self.swap.wait()
+            total = self.own[...].astype(F32) + self.mate[...].astype(F32)
+            self.own[...] = total.astype(self.own.dtype)
+            self.down.start()
+
+    def ready(self):
+        @pl.when(self.edge)
+        def _():
+            self.up.wait_send()
+            self.down.wait_recv()
+            self.own[...] = self.mate[...]
+
+        @pl.when(self.inner)
+        def _():
+            self.down.wait_send()
+
+
+ACROSS_SEMS = pltpu.SemaphoreType.DMA((6,))
+
+
 def own_lanes(parity):
     lane = lax.broadcasted_iota(jnp.int32, (1, 128), 1)
     return (lane // HD) == parity, lane == HD * (1 - parity)
 
 
 def project_kernel(
-    seq, x_send, wqkv, vecs, x_full, n1_out, q_out, k_out, v_out, ssem, rsem, psend, precv, xv, lsem
+    seq, x_send, wqkv_send, wo_send,
+    first_gain, first_shift, query_bias, value_bias, output_bias, second_gain, second_shift,
+    outer_bias, inner_bias,
+    x_full, n1_out, q_out, k_out, v_out, wqkv_out, wo_out, vecs_out, ibias_out,
+    ssem, rsem, psend, precv,
+    qsend, qrecv, qlocal, osend, orecv, olocal, vsend, vrecv, vlocal,
+    xv, wqkv, small, smalls, lsem, wsem,
 ):
+    f, z, m, c = where_am_i()
+    n_f = lax.axis_size("fsdp")
+    share = first_gain.shape[1]
+    piece = inner_bias.shape[1]
+    small[...] = jnp.zeros_like(small)
+    for r, ref in enumerate(
+        (
+            first_gain,
+            first_shift,
+            query_bias,
+            value_bias,
+            output_bias,
+            second_gain,
+            second_shift,
+            outer_bias,
+        )
+    ):
+        small[r : r + 1, :share] = ref[...].astype(F32)
+    small[8:9, :piece] = inner_bias[...].astype(F32)
+    meet(all_peers(seq))
+    gather = Gather(x_send, x_full, ssem, rsem, psend, precv, seq)
+    vectors = Spread(lambda to: small, smalls, vsend, vrecv, vlocal, 1)
+    weights = Spread(lambda to: wqkv_send.at[to % 2], wqkv, qsend, qrecv, qlocal, 1)
+    later = Spread(lambda to: wo_send, wo_out, osend, orecv, olocal, 1)
+    vectors.start()
+    gather.start()
+    weights.start()
+    half = xv.shape[2]
+    mine = q_out.shape[1]
+    width = n1_out.shape[1]
+
+    vectors.ready()
+    row = lax.broadcasted_iota(jnp.int32, (128, width), 0)
+    col = lax.broadcasted_iota(jnp.int32, (128, width), 1)
+    vecs = jnp.zeros((16, width), F32)
+    for k in range(n_f):
+        spot = jnp.logical_and(col - k * share == row, row < share)
+        vecs = vecs + nn(
+            smalls[k, :, :128].astype(BF16), jnp.where(spot, 1.0, 0.0).astype(BF16)
+        )
+    vecs_out[...] = vecs[:8]
+    for k in range(n_f // 2):
+        ibias_out[0:1, k * piece : (k + 1) * piece] = smalls[2 * k + c, 8:9, :piece]
+    weights.ready()
+    later.start()
+    keep_weights = pltpu.make_async_copy(wqkv, wqkv_out, wsem)
+    keep_weights.start()
+    for k in range(seq):
+        gather.hand_on(k)
+    gain = vecs_out[0:1, :]
+    shift = vecs_out[1:2, :]
+    cols = pl.ds(pl.multiple_of(c * mine, 128), mine)
+    qb = vecs_out[2:3, cols]
+    vb = vecs_out[3:4, cols]
+
+    for k in range(seq):
+        gather.ready(k)
+        copy = pltpu.make_async_copy(x_full.at[k], xv.at[k], lsem.at[k])
+        copy.start()
+        copy.wait()
+        rows = pl.ds(k * 2 * half, 2 * half)
+        hat, _ = normalize(xv[k].reshape(2 * half, width).astype(F32))
+        normed = (hat * gain + shift).astype(BF16)
+        n1_out[rows, :] = normed
+        qkv = nn(normed, wqkv[...].reshape(width, 3 * mine))
+        q_out[rows, :] = (qkv[:, :mine] + qb).astype(BF16)
+        k_out[rows, :] = qkv[:, mine : 2 * mine].astype(BF16)
+        v_out[rows, :] = (qkv[:, 2 * mine :] + vb).astype(BF16)
+    gather.finish()
+    later.ready()
+    vectors.finish()
+    weights.finish()
+    later.finish()
+    keep_weights.wait()
+
+
+def project(x_send, wqkv_send, wo_send, vectors, seq):
+    _, _, half, width = x_send.shape
+    n_f = lax.axis_size("fsdp")
+    rows = seq * 2 * half
+    share = wo_send.shape[0]
+    mine = wqkv_send.shape[2] // 3
+    piece = vectors[-1].shape[1]
+    lanes = max(128, piece)
+    return pl.pallas_call(
+        lambda *refs: project_kernel(seq, *refs),
+        in_specs=[ANY] * 3 + [VMEM] * 9,
+        out_specs=[ANY, VMEM, VMEM, VMEM, VMEM, ANY, ANY, VMEM, VMEM],
+        out_shape=[
+            jax.ShapeDtypeStruct((seq, 2, half, width), BF16),
+            jax.ShapeDtypeStruct((rows, width), BF16),
+        ]
+        + [jax.ShapeDtypeStruct((rows, mine), BF16)] * 3
+        + [
+            jax.ShapeDtypeStruct((n_f, share, 3 * mine), BF16),
+            jax.ShapeDtypeStruct((n_f, share, width), BF16),
+            jax.ShapeDtypeStruct((8, width), F32),
+            jax.ShapeDtypeStruct((1, piece * n_f // 2), F32),
+        ],
+        scratch_shapes=GATHER_SEMS(seq)
+        + spread_sems(n_f)
+        + spread_sems(n_f)
+        + spread_sems(n_f)
+        + [
+            pltpu.VMEM((seq, 2, half, width), BF16),
+            pltpu.VMEM((n_f, share, 3 * mine), BF16),
+            pltpu.VMEM((16, lanes), F32),
+            pltpu.VMEM((n_f, 16, lanes), F32),
+            pltpu.SemaphoreType.DMA((seq,)),
+            pltpu.SemaphoreType.DMA,
+        ],
+        compiler_params=pltpu.CompilerParams(
+            collective_id=0, has_side_effects=True, vmem_limit_bytes=LIMIT
+        ),
+        name="project",
+    )(x_send, wqkv_send, wo_send, *vectors)
+
+
+def project_plain_kernel(seq, x_send, wqkv, vecs, x_full, n1_out, q_out, k_out, v_out,
+                         ssem, rsem, psend, precv, xv, lsem):
     f, z, m, c = where_am_i()
     meet(column_peers(seq))
     gather = Gather(x_send, x_full, ssem, rsem, psend, precv, seq)
     gather.start()
     half = xv.shape[1]
-    width = q_out.shape[1]
+    mine = q_out.shape[1]
     for k in range(seq):
         gather.hand_on(k)
     gain = vecs[0:1, :]
     shift = vecs[1:2, :]
-    cols = pl.ds(pl.multiple_of(c * width, 128), width)
+    cols = pl.ds(pl.multiple_of(c * mine, 128), mine)
     qb = vecs[2:3, cols]
     vb = vecs[3:4, cols]
-
     for k in range(seq):
         gather.ready(k)
         copy = pltpu.make_async_copy(x_full.at[k], xv, lsem)
@@ -220,18 +485,18 @@
         normed = (hat * gain + shift).astype(BF16)
         n1_out[rows, :] = normed
         qkv = nn(normed, wqkv[...])
-        q_out[rows, :] = (qkv[:, :width] + qb).astype(BF16)
-        k_out[rows, :] = qkv[:, width : 2 * width].astype(BF16)
-        v_out[rows, :] = (qkv[:, 2 * width :] + vb).astype(BF16)
+        q_out[rows, :] = (qkv[:, :mine] + qb).astype(BF16)
+        k_out[rows, :] = qkv[:, mine : 2 * mine].astype(BF16)
+        v_out[rows, :] = (qkv[:, 2 * mine :] + vb).astype(BF16)
     gather.finish()
 
 
-def project(x_send, wqkv, vecs, seq):
+def project_plain(x_send, wqkv, vecs, seq):
     _, _, half, width = x_send.shape
     rows = seq * 2 * half
     mine = wqkv.shape[1] // 3
     return pl.pallas_call(
-        lambda *refs: project_kernel(seq, *refs),
+        lambda *refs: project_plain_kernel(seq, *refs),
         in_specs=[ANY, VMEM, VMEM],
         out_specs=[ANY, VMEM, VMEM, VMEM, VMEM],
         out_shape=[
@@ -242,15 +507,17 @@
         scratch_shapes=GATHER_SEMS(seq)
         + [pltpu.VMEM((2, half, width), BF16), pltpu.SemaphoreType.DMA],
         compiler_params=pltpu.CompilerParams(
-            collective_id=0, has_side_effects=True, vmem_limit_bytes=LIMIT
+            collective_id=5, has_side_effects=True, vmem_limit_bytes=LIMIT
         ),
-        name="project",
+        name="project_plain",
     )(x_send, wqkv, vecs)
 
 
 def attend_kernel(
-    seq, local, heads, cot_send, q, k, v, e_out, o_out, linv_out, mixed_out, cot_full,
-    ssem, rsem, psend, precv, stage, ka, va, msend, mrecv, mlocal,
+    seq, local, heads, cot_send, wi_send, wu_send, q, k, v,
+    e_out, o_out, linv_out, mixed_out, cot_full, wi_out, wu_out,
+    ssem, rsem, psend, precv, isend, irecv, ilocal, usend, urecv, ulocal,
+    stage, ka, va, msend, mrecv, mlocal,
 ):
     f, z, m, c = where_am_i()
     h = pl.program_id(0)
@@ -258,12 +525,18 @@
     parity = h % 2
     rows = q.shape[0]
     gather = Gather(cot_send, cot_full, ssem, rsem, psend, precv, seq)
+    weights = [
+        Spread(lambda to: wi_send.at[to % 2], wi_out, isend, irecv, ilocal, 1),
+        Spread(lambda to: wu_send, wu_out, usend, urecv, ulocal, 2),
+    ]
     other = (m * 2 + 1 - c, z)
 
     @pl.when(h == 0)
     def _():
-        meet(column_peers(seq))
+        meet(all_peers(seq))
         gather.start()
+        for item in weights:
+            item.start()
 
     mine, first = own_lanes(parity)
     place = lax.broadcasted_iota(jnp.int32, (rows, 1), 0) % (rows // seq)
@@ -318,6 +591,9 @@
         for item in range(seq):
             gather.ready(item)
         gather.finish()
+        for item in weights:
+            item.ready()
+            item.finish()
         for p in range(heads // 2):
             here, there, back = mixed_copies(p)
             here.wait()
@@ -325,8 +601,9 @@
             back.wait_recv()
 
 
-def attend(cot_send, q, k, v, local, seq):
+def attend(cot_send, wi_send, wu_send, q, k, v, local, seq):
     rows, mine = q.shape
+    n_f = lax.axis_size("fsdp")
     heads = mine // HD
     _, _, half, width = cot_send.shape
     pairs = heads // 2
@@ -334,11 +611,13 @@
     return pl.pallas_call(
         lambda *refs: attend_kernel(seq, local, heads, *refs),
         grid=(heads,),
-        in_specs=[ANY, by_pair, by_pair, by_pair],
+        in_specs=[ANY, ANY, ANY, by_pair, by_pair, by_pair],
         out_specs=[
             pl.BlockSpec((1, rows, rows), lambda h: (h, 0, 0)),
             by_pair,
             by_pair,
+            ANY,
+            ANY,
             ANY,
             ANY,
         ],
@@ -348,8 +627,12 @@
             jax.ShapeDtypeStruct((rows, mine), F32),
             jax.ShapeDtypeStruct((2, pairs, rows, 128), BF16),
             jax.ShapeDtypeStruct((seq, 2, half, width), BF16),
+            jax.ShapeDtypeStruct((n_f,) + wi_send.shape[1:], BF16),
+            jax.ShapeDtypeStruct((n_f // 2,) + wu_send.shape, BF16),
         ],
         scratch_shapes=GATHER_SEMS(seq)
+        + spread_sems(n_f)
+        + spread_sems(n_f // 2)
         + [
             pltpu.VMEM((pairs, rows, 128), BF16),
             pltpu.VMEM((rows, 128), BF16),
@@ -362,7 +645,7 @@
             collective_id=1, has_side_effects=True, vmem_limit_bytes=LIMIT
         ),
         name="attend",
-    )(cot_send, q, k, v)
+    )(cot_send, wi_send, wu_send, q, k, v)
 
 
 def gelu_parts(u):
@@ -380,22 +663,32 @@
 
 def dense_kernel(
     seq, x, mixed, cot, wo, wi, wu, vecs, ibias,
-    out_own, gres_own, gm_out, gwo_out, gwi_out, gwu_out, gvec_out, gib_out,
-    n2, hat2, inv2, keep, gown, pstage, precv, gstage, grecv, psem, prsem, gsem, grsem,
+    out_back, gres_own, gm_out, gwo_out, gwi_out, ru_out, gvec_out, gib_out,
+    n2, hat2, inv2, keep, slope, out_own, pstage, precv, gstage, grecv,
+    gwo, gwi, shared, ugot, upart,
+    psem, prsem, gsem, grsem, bsend, brecv, usend, urecv,
 ):
     f, z, m, c = where_am_i()
     other = (m * 2 + 1 - c, z)
-    meet([other])
+    meet(all_peers(seq))
     half = x.shape[2]
     chunk = 2 * half
     width = x.shape[3]
     mine = gm_out.shape[1]
+    hidden = wi.shape[1]
+    n_m = gwi_out.shape[0]
+    share = gwi_out.shape[2]
+    piece = upart.shape[1]
     obias, gain, shift, ubias = vecs[4:5, :], vecs[5:6, :], vecs[6:7, :], vecs[7:8, :]
     gvec_out[...] = jnp.zeros_like(gvec_out)
     gib_out[...] = jnp.zeros_like(gib_out)
-    gwo_out[...] = jnp.zeros_like(gwo_out)
-    gwi_out[...] = jnp.zeros_like(gwi_out)
-    gwu_out[...] = jnp.zeros_like(gwu_out)
+    gwo[...] = jnp.zeros_like(gwo)
+    gwi[...] = jnp.zeros_like(gwi)
+    gwu = shared.at[:hidden]
+    gown = shared.at[: seq * chunk]
+    gwu[...] = jnp.zeros_like(gwu)
+    back = Return(out_own, out_back, bsend, brecv, seq)
+    outer = Scatter(upart, ugot, usend, urecv)
 
     def p_copy(i):
         return remote(pstage.at[i], precv.at[i], psem.at[i], prsem.at[i], other)
@@ -409,7 +702,7 @@
             [mixed[a, p, rows, :] for a in range(2) for p in range(mixed.shape[1])], axis=1
         )
 
-    def first(i, _):
+    def forward(i, _):
         rows = pl.ds(i * chunk, chunk)
         resid = (
             x[i].reshape(chunk, width).astype(F32) + nn(mixed_rows(i), wo[...]) + obias
@@ -422,37 +715,42 @@
         inner = nn(normed, wi[...]) + ibias[...]
         phi, bump = gelu_parts(inner)
         active = (inner * phi).astype(BF16)
-        slope = phi + bump
+        slope[rows, :] = (phi + bump).astype(slope.dtype)
         pout = nn(active, wu[...])
         full = resid + ubias
 
         @pl.when(c == 0)
         def _():
             keep[i] = full[:half] + pout[:half]
-            pstage[i] = pout[half:]
+            pstage[i] = pout[half:].astype(pstage.dtype)
 
         @pl.when(c == 1)
         def _():
             keep[i] = full[half:] + pout[half:]
-            pstage[i] = pout[:half]
+            pstage[i] = pout[:half].astype(pstage.dtype)
 
         p_copy(i).start()
         g = cot[i].reshape(chunk, width)
-        gi = (nt(g, wu[...]) * slope).astype(BF16)
+        gwu[...] += tn(active, g)
+        gvec_out[0:1, :] += jnp.sum(g.astype(F32), 0, keepdims=True)
+        return 0
+
+    def middle(i, _):
+        rows = pl.ds(i * chunk, chunk)
+        g = cot[i].reshape(chunk, width)
+        gi = (nt(g, wu[...]) * slope[rows, :].astype(F32)).astype(BF16)
         gn2 = nt(gi, wi[...])
-        gown[i] = gn2
+        gown[rows, :] = gn2
         gstage[i] = gn2.astype(gstage.dtype)
         g_copy(i).start()
-        gwu_out[...] += tn(active, g)
-        gwi_out[...] += tn(normed, gi)
+        gwi[...] += tn(n2[rows, :], gi)
         gib_out[...] += jnp.sum(gi.astype(F32), 0, keepdims=True)
-        gvec_out[0:1, :] += jnp.sum(g.astype(F32), 0, keepdims=True)
         return 0
 
-    def second(i, _):
+    def backward(i, _):
         rows = pl.ds(i * chunk, chunk)
         g_copy(i).wait_recv()
-        gn2 = gown[i] + grecv[i].astype(F32)
+        gn2 = gown[rows, :] + grecv[i].astype(F32)
         hat = hat2[rows, :]
         gvec_out[1:2, :] += jnp.sum(gn2 * hat, 0, keepdims=True)
         gvec_out[2:3, :] += jnp.sum(gn2, 0, keepdims=True)
@@ -467,19 +765,33 @@
         @pl.when(c == 0)
         def _():
             gres_own[i] = gres[:half]
-            gwo_out[...] += tn(mix, branch[:, :mine])
+            gwo[...] += tn(mix, branch[:, :mine])
 
         @pl.when(c == 1)
         def _():
             gres_own[i] = gres[half:]
-            gwo_out[...] += tn(mix, branch[:, mine:])
-
-        p_copy(i).wait_recv()
-        out_own[i] = (keep[i] + precv[i]).astype(BF16)
+            gwo[...] += tn(mix, branch[:, mine:])
+
         return 0
 
-    lax.fori_loop(0, seq, first, 0)
-    lax.fori_loop(0, seq, second, 0)
+    lax.fori_loop(0, seq, forward, 0)
+    for k in range(n_m):
+        upart[k] = gwu[k * piece : (k + 1) * piece, :].astype(BF16)
+    outer.start()
+    for k in range(seq):
+        p_copy(k).wait_recv()
+        out_own[k] = (keep[k] + precv[k].astype(F32)).astype(BF16)
+    back.start()
+    lax.fori_loop(0, seq, middle, 0)
+    for k in range(n_m):
+        for j in range(2):
+            at = (2 * k + j) * share
+            gwi_out[k, j] = gwi[at : at + share, :].astype(BF16)
+    lax.fori_loop(0, seq, backward, 0)
+    for k in range(n_m):
+        for j in range(2):
+            at = (2 * k + j) * share
+            gwo_out[k, j] = gwo[at : at + share, :].astype(BF16)
 
     def last(i, _):
         p_copy(i).wait_send()
@@ -487,6 +799,13 @@
         return 0
 
     lax.fori_loop(0, seq, last, 0)
+    outer.ready()
+    total = upart[m].astype(F32)
+    for k in range(n_m - 1):
+        total = total + ugot[k].astype(F32)
+    ru_out[...] = total.astype(BF16)
+    outer.finish()
+    back.finish()
 
 
 def dense(x, mixed, cot, wo, wi, wu, vecs, ibias):
@@ -494,17 +813,21 @@
     rows = seq * 2 * half
     hidden = wi.shape[1]
     mine = width // 2
+    n_f = lax.axis_size("fsdp")
+    n_m = n_f // 2
+    share = width // n_f
+    piece = hidden // n_m
     return pl.pallas_call(
         lambda *refs: dense_kernel(seq, *refs),
         in_specs=[VMEM] * 8,
-        out_specs=[VMEM] * 8,
+        out_specs=[ANY] + [VMEM] * 7,
         out_shape=[
-            jax.ShapeDtypeStruct((seq, half, width), BF16),
+            jax.ShapeDtypeStruct((2, 2, half, width), BF16),
             jax.ShapeDtypeStruct((seq, half, width), F32),
             jax.ShapeDtypeStruct((rows, mine), BF16),
-            jax.ShapeDtypeStruct((width, mine), F32),
-            jax.ShapeDtypeStruct((width, hidden), F32),
-            jax.ShapeDtypeStruct((hidden, width), F32),
+            jax.ShapeDtypeStruct((n_m, 2, share, mine), BF16),
+            jax.ShapeDtypeStruct((n_m, 2, share, hidden), BF16),
+            jax.ShapeDtypeStruct((piece, width), BF16),
             jax.ShapeDtypeStruct((8, width), F32),
             jax.ShapeDtypeStruct((1, hidden), F32),
         ],
@@ -513,16 +836,24 @@
             pltpu.VMEM((rows, width), F32),
             pltpu.VMEM((rows, 128), F32),
             pltpu.VMEM((seq, half, width), F32),
-            pltpu.VMEM((seq, 2 * half, width), F32),
-            pltpu.VMEM((seq, half, width), F32),
-            pltpu.VMEM((seq, half, width), F32),
+            pltpu.VMEM((rows, hidden), BF16),
+            pltpu.VMEM((seq, half, width), BF16),
+            pltpu.VMEM((seq, half, width), BF16),
+            pltpu.VMEM((seq, half, width), BF16),
             pltpu.VMEM((seq, 2 * half, width), BF16),
             pltpu.VMEM((seq, 2 * half, width), BF16),
+            pltpu.VMEM((width, mine), F32),
+            pltpu.VMEM((width, hidden), F32),
+            pltpu.VMEM((max(rows, hidden), width), F32),
+            pltpu.VMEM((n_m - 1, piece, width), BF16),
+            pltpu.VMEM((n_m, piece, width), BF16),
             pltpu.SemaphoreType.DMA((seq,)),
             pltpu.SemaphoreType.DMA((seq,)),
             pltpu.SemaphoreType.DMA((seq,)),
             pltpu.SemaphoreType.DMA((seq,)),
-        ],
+        ]
+        + RETURN_SEMS(seq)
+        + scatter_sems(),
         compiler_params=pltpu.CompilerParams(
             collective_id=2, has_side_effects=True, vmem_limit_bytes=LIMIT
         ),
@@ -531,18 +862,26 @@
 
 
 def attend_back_kernel(
-    seq, heads, out_own, q, k, v, gm, o, linv, e, gq_out, gk_out, gv_out, out_back,
-    ssem, rsem, do, dot_, qt, va, km, dqs, dvt, dkt,
+    seq, heads, gwi, gwo, ru, q, k, v, gm, o, linv, e,
+    gq_out, gk_out, gv_out, igot, ogot, gwu_out,
+    isend, irecv, osend, orecv, zsems, zown, zmate, zend, lsem,
+    do, dot_, qt, va, km, dqs, dvt, dkt,
 ):
     h = pl.program_id(0)
     parity = h % 2
     rows = q.shape[0]
-    back = Return(out_own, out_back, ssem, rsem, seq)
+    scatters = [Scatter(gwi, igot, isend, irecv), Scatter(gwo, ogot, osend, orecv)]
+    outer = Across(zown, zmate, zend, zsems)
 
     @pl.when(h == 0)
     def _():
-        meet(column_peers(seq))
-        back.start()
+        load = pltpu.make_async_copy(ru, zown, lsem)
+        load.start()
+        meet(all_peers(seq))
+        for item in scatters:
+            item.start()
+        load.wait()
+        outer.rise()
 
     mine, first = own_lanes(parity)
     third = HD ** (-0.5)
@@ -595,25 +934,44 @@
         gv_out[...] = dvt[...].T.astype(BF16)
         gk_out[...] = (dkt[...] * third).T.astype(BF16)
 
+    pl.when(h == 1)(outer.exchange)
+    pl.when(h == 3)(outer.settle)
+
     @pl.when(h == heads - 1)
     def _():
-        back.finish()
-
-
-def attend_back(out_own, q, k, v, gm, o, linv, e):
+        outer.ready()
+        gwu_out[...] = zown[...].astype(F32)
+        for item in scatters:
+            item.ready()
+            item.finish()
+
+
+def attend_back(gwi, gwo, ru, q, k, v, gm, o, linv, e, seq):
     rows, mine = q.shape
     heads = mine // HD
-    seq, half, width = out_own.shape
+    n_m = gwi.shape[0]
+    piece, width = ru.shape
     by_pair = pl.BlockSpec((rows, 128), lambda h: (0, h // 2))
     return pl.pallas_call(
         lambda *refs: attend_back_kernel(seq, heads, *refs),
         grid=(heads,),
-        in_specs=[ANY] + [by_pair] * 6 + [pl.BlockSpec((1, rows, rows), lambda h: (h, 0, 0))],
-        out_specs=[by_pair] * 3 + [ANY],
+        in_specs=[ANY] * 3
+        + [by_pair] * 6
+        + [pl.BlockSpec((1, rows, rows), lambda h: (h, 0, 0))],
+        out_specs=[by_pair] * 3
+        + [ANY, ANY, pl.BlockSpec((piece, width), lambda h: (0, 0))],
         out_shape=[jax.ShapeDtypeStruct((rows, mine), BF16)] * 3
-        + [jax.ShapeDtypeStruct((2, 2, half, width), BF16)],
-        scratch_shapes=RETURN_SEMS(seq)
         + [
+            jax.ShapeDtypeStruct((n_m - 1,) + gwi.shape[1:], BF16),
+            jax.ShapeDtypeStruct((n_m - 1,) + gwo.shape[1:], BF16),
+            jax.ShapeDtypeStruct((piece, width), F32),
+        ],
+        scratch_shapes=scatter_sems()
+        + scatter_sems()
+        + [ACROSS_SEMS]
+        + [pltpu.VMEM((piece, width), BF16)] * 3
+        + [
+            pltpu.SemaphoreType.DMA,
             pltpu.VMEM((rows, 128), BF16),
             pltpu.VMEM((128, rows), BF16),
             pltpu.VMEM((128, rows), BF16),
@@ -627,34 +985,65 @@
             collective_id=3, has_side_effects=True, vmem_limit_bytes=LIMIT
         ),
         name="attend_back",
-    )(out_own, q, k, v, gm, o, linv, e)
+    )(gwi, gwo, ru, q, k, v, gm, o, linv, e)
 
 
 def project_back_kernel(
-    seq, x, n1, gq, gk, gv, gres, wqkv, vecs, gw_out, gvec_out, ig_back,
-    gown, gstage, grecv, ig_own, gsem, grsem, ssem, rsem,
+    seq, x, n1, gq, gk, gv, gres, wqkv, vecs, vpart, gwi, igot, gwo, ogot,
+    gwq_out, gwk_out, gwv_out, gwo_out, gwi_out, vec_out, ig_back,
+    gown, gstage, grecv, ig_own, gw, qpart, qgot, vgot,
+    ri, imate, iend, ito, ra, amate, aend, ato, vown, vmate, vend, vto,
+    gsem, grsem, bsend, brecv, qsend, qrecv, vsend, vrecv, zi, za, zv, pair_sems,
 ):
     f, z, m, c = where_am_i()
     other = (m * 2 + 1 - c, z)
-    meet(column_peers(seq))
+    meet(all_peers(seq))
     half = x.shape[2]
     chunk = 2 * half
     width = x.shape[3]
     mine = gq.shape[1]
+    n_m = gwi.shape[0]
+    share = gwi.shape[2]
     gain = vecs[0:1, :]
+    inner = Across(ri, imate, iend, zi)
+    parts = [Across(ra.at[k], amate.at[k], aend.at[k], za.at[k]) for k in range(4)]
+    vectors = Across(vown, vmate, vend, zv)
+    queries = [
+        Scatter(qpart.at[k], qgot.at[k], qsend.at[k], qrecv.at[k]) for k in range(3)
+    ]
+    vspread = [
+        remote(
+            vown,
+            vgot.at[d - 1],
+            vsend.at[d],
+            vrecv.at[d],
+            (((m + d) % n_m) * 2 + c, z),
+        )
+        for d in range(1, n_m)
+    ]
+    back = Return(ig_own, ig_back, bsend, brecv, seq)
 
     def g_copy(i):
         return remote(gstage.at[i], grecv.at[i], gsem.at[i], grsem.at[i], other)
 
-    def grads(i):
+    def cross(k, src, dst):
+        return remote(src, dst, pair_sems.at[0, k], pair_sems.at[1, k], other)
+
+    total = gwi[m].astype(F32)
+    for k in range(n_m - 1):
+        total = total + igot[k].astype(F32)
+    ri[...] = total.astype(BF16)
+    inner.rise()
+    total = gwo[m].astype(F32)
+    for k in range(n_m - 1):
+        total = total + ogot[k].astype(F32)
+    ra[3] = total.astype(BF16)
+    parts[3].rise()
+
+    def first(i, _):
         rows = pl.ds(i * chunk, chunk)
-        return jnp.concatenate([gq[rows, :], gk[rows, :], gv[rows, :]], axis=1)
-
-    gw_out[...] = jnp.zeros_like(gw_out)
-    gvec_out[...] = jnp.zeros_like(gvec_out)
-
-    def first(i, _):
-        gn1 = nt(grads(i), wqkv[...])
+        grads = jnp.concatenate([gq[rows, :], gk[rows, :], gv[rows, :]], axis=1)
+        gn1 = nt(grads, wqkv[...])
 
         @pl.when(c == 0)
         def _():
@@ -669,47 +1058,103 @@
         g_copy(i).start()
         return 0
 
-    def second(i, _):
-        g_copy(i).wait_recv()
-        gn1 = gown[i] + grecv[i]
-        hat, inv = normalize(x[i, c].astype(F32))
-        gvec_out[0:1, :] += jnp.sum(gn1 * hat, 0, keepdims=True)
-        gvec_out[1:2, :] += jnp.sum(gn1, 0, keepdims=True)
-        ig_own[i] = (gres[i] + norm_back(gn1, gain, hat, inv)).astype(BF16)
-        return 0
-
     lax.fori_loop(0, seq, first, 0)
-    lax.fori_loop(0, seq, second, 0)
-    back = Return(ig_own, ig_back, ssem, rsem, seq)
+    for k, ref in enumerate((gq, gk, gv)):
+        gw[...] = tn(n1[...], ref[...])
+        for j in range(n_m):
+            for b in range(2):
+                at = (2 * j + b) * share
+                qpart[k, j, b] = gw[at : at + share, :].astype(BF16)
+        queries[k].start()
+        if k == 0:
+            inner.exchange()
+            parts[3].exchange()
+    for k in range(seq):
+        g_copy(k).wait_recv()
+        gn1 = gown[k] + grecv[k]
+        hat, inv = normalize(x[k, c].astype(F32))
+        line = jnp.sum(gn1 * hat, 0, keepdims=True)
+        flat = jnp.sum(gn1, 0, keepdims=True)
+        if k == 0:
+            gain_sum, shift_sum = line, flat
+        else:
+            gain_sum, shift_sum = gain_sum + line, shift_sum + flat
+        ig_own[k] = (gres[k] + norm_back(gn1, gain, hat, inv)).astype(BF16)
     back.start()
-
-    def third(i, _):
-        rows = pl.ds(i * chunk, chunk)
-        g = grads(i)
-        gw_out[...] += tn(n1[rows, :], g)
-        gvec_out[2:3, :mine] += jnp.sum(g[:, :mine].astype(F32), 0, keepdims=True)
-        gvec_out[3:4, :mine] += jnp.sum(g[:, 2 * mine :].astype(F32), 0, keepdims=True)
-        return 0
-
-    lax.fori_loop(0, seq, third, 0)
-
-    def last(i, _):
-        g_copy(i).wait_send()
-        return 0
-
-    lax.fori_loop(0, seq, last, 0)
+    inner.settle()
+    parts[3].settle()
+    vown[...] = vpart[...]
+    vown[0:1, :] = gain_sum
+    vown[1:2, :] = shift_sum
+    cols = pl.ds(pl.multiple_of(c * mine, 128), mine)
+    vown[2:3, cols] = jnp.sum(gq[...].astype(F32), 0, keepdims=True)
+    vown[3:4, cols] = jnp.sum(gv[...].astype(F32), 0, keepdims=True)
+    for item in vspread:
+        item.start()
+    for item in vspread:
+        item.wait()
+    total = vown[...]
+    for k in range(n_m - 1):
+        total = total + vgot[k]
+    vown[...] = total
+    vectors.rise()
+    for k in range(3):
+        queries[k].ready()
+        total = qpart[k, m].astype(F32)
+        for j in range(n_m - 1):
+            total = total + qgot[k, j].astype(F32)
+        ra[k] = total.astype(BF16)
+        parts[k].rise()
+    vectors.exchange()
+    for k in range(3):
+        parts[k].exchange()
+    vectors.settle()
+    for k in range(3):
+        parts[k].settle()
+    inner.ready()
+    icross = cross(0, ri.at[1 - c], ito)
+    icross.start()
+    vectors.ready()
+    vcross = cross(5, vown, vto)
+    vcross.start()
+    crosses = []
+    for k in (3, 0, 1, 2):
+        parts[k].ready()
+        crosses.append(cross(1 + k, ra.at[k, 1 - c], ato.at[k]))
+        crosses[-1].start()
+    outs = {0: gwq_out, 1: gwk_out, 2: gwv_out, 3: gwo_out}
+    here = pl.ds(pl.multiple_of(c * mine, 128), mine)
+    there = pl.ds(pl.multiple_of((1 - c) * mine, 128), mine)
+    icross.wait()
+    gwi_out[c] = ri[c].astype(F32)
+    gwi_out[1 - c] = ito[...].astype(F32)
+    vcross.wait()
+    vec_out[...] = vown[...] + vto[...]
+    for k, item in zip((3, 0, 1, 2), crosses):
+        item.wait()
+        outs[k][:, here] = ra[k, c].astype(F32)
+        outs[k][:, there] = ato[k].astype(F32)
+    for k in range(seq):
+        g_copy(k).wait_send()
+    for k in range(3):
+        queries[k].finish()
     back.finish()
 
 
-def project_back(x, n1, gq, gk, gv, gres, wqkv, vecs):
+def project_back(x, n1, gq, gk, gv, gres, wqkv, vecs, vpart, gwi, igot, gwo, ogot):
     seq, _, half, width = x.shape
+    n_m, _, share, hidden = gwi.shape
+    mine = gq.shape[1]
+    square = jax.ShapeDtypeStruct((share, width), F32)
+    block = (2, share, mine)
     return pl.pallas_call(
         lambda *refs: project_back_kernel(seq, *refs),
-        in_specs=[VMEM] * 8,
-        out_specs=[VMEM, VMEM, ANY],
-        out_shape=[
-            jax.ShapeDtypeStruct(wqkv.shape, F32),
-            jax.ShapeDtypeStruct((8, width), F32),
+        in_specs=[VMEM] * 13,
+        out_specs=[VMEM] * 6 + [ANY],
+        out_shape=[square] * 4
+        + [
+            jax.ShapeDtypeStruct((2, share, hidden), F32),
+            jax.ShapeDtypeStruct((16, width), F32),
             jax.ShapeDtypeStruct((2, 2, half, width), BF16),
         ],
         scratch_shapes=[
@@ -717,15 +1162,41 @@
             pltpu.VMEM((seq, half, width), F32),
             pltpu.VMEM((seq, half, width), F32),
             pltpu.VMEM((seq, half, width), BF16),
+            pltpu.VMEM((width, mine), F32),
+            pltpu.VMEM((3, n_m) + block, BF16),
+            pltpu.VMEM((3, n_m - 1) + block, BF16),
+            pltpu.VMEM((n_m - 1, 16, width), F32),
+            pltpu.VMEM((2, share, hidden), BF16),
+            pltpu.VMEM((2, share, hidden), BF16),
+            pltpu.VMEM((2, share, hidden), BF16),
+            pltpu.VMEM((share, hidden), BF16),
+            pltpu.VMEM((4,) + block, BF16),
+            pltpu.VMEM((4,) + block, BF16),
+            pltpu.VMEM((4,) + block, BF16),
+            pltpu.VMEM((4, share, mine), BF16),
+            pltpu.VMEM((16, width), F32),
+            pltpu.VMEM((16, width), F32),
+            pltpu.VMEM((16, width), F32),
+            pltpu.VMEM((16, width), F32),
             pltpu.SemaphoreType.DMA((seq,)),
             pltpu.SemaphoreType.DMA((seq,)),
         ]
-        + RETURN_SEMS(seq),
+        + RETURN_SEMS(seq)
+        + [
+            pltpu.SemaphoreType.DMA((3, n_m)),
+            pltpu.SemaphoreType.DMA((3, n_m)),
+            pltpu.SemaphoreType.DMA((n_m,)),
+            pltpu.SemaphoreType.DMA((n_m,)),
+            ACROSS_SEMS,
+            pltpu.SemaphoreType.DMA((4, 6)),
+            ACROSS_SEMS,
+            pltpu.SemaphoreType.DMA((2, 6)),
+        ],
         compiler_params=pltpu.CompilerParams(
             collective_id=4, has_side_effects=True, vmem_limit_bytes=LIMIT
         ),
         name="project_back",
-    )(x, n1, gq, gk, gv, gres, wqkv, vecs)
+    )(x, n1, gq, gk, gv, gres, wqkv, vecs, vpart, gwi, igot, gwo, ogot)
 
 
 def per_device(
@@ -751,96 +1222,107 @@
     seq = lax.axis_size("seq")
     n_f = lax.axis_size("fsdp")
     f = lax.axis_index("fsdp")
-    c = f % 2
+    m, c = f // 2, f % 2
     slots, local, width = frames.shape
     chunk = -(-local // 128) * 128
     half = chunk // 2
     mine = width // 2
-    hidden = n_f * inner_bias.shape[0]
-    piece = hidden // n_f
-
-    def gathered(value):
-        return lax.all_gather(value, "fsdp", axis=0, tiled=True)
-
-    def my_columns(value):
-        return lax.dynamic_slice_in_dim(value, c * mine, mine, axis=1)
+    share = width // n_f
+    piece = inner_bias.shape[0]
+    hidden = piece * n_f // 2
 
     keep = valid_slots.astype(BF16)[:, None, None]
     pad = ((0, 0), (0, chunk - local), (0, 0))
     x_send = jnp.pad(frames, pad).reshape(slots, 2, half, width)
     cot_send = jnp.pad(cotangent * keep, pad).reshape(slots, 2, half, width)
-    wqkv = jnp.concatenate(
-        [my_columns(gathered(w)) for w in (query_weight, key_weight, value_weight)], axis=1
+    wi_send = inner_weight.reshape(share, n_f // 2, 2, piece).transpose(2, 0, 1, 3)
+    wi_send = wi_send.reshape(2, share, hidden)
+    vectors = (
+        first_gain,
+        first_shift,
+        query_bias,
+        value_bias,
+        output_bias,
+        second_gain,
+        second_shift,
+        outer_bias,
     )
-    wo = gathered(output_weight)
-    wi = gathered(inner_weight).reshape(width, n_f // 2, 2, piece)
-    wi = lax.dynamic_index_in_dim(wi, c, 2, keepdims=False).reshape(width, hidden // 2)
-    wu = gathered(outer_weight).reshape(n_f // 2, 2, piece, width)
-    wu = lax.dynamic_index_in_dim(wu, c, 1, keepdims=False).reshape(hidden // 2, width)
-    small = jnp.stack(
-        [
-            first_gain,
-            first_shift,
-            query_bias,
-            value_bias,
-            output_bias,
-            second_gain,
-            second_shift,
-            outer_bias,
-        ]
+    if share % 16 == 0 and piece % 128 == 0:
+        wqkv_send = jnp.concatenate(
+            [
+                w.reshape(share, 2, mine).transpose(1, 0, 2)
+                for w in (query_weight, key_weight, value_weight)
+            ],
+            axis=-1,
+        )
+        x, n1, q, k, v, wqkv, wo, vecs, ibias = project(
+            x_send,
+            wqkv_send,
+            output_weight,
+            [value[None] for value in vectors] + [inner_bias[None]],
+            seq,
+        )
+        wqkv = wqkv.reshape(width, 3 * mine)
+        wo = wo.reshape(width, width)
+    else:
+
+        def gathered(value, axis=0):
+            return lax.all_gather(value, "fsdp", axis=axis, tiled=True)
+
+        def my_columns(value):
+            return lax.dynamic_slice_in_dim(value, c * mine, mine, axis=1)
+
+        wqkv = jnp.concatenate(
+            [my_columns(gathered(w)) for w in (query_weight, key_weight, value_weight)], axis=1
+        )
+        wo = gathered(output_weight)
+        vecs = gathered(jnp.stack(vectors), 1).astype(F32)
+        ibias = gathered(inner_bias).astype(F32).reshape(n_f // 2, 2, piece)
+        ibias = lax.dynamic_index_in_dim(ibias, c, 1, keepdims=False).reshape(1, hidden)
+        x, n1, q, k, v = project_plain(x_send, wqkv, vecs, seq)
+
+    e, o, linv, mixed, cot, wi, wu = attend(
+        cot_send, wi_send, outer_weight, q, k, v, local, seq
     )
-    vecs = lax.all_gather(small, "fsdp", axis=1, tiled=True).astype(F32)
-    ibias = gathered(inner_bias).astype(F32).reshape(n_f // 2, 2, piece)
-    ibias = lax.dynamic_index_in_dim(ibias, c, 1, keepdims=False).reshape(1, hidden // 2)
-
-    x, n1, q, k, v = project(x_send, wqkv, vecs, seq)
-    e, o, linv, mixed, cot = attend(cot_send, q, k, v, local, seq)
-    out_own, gres, gm, gwo, gwi, gwu, gvec_b, gib = dense(x, mixed, cot, wo, wi, wu, vecs, ibias)
-    gq, gk, gv, out_back = attend_back(out_own, q, k, v, gm, o, linv, e)
-    gw, gvec_a, ig_back = project_back(x, n1, gq, gk, gv, gres, wqkv, vecs)
-
+    wi = wi.reshape(width, hidden)
+    wu = wu.reshape(hidden, width)
+    out_back, gres, gm, gwo, gwi, ru, gvec, gib = dense(x, mixed, cot, wo, wi, wu, vecs, ibias)
+    gq, gk, gv, igot, ogot, gwu = attend_back(gwi, gwo, ru, q, k, v, gm, o, linv, e, seq)
+    vpart = jnp.zeros((16, width), F32)
+    vpart = vpart.at[4:8].set(0.5 * gvec[jnp.array([3, 1, 2, 0])])
+    bias_rows = hidden // width
+    vpart = lax.dynamic_update_slice(
+        vpart, gib.reshape(bias_rows, width), (8 + c * bias_rows, 0)
+    )
+    gwq, gwk, gwv, gwo, gwi, vec, ig_back = project_back(
+        x, n1, gq, gk, gv, gres, wqkv, vecs, vpart, gwi, igot, gwo, ogot
+    )
     keep32 = valid_slots.astype(F32)[:, None, None]
     outputs = (out_back.reshape(slots, chunk, width)[:, :local].astype(F32) * keep32).astype(BF16)
     input_grad = ig_back.reshape(slots, chunk, width)[:, :local]
-
-    def both_columns(value):
-        wide = jnp.zeros((value.shape[0], 2 * mine), F32)
-        return lax.dynamic_update_slice_in_dim(wide, value, c * mine, axis=1)
-
-    def both_blocks(value, axis):
-        shape = list(value.shape)
-        shape[axis : axis + 1] = [n_f // 2, 1, piece]
-        full = list(shape)
-        full[axis + 1] = 2
-        wide = jnp.zeros(full, F32)
-        wide = lax.dynamic_update_slice_in_dim(wide, value.reshape(shape), c, axis=axis + 1)
-        shape = list(value.shape)
-        shape[axis] = hidden
-        return wide.reshape(shape)
-
-    def reduced(value):
-        return lax.psum_scatter(
-            lax.psum(value, "seq"), "fsdp", scatter_dimension=0, tiled=True
-        )
-
-    grads = dict(
-        first_gain=gvec_a[0],
-        first_shift=gvec_a[1],
-        query_weight=both_columns(gw[:, :mine]),
-        query_bias=both_columns(gvec_a[2:3, :mine])[0],
-        key_weight=both_columns(gw[:, mine : 2 * mine]),
-        value_weight=both_columns(gw[:, 2 * mine :]),
-        value_bias=both_columns(gvec_a[3:4, :mine])[0],
-        output_weight=both_columns(gwo),
-        output_bias=0.5 * gvec_b[3],
-        second_gain=0.5 * gvec_b[1],
-        second_shift=0.5 * gvec_b[2],
-        inner_weight=both_blocks(gwi, 1),
-        inner_bias=both_blocks(gib, 1)[0],
-        outer_weight=both_blocks(gwu, 0),
-        outer_bias=0.5 * gvec_b[0],
+    gwi = gwi.reshape(2, share, n_f // 2, piece).transpose(1, 2, 0, 3).reshape(share, 2 * hidden)
+    own = lax.dynamic_slice(vec, (0, f * share), (8, share))
+    biases = vec[8 : 8 + 2 * bias_rows].reshape(2, n_f // 2, piece)
+    gib = lax.dynamic_slice(biases, (c, m, 0), (1, 1, piece)).reshape(piece)
+    return (
+        outputs,
+        input_grad,
+        own[0],
+        own[1],
+        gwq,
+        own[2],
+        gwk,
+        gwv,
+        own[3],
+        gwo,
+        own[4],
+        own[5],
+        own[6],
+        gwi,
+        gib,
+        gwu,
+        own[7],
     )
-    return (outputs, input_grad) + tuple(reduced(value) for value in grads.values())
 
 
 def solution(mesh):

time: 861 us -> 340 us (0.39)
  waiting for transfers between devices: 368 us -> 0 us
  local copies, waits for them, and re-layouts: 183 us -> 22 us
  Pallas kernels: 219 us -> 306 us
  blocking collectives: 57.7 us -> 0 us
  between operations: 16.2 us -> 1.13 us
    reduce_scatter x6 -> x0, waiting for transfers between devices: 222 us -> none  [reduced(): lax.psum_scatter(lax.psum(value, 'seq'), 'fsdp', scatter_dimension=0, til...]
    psum x1 -> x0, waiting for transfers between devices: 91.5 us -> none  [reduced(): lax.psum(value, 'seq')]
    dynamic_update_slice x9 -> x1, local copies, waits for them, and re-layouts: 89.4 us -> 0.01 us  [per_device(): lax.dynamic_update_slice(vpart, gib.reshape(bias_rows, width), (8 + c * b...]
    pallas_call x1, Pallas kernels: 35.2 us -> 86.6 us  [project_back(): pl.pallas_call(lambda *refs: project_back_kernel(seq, *refs), in_specs=[V...]
    all_gather x6 -> x0, waiting for transfers between devices: 51 us -> none  [gathered(): return lax.all_gather(value, 'fsdp', axis=0, tiled=True)]
    reshape x4 -> x8, local copies, waits for them, and re-layouts: 33.2 us -> 4.11 us  [the longest x2 2.36 us: per_device(): gwi.reshape(2, share, n_f // 2, piece).transpose(1, 2, 0, 3)]
    unnamed x1 -> x0, blocking collectives: 24.8 us -> none
    dynamic_slice x6 -> x2, local copies, waits for them, and re-layouts: 23.6 us -> 1.37 us  [the longest x1 0.77 us: per_device(): own = lax.dynamic_slice(vec, (0, f * share), (8, share))]
  transfers between devices with their start and end apart: 13 -> 0, of which waited for: 8 -> 0; matrix products, arithmetic and copies ran while one was open for 20% -> 0% of each run, Pallas kernels for 10% -> 0%
where the time goes in v2:
time: 340 us; the launch traced here: 334 us
  Pallas kernels  306 us (90%)
  local copies, waits for them, and re-layouts  22 us (6%)
  other arithmetic  4.59 us (1%)
    pallas_call x1, Pallas kernels, project_back(): pl.pallas_call(lambda *refs: project_back_kernel(seq, *refs), in_specs=[V...  86.6 us
    pallas_call x1, Pallas kernels, dense(): pl.pallas_call(lambda *refs: dense_kernel(seq, *refs), in_specs=[VMEM] *...  63.6 us
    pallas_call x1, Pallas kernels, attend(): pl.pallas_call(lambda *refs: attend_kernel(seq, local, heads, *refs), gri...  61.8 us
    pallas_call x1, Pallas kernels, attend_back(): pl.pallas_call(lambda *refs: attend_back_kernel(seq, heads, *refs), grid=...  50.3 us
    pallas_call x1, Pallas kernels, project(): pl.pallas_call(lambda *refs: project_kernel(seq, *refs), in_specs=[ANY] *...  43.9 us
    unnamed x40, local copies, waits for them, and re-layouts  8.19 us

profile of v2, /device:TPU:0, one launch (start us, length us, event | category | flops | bytes accessed | tf_op | source)
XLA Modules:
  0.0 333.8 jit_solution(3730076750954826481)
XLA Ops:
  0.7 0.7 fusion
  1.4 1.4 copy.53
  2.8 1.1 pad.10.clone
  4.1 0.8 pad_maximum_fusion.refs_1_
  4.9 0.6 broadcast_in_dim.41.refs_11_
  5.4 43.9 %project.1 = (bf16[4,2,192,768]{3,2,1,0:T(8,128)(2,1)}, bf16[1536,768]{1,0:T(8,128)(2,1)}, bf16[1536,384]{1,0:T(8,128)(2,1)}, bf16[1536,384]{1,0:T(8,128)(2,1)},...) custom-call(bf16[2,2,192,768]{3,2,1,0:T(8,128)(2,1)} %bitcast.53, ...), custom_call_target="tpu_custom_call" | custom-call | tf_op jit(solution)/shard_map/project/pallas_call | solution.py:429
  49.3 1.1 broadcast_multiply_fusion
  50.5 1.1 pad.11.clone
  51.8 0.4 reshape.121
  52.4 1.0 reshape.122.refs_1_
  53.5 61.8 %attend.1 = (bf16[6,1536,1536]{2,1,0:T(8,128)(2,1)}, f32[1536,384]{1,0:T(8,128)}, f32[1536,384]{1,0:T(8,128)}, bf16[2,3,1536,128]{3,2,1,0:T(8,128)(2,1)}, bf16[4...) custom-call(bf16[2,2,192,768]{3,2,1,0:T(8,128)(2,1)} %bitcast.55, ...), custom_call_target="tpu_custom_call" | custom-call | tf_op jit(solution)/shard_map/attend/pallas_call | solution.py:611
  115.2 63.6 %dense.1 = (bf16[2,2,192,768]{3,2,1,0:T(8,128)(2,1)}, f32[4,192,768]{2,1,0:T(8,128)}, bf16[1536,384]{1,0:T(8,128)(2,1)}, bf16[4,2,96,384]{3,2,1,0:T(8,128)(2,1)}...) custom-call(bf16[4,2,192,768]{3,2,1,0:T(8,128)(2,1)} %get-tuple-element.66., ...), custom_call_target="tpu_custom_call" | custom-call | tf_op jit(solution)/shard_map/dense/pallas_call | solution.py:820
  178.9 1.3 slice.62
  180.2 2.0 multiply_convert_fusion
  182.2 50.3 %attend_back.1 = (bf16[1536,384]{1,0:T(8,128)(2,1)}, bf16[1536,384]{1,0:T(8,128)(2,1)}, bf16[1536,384]{1,0:T(8,128)(2,1)}, bf16[3,2,96,1536]{3,2,1,0:T(8,128)(2,...) custom-call(bf16[4,2,96,1536]{3,2,1,0:T(8,128)(2,1)} %get-tuple-element.79.refs_0_.refs_9_, ...), custom_call_target="tpu_custom_call" | custom-call | tf_op jit(solution)/shard_map/attend_back/pallas_call | solution.py:955
  232.5 0.6 gather_fusion
  233.2 0.6 copy-done.9
  233.8 86.6 %project_back.1 = (f32[96,768]{1,0:T(8,128)}, f32[96,768]{1,0:T(8,128)}, f32[96,768]{1,0:T(8,128)}, f32[96,768]{1,0:T(8,128)}, f32[2,96,1536]{2,1,0:T(8,128)}, /...) custom-call(bf16[4,2,192,768]{3,2,1,0:T(8,128)(2,1)} %get-tuple-element.66.refs_0_, ...), custom_call_target="tpu_custom_call" | custom-call | tf_op jit(solution)/shard_map/project_back/pallas_call | solution.py:1150
  320.4 1.3 slice.63
  321.8 1.9 copy.52
  323.6 0.8 constant_dynamic-slice_fusion
  324.4 0.5 slice_bitcast_fusion
  325.0 0.4 reshape.130
  325.4 0.9 copy.50
  326.3 2.0 reshape.131
  328.3 0.8 slice.58
  329.1 0.6 dynamic-slice_reduce_fusion
  329.7 0.7 copy.71
  330.4 0.7 copy.72
  331.2 0.7 copy.73
  331.9 0.7 copy.74
  332.6 1.0 copy.75
  (42 shorter events, 0.8 us)
Async XLA Ops:
  2.8 1.1 copy-start.11
  2.8 1.1 copy-start.12
  2.8 1.2 copy-start.10
  3.9 1.0 copy-start.14
  4.1 45.2 %copy-start.2 = (bf16[2,375,768]{2,0,1:T(2,128)(2,1)S(1)}, bf16[2,375,768]{2,0,1:T(2,128)(2,1)}, u32[]{:S(2)}) copy-start(bf16[2,375,768]{2,0,1:T(2,128)(2,1)} %param.22) | copy-start | bytes 3456004
  50.5 1.3 copy-start.3
  182.2 50.3 %copy-start.15 = (s32[4]{0:T(128)S(1)}, s32[4]{0:T(128)}, u32[]{:S(2)}) copy-start(s32[4]{0:T(128)} %constant.92) | copy-start | bytes 52
  182.2 50.3 %copy-start.4 = (f32[8,768]{1,0:T(8,128)S(1)}, f32[8,768]{1,0:T(8,128)}, u32[]{:S(2)}) copy-start(f32[8,768]{1,0:T(8,128)} %get-tuple-element.91) | copy-start | bytes 73732
  182.2 50.9 %copy-start.13 = (f32[1,1536]{1,0:T(1,128)S(1)}, f32[1,1536]{1,0:T(1,128)}, u32[]{:S(2)}) copy-start(f32[1,1536]{1,0:T(1,128)} %get-tuple-element.92) | copy-start | bytes 18436
  233.2 0.6 copy-start.9
  321.7 3.2 copy-start.1
  326.3 3.4 %copy-start.8 = (f32[96,768]{1,0:T(8,128)S(1)}, f32[96,768]{1,0:T(8,128)}, u32[]{:S(2)}) copy-start(f32[96,768]{1,0:T(8,128)} %get-tuple-element.136) | copy-start | bytes 884740
  326.3 4.1 %copy-start.7 = (f32[96,768]{1,0:T(8,128)S(1)}, f32[96,768]{1,0:T(8,128)}, u32[]{:S(2)}) copy-start(f32[96,768]{1,0:T(8,128)} %get-tuple-element.138) | copy-start | bytes 884740
  328.3 2.9 copy-start.6
  328.3 3.6 %copy-start.5 = (f32[96,768]{1,0:T(8,128)S(1)}, f32[96,768]{1,0:T(8,128)}, u32[]{:S(2)}) copy-start(f32[96,768]{1,0:T(8,128)} %get-tuple-element.141) | copy-start | bytes 884740
  329.7 2.9 copy-start

commit v3 on v2

v3 whole, which is shorter than its diff:
```python
import math

import jax
import jax.numpy as jnp
from jax import lax
from jax.experimental import pallas as pl
from jax.experimental.pallas import tpu as pltpu
from jax.sharding import PartitionSpec as P

H = 12
HD = 64
EPS = 1e-05
MESH = pl.DeviceIdType.MESH
F32 = jnp.float32
BF16 = jnp.bfloat16
ANY = pl.BlockSpec(memory_space=pl.ANY)
VMEM = pl.BlockSpec(memory_space=pltpu.VMEM)
LIMIT = 62 << 20
QB = 256


def nn(a, b):
    return lax.dot_general(a, b, (((1,), (0,)), ((), ())), preferred_element_type=F32)


def nt(a, b):
    return lax.dot_general(a, b, (((1,), (1,)), ((), ())), preferred_element_type=F32)


def tn(a, b):
    return lax.dot_general(a, b, (((0,), (0,)), ((), ())), preferred_element_type=F32)


def normalize(rows):
    center = rows - jnp.mean(rows, -1, keepdims=True)
    inv = lax.rsqrt(jnp.mean(center * center, -1, keepdims=True) + EPS)
    return center * inv, inv


def norm_back(grad, gain, hat, inv):
    tilted = grad * gain
    first = jnp.mean(tilted, -1, keepdims=True)
    cross = jnp.mean(tilted * hat, -1, keepdims=True)
    return inv * (tilted - first - hat * cross)


def where_am_i():
    f = lax.axis_index("fsdp")
    z = lax.axis_index("seq")
    return f, z, f // 2, f % 2


def meet(peers):
    barrier = pltpu.get_barrier_semaphore()
    for peer in peers:
        pl.semaphore_signal(barrier, inc=1, device_id=peer, device_id_type=MESH)
    pl.semaphore_wait(barrier, len(peers))


def column_peers(seq):
    f, z, m, c = where_am_i()
    peers = []
    for dc in range(2):
        for dz in range(seq):
            if dc or dz:
                peers.append((m * 2 + (c + dc) % 2, (z + dz) % seq))
    return peers


class Ship:
    def __init__(self, src, dst, send, recv, target):
        f, z, _, _ = where_am_i()
        self.here = jnp.logical_and(target[0] == f, target[1] == z)
        self.local = pltpu.make_async_copy(src, dst, recv)
        self.remote = pltpu.make_async_remote_copy(
            src, dst, send, recv, device_id=target, device_id_type=MESH
        )

    def start(self):
        pl.when(self.here)(self.local.start)
        pl.when(jnp.logical_not(self.here))(self.remote.start)

    def wait_send(self):
        pl.when(jnp.logical_not(self.here))(self.remote.wait_send)


def remote(src, dst, send, recv, target):
    return pltpu.make_async_remote_copy(
        src, dst, send, recv, device_id=target, device_id_type=MESH
    )


class Gather:
    def __init__(self, send_ref, full_ref, send_sem, recv_sem, pass_send, pass_recv, seq):
        f, z, m, c = where_am_i()
        self.ships = []
        for i in range(2):
            for h in range(2):
                slot = 2 * c + i
                self.ships.append(
                    Ship(
                        send_ref.at[i, h],
                        full_ref.at[z, h],
                        send_sem.at[i, h],
                        recv_sem.at[z],
                        (m * 2 + h, slot),
                    )
                )
        other = (m * 2 + 1 - c, z)
        chips = [(z + d) % seq for d in range(seq)]
        self.arrivals = [
            remote(send_ref.at[0, 0], full_ref.at[k, c], send_sem.at[0, 0], recv_sem.at[k], other)
            for k in chips
        ]
        self.passes = [
            remote(full_ref.at[k, c], full_ref.at[k, c], pass_send.at[d], pass_recv.at[d], other)
            for d, k in enumerate(chips)
        ]
        self.handed = [
            remote(
                full_ref.at[k, c], full_ref.at[k, 1 - c], pass_send.at[d], pass_recv.at[d], other
            )
            for d, k in enumerate(chips)
        ]

    def start(self):
        for ship in self.ships:
            ship.start()

    def hand_on(self, k):
        self.arrivals[k].wait_recv()
        self.passes[k].start()

    def ready(self, k):
        self.handed[k].wait_recv()

    def finish(self):
        for ship in self.ships:
            ship.wait_send()
        for item in self.passes:
            item.wait_send()


GATHER_SEMS = lambda seq: [
    pltpu.SemaphoreType.DMA((2, 2)),
    pltpu.SemaphoreType.DMA((seq,)),
    pltpu.SemaphoreType.DMA((seq,)),
    pltpu.SemaphoreType.DMA((seq,)),
]


class Return:
    def __init__(self, own_ref, back_ref, send_sem, recv_sem, seq):
        f, z, m, c = where_am_i()
        home = z // 2
        self.ships = [
            Ship(
                own_ref.at[k],
                back_ref.at[z % 2, c],
                send_sem.at[k],
                recv_sem.at[z % 2, c],
                (m * 2 + home, k),
            )
            for k in range(seq)
        ]
        self.arrivals = [
            remote(
                own_ref.at[0],
                back_ref.at[i, h],
                send_sem.at[0],
                recv_sem.at[i, h],
                (m * 2 + 1 - c, z),
            )
            for i in range(2)
            for h in range(2)
        ]

    def start(self):
        for ship in self.ships:
            ship.start()

    def finish(self):
        for ship in self.ships:
            ship.wait_send()
        for item in self.arrivals:
            item.wait_recv()


RETURN_SEMS = lambda seq: [pltpu.SemaphoreType.DMA((seq,)), pltpu.SemaphoreType.DMA((2, 2))]


class Spread:
    def __init__(self, source, full_ref, send_sem, recv_sem, local_sem, stride):
        f, z, m, c = where_am_i()
        n_f = lax.axis_size("fsdp")
        steps = n_f // stride
        slot = f if stride == 1 else m
        self.local = pltpu.make_async_copy(source(f), full_ref.at[slot], local_sem)
        self.sends = []
        self.arrivals = []
        for d in range(1, steps):
            to = (f + d * stride) % n_f
            back = (f + n_f - d * stride) % n_f
            self.sends.append(
                remote(source(to), full_ref.at[slot], send_sem.at[d], recv_sem.at[d], (to, z))
            )
            place = back if stride == 1 else back // 2
            self.arrivals.append(
                remote(source(f), full_ref.at[place], send_sem.at[d], recv_sem.at[d], (to, z))
            )

    def start(self):
        self.local.start()
        for item in self.sends:
            item.start()

    def relay(self):
        pass

    def ready(self):
        self.local.wait()
        for item in self.arrivals:
            item.wait_recv()

    def finish(self):
        for item in self.sends:
            item.wait_send()


class Relay:
    def __init__(self, source, full_ref, send_sem, recv_sem, local_sem, stride):
        f, z, m, c = where_am_i()
        x, y = m % 2, m // 2
        beside, above, far = y * 2 + 1 - x, (1 - y) * 2 + x, (1 - y) * 2 + 1 - x

        def slot(chip, core):
            return chip * 2 + core if stride == 1 else chip

        self.local = pltpu.make_async_copy(source(f), full_ref.at[slot(m, c)], local_sem)
        self.sends, self.inner, self.near, self.relays, self.rest = [], [], [], [], []
        rows = full_ref.shape[1] // 2
        parts = [pl.ds(0, rows), pl.ds(rows, rows)]
        k = 0
        for dc in range(2 // stride):
            core = (c + dc) % 2
            chips = [beside, above] + ([m] if dc else [])
            for chip in chips:
                to = (chip * 2 + core, z)
                mine = full_ref.at[slot(m, c)]
                theirs = full_ref.at[slot(chip, core)]
                src = source(chip * 2 + core)
                self.sends.append(remote(src, mine, send_sem.at[k], recv_sem.at[k], to))
                got = remote(src, theirs, send_sem.at[k], recv_sem.at[k], to)
                (self.inner if chip is m else self.near).append(got)
                k += 1
            for chip, onto, part in ((beside, above, parts[0]), (above, beside, parts[1])):
                to = (onto * 2 + c, z)
                piece = full_ref.at[slot(chip, core), part]
                self.relays.append(remote(piece, piece, send_sem.at[k], recv_sem.at[k], to))
                lands = full_ref.at[slot(far, core), part]
                self.rest.append(remote(lands, lands, send_sem.at[k], recv_sem.at[k], to))
                k += 1

    def start(self):
        self.local.start()
        for item in self.sends:
            item.start()

    def relay(self):
        for item in self.near:
            item.wait_recv()
        for item in self.relays:
            item.start()

    def ready(self):
        self.local.wait()
        for item in self.inner + self.rest:
            item.wait_recv()

    def finish(self):
        for item in self.sends + self.relays:
            item.wait_send()


def spreading(source, full_ref, sems, stride):
    kind = Relay if lax.axis_size("fsdp") == 8 else Spread
    return kind(source, full_ref, *sems, stride)


def spread_sems(steps):
    steps = max(steps, 9)
    return [
        pltpu.SemaphoreType.DMA((steps,)),
        pltpu.SemaphoreType.DMA((steps,)),
        pltpu.SemaphoreType.DMA,
    ]


def fsdp_peers():
    f, z, _, _ = where_am_i()
    n_f = lax.axis_size("fsdp")
    return [((f + d) % n_f, z) for d in range(1, n_f)]


def all_peers(seq):
    f, z, m, c = where_am_i()
    other = m * 2 + 1 - c
    peers = fsdp_peers()
    for d in range(1, seq):
        peers.append((f, (z + d) % seq))
        peers.append((other, (z + d) % seq))
    return peers


class Scatter:
    def __init__(self, part, got_ref, send_sem, recv_sem):
        f, z, m, c = where_am_i()
        n_m = lax.axis_size("fsdp") // 2
        self.part, self.got, self.chip = part, got_ref, m
        self.copies = []
        for d in range(1, n_m):
            to = (m + d) % n_m
            self.copies.append(
                remote(
                    part(to),
                    got_ref.at[d - 1],
                    send_sem.at[d],
                    recv_sem.at[d],
                    (to * 2 + c, z),
                )
            )

    def start(self):
        for item in self.copies:
            item.start()

    def total(self, own):
        for item in self.copies:
            item.wait_recv()
        result = own.astype(F32)
        for k in range(len(self.copies)):
            result = result + self.got[k].astype(F32)
        return result

    def finish(self):
        for item in self.copies:
            item.wait_send()


def scatter_sems():
    n_m = lax.axis_size("fsdp") // 2
    return [pltpu.SemaphoreType.DMA((n_m,)), pltpu.SemaphoreType.DMA((n_m,))]


class Across:
    def __init__(self, own_ref, spare_ref, sems):
        f, z, _, _ = where_am_i()
        self.own, self.spare = own_ref, spare_ref
        self.edge = jnp.logical_or(z == 0, z == 3)
        self.inner = jnp.logical_not(self.edge)
        beside = jnp.where(z < 2, 1 - z, 5 - z)
        self.up = remote(own_ref, spare_ref.at[0], sems.at[0], sems.at[1], (f, beside))
        self.swap = remote(own_ref, spare_ref.at[1], sems.at[2], sems.at[3], (f, 3 - z))
        self.down = remote(own_ref, spare_ref.at[1], sems.at[4], sems.at[5], (f, beside))

    def add(self, k):
        total = self.own[...].astype(F32) + self.spare[k].astype(F32)
        self.own[...] = total.astype(self.own.dtype)

    def rise(self):
        pl.when(self.edge)(self.up.start)

    def risen(self):
        @pl.when(self.inner)
        def _():
            self.up.wait_recv()
            self.add(0)

        pl.when(self.edge)(self.up.wait_send)

    def cross(self):
        pl.when(self.inner)(self.swap.start)

    def crossed(self):
        @pl.when(self.inner)
        def _():
            self.swap.wait()
            self.add(1)

    def fall(self):
        pl.when(self.inner)(self.down.start)

    def fallen(self):
        @pl.when(self.edge)
        def _():
            self.down.wait_recv()
            self.own[...] = self.spare[1]

        pl.when(self.inner)(self.down.wait_send)


ACROSS_SEMS = pltpu.SemaphoreType.DMA((6,))


def project_kernel(
    seq, x_send, wqkv_send, wo_send,
    first_gain, first_shift, query_bias, value_bias, output_bias, second_gain, second_shift,
    outer_bias, inner_bias,
    x_full, n1_out, q_out, k_out, v_out, wqkv_out, wo_out, vecs_out, ibias_out,
    ssem, rsem, psend, precv,
    qsend, qrecv, qlocal, osend, orecv, olocal, vsend, vrecv, vlocal,
    xv, wqkv, small, smalls, lsem, wsem,
):
    f, z, m, c = where_am_i()
    n_f = lax.axis_size("fsdp")
    share = first_gain.shape[1]
    piece = inner_bias.shape[1]
    small[...] = jnp.zeros_like(small)
    for r, ref in enumerate(
        (
            first_gain,
            first_shift,
            query_bias,
            value_bias,
            output_bias,
            second_gain,
            second_shift,
            outer_bias,
        )
    ):
        small[r : r + 1, :share] = ref[...].astype(F32)
    small[8:9, :piece] = inner_bias[...].astype(F32)
    meet(all_peers(seq))
    gather = Gather(x_send, xv, ssem, rsem, psend, precv, seq)
    vectors = Spread(lambda to: small, smalls, vsend, vrecv, vlocal, 1)
    weights = spreading(lambda to: wqkv_send.at[to % 2], wqkv, (qsend, qrecv, qlocal), 1)
    later = spreading(lambda to: wo_send, wo_out, (osend, orecv, olocal), 1)
    vectors.start()
    gather.start()
    weights.start()
    half = xv.shape[2]
    mine = q_out.shape[1]
    width = n1_out.shape[1]

    vectors.ready()
    row = lax.broadcasted_iota(jnp.int32, (128, width), 0)
    col = lax.broadcasted_iota(jnp.int32, (128, width), 1)
    vecs = jnp.zeros((16, width), F32)
    for k in range(n_f):
        spot = jnp.logical_and(col - k * share == row, row < share)
        vecs = vecs + nn(
            smalls[k, :, :128].astype(BF16), jnp.where(spot, 1.0, 0.0).astype(BF16)
        )
    vecs_out[...] = vecs[:8]
    for k in range(n_f // 2):
        ibias_out[0:1, k * piece : (k + 1) * piece] = smalls[2 * k + c, 8:9, :piece]
    weights.relay()
    later.start()
    weights.ready()
    keep_weights = pltpu.make_async_copy(wqkv, wqkv_out, wsem)
    keep_weights.start()
    gain = vecs_out[0:1, :]
    shift = vecs_out[1:2, :]
    cols = pl.ds(pl.multiple_of(c * mine, 128), mine)
    qb = vecs_out[2:3, cols]
    vb = vecs_out[3:4, cols]
    keeps = []
    for d in sorted(range(seq), key=lambda d: min(d, seq - d)):
        k = (z + d) % seq
        gather.hand_on(d)
        gather.ready(d)
        keeps.append(pltpu.make_async_copy(xv.at[k], x_full.at[k], lsem.at[d]))
        keeps[-1].start()
        rows = pl.ds(pl.multiple_of(k * 2 * half, 16), 2 * half)
        hat, _ = normalize(xv[k].reshape(2 * half, width).astype(F32))
        normed = (hat * gain + shift).astype(BF16)
        n1_out[rows, :] = normed
        qkv = nn(normed, wqkv[...].reshape(width, 3 * mine))
        q_out[rows, :] = (qkv[:, :mine] + qb).astype(BF16)
        k_out[rows, :] = qkv[:, mine : 2 * mine].astype(BF16)
        v_out[rows, :] = (qkv[:, 2 * mine :] + vb).astype(BF16)
        if d == 1:
            later.relay()
    gather.finish()
    for item in keeps:
        item.wait()
    later.ready()
    vectors.finish()
    weights.finish()
    later.finish()
    keep_weights.wait()


def project(x_send, wqkv_send, wo_send, vectors, seq):
    _, _, half, width = x_send.shape
    n_f = lax.axis_size("fsdp")
    rows = seq * 2 * half
    share = wo_send.shape[0]
    mine = wqkv_send.shape[2] // 3
    piece = vectors[-1].shape[1]
    lanes = max(128, piece)
    return pl.pallas_call(
        lambda *refs: project_kernel(seq, *refs),
        in_specs=[ANY] * 3 + [VMEM] * 9,
        out_specs=[ANY, VMEM, VMEM, VMEM, VMEM, ANY, ANY, VMEM, VMEM],
        out_shape=[
            jax.ShapeDtypeStruct((seq, 2, half, width), BF16),
            jax.ShapeDtypeStruct((rows, width), BF16),
        ]
        + [jax.ShapeDtypeStruct((rows, mine), BF16)] * 3
        + [
            jax.ShapeDtypeStruct((n_f, share, 3 * mine), BF16),
            jax.ShapeDtypeStruct((n_f, share, width), BF16),
            jax.ShapeDtypeStruct((8, width), F32),
            jax.ShapeDtypeStruct((1, piece * n_f // 2), F32),
        ],
        scratch_shapes=GATHER_SEMS(seq)
        + spread_sems(n_f)
        + spread_sems(n_f)
        + spread_sems(n_f)
        + [
            pltpu.VMEM((seq, 2, half, width), BF16),
            pltpu.VMEM((n_f, share, 3 * mine), BF16),
            pltpu.VMEM((16, lanes), F32),
            pltpu.VMEM((n_f, 16, lanes), F32),
            pltpu.SemaphoreType.DMA((seq,)),
            pltpu.SemaphoreType.DMA,
        ],
        compiler_params=pltpu.CompilerParams(
            collective_id=0, has_side_effects=True, vmem_limit_bytes=LIMIT
        ),
        name="project",
    )(x_send, wqkv_send, wo_send, *vectors)


def project_plain_kernel(seq, x_send, wqkv, vecs, x_full, n1_out, q_out, k_out, v_out,
                         ssem, rsem, psend, precv, xv, lsem):
    f, z, m, c = where_am_i()
    meet(column_peers(seq))
    gather = Gather(x_send, x_full, ssem, rsem, psend, precv, seq)
    gather.start()
    half = xv.shape[1]
    mine = q_out.shape[1]
    for d in range(seq):
        gather.hand_on(d)
    for d in range(seq):
        gather.ready(d)
    gain = vecs[0:1, :]
    shift = vecs[1:2, :]
    cols = pl.ds(pl.multiple_of(c * mine, 128), mine)
    qb = vecs[2:3, cols]
    vb = vecs[3:4, cols]
    for k in range(seq):
        copy = pltpu.make_async_copy(x_full.at[k], xv, lsem)
        copy.start()
        copy.wait()
        rows = pl.ds(k * 2 * half, 2 * half)
        hat, _ = normalize(xv[...].reshape(2 * half, -1).astype(F32))
        normed = (hat * gain + shift).astype(BF16)
        n1_out[rows, :] = normed
        qkv = nn(normed, wqkv[...])
        q_out[rows, :] = (qkv[:, :mine] + qb).astype(BF16)
        k_out[rows, :] = qkv[:, mine : 2 * mine].astype(BF16)
        v_out[rows, :] = (qkv[:, 2 * mine :] + vb).astype(BF16)
    gather.finish()


def project_plain(x_send, wqkv, vecs, seq):
    _, _, half, width = x_send.shape
    rows = seq * 2 * half
    mine = wqkv.shape[1] // 3
    return pl.pallas_call(
        lambda *refs: project_plain_kernel(seq, *refs),
        in_specs=[ANY, VMEM, VMEM],
        out_specs=[ANY, VMEM, VMEM, VMEM, VMEM],
        out_shape=[
            jax.ShapeDtypeStruct((seq, 2, half, width), BF16),
            jax.ShapeDtypeStruct((rows, width), BF16),
        ]
        + [jax.ShapeDtypeStruct((rows, mine), BF16)] * 3,
        scratch_shapes=GATHER_SEMS(seq)
        + [pltpu.VMEM((2, half, width), BF16), pltpu.SemaphoreType.DMA],
        compiler_params=pltpu.CompilerParams(
            collective_id=5, has_side_effects=True, vmem_limit_bytes=LIMIT
        ),
        name="project_plain",
    )(x_send, wqkv, vecs)


def attend_kernel(
    seq, local, pairs, cot_send, wi_send, q, k, v,
    e_out, o_out, linv_out, mixed_out, cot_full, wi_out,
    ssem, rsem, psend, precv, isend, irecv, ilocal,
    stage, qa, ka, va, msend, mrecv, mlocal,
):
    f, z, m, c = where_am_i()
    pair = pl.program_id(0)
    rows = q.shape[0]
    gather = Gather(cot_send, cot_full, ssem, rsem, psend, precv, seq)
    weights = spreading(lambda to: wi_send.at[to % 2], wi_out, (isend, irecv, ilocal), 1)
    other = (m * 2 + 1 - c, z)

    @pl.when(pair == 0)
    def _():
        meet(all_peers(seq))
        gather.start()
        weights.start()

    pl.when(pair == pairs - 1)(weights.relay)

    lane = lax.broadcasted_iota(jnp.int32, (1, 128), 1)
    low = lane < HD
    place = lax.broadcasted_iota(jnp.int32, (rows, 1), 0) % (rows // seq)
    bar = jnp.where(place < local, 0.0, -1e38).astype(F32)
    qf, kf, vf = q[...].astype(F32), k[...].astype(F32), v[...].astype(F32)
    for a in range(2):
        mine = low if a == 0 else jnp.logical_not(low)
        first = lane == HD * (1 - a)
        qa[a] = jnp.where(mine, qf, jnp.where(first, 1.0, 0.0)).astype(BF16)
        ka[a] = jnp.where(mine, kf, jnp.where(first, bar, 0.0)).astype(BF16)
        va[a] = jnp.where(mine, vf, 1.0).astype(BF16)
    factor = HD ** (-0.5) * math.log2(math.e)
    steps = [(i, a) for i in range(rows // QB) for a in range(2)]

    def block(i):
        return slice(i * QB, (i + 1) * QB)

    def scored(t):
        i, a = steps[t]
        return nt(qa[a, block(i), :], ka[a])

    raws = {}

    def finish(t, expo):
        i, a = steps[t]
        raws[a] = nn(expo, va[a])
        if a == 1:
            sl = block(i)
            total = pltpu.roll(jnp.where(low, raws[1], raws[0]), HD, 1)
            inv = 1.0 / total
            res = jnp.where(low, raws[0], raws[1]) * inv
            o_out[sl, :] = res
            linv_out[sl, :] = inv
            stage[pair, sl, :] = res.astype(BF16)

    scores, before = scored(0), None
    for t, (i, a) in enumerate(steps):
        peak = jnp.max(scores, -1, keepdims=True)
        upcoming = scored(t + 1) if t + 1 < len(steps) else None
        if before is not None:
            finish(t - 1, before)
        expo = jnp.exp2((scores - peak) * factor).astype(BF16)
        e_out[a, block(i), :] = expo
        scores, before = upcoming, expo
    finish(len(steps) - 1, before)

    def mixed_copies(p):
        return (
            pltpu.make_async_copy(stage.at[p], mixed_out.at[c, p], mlocal.at[p]),
            remote(stage.at[p], mixed_out.at[c, p], msend.at[p], mrecv.at[p], other),
            remote(stage.at[p], mixed_out.at[1 - c, p], msend.at[p], mrecv.at[p], other),
        )

    here, there, _ = mixed_copies(pair)
    here.start()
    there.start()

    @pl.when(pair == pairs - 1)
    def _():
        for item in range(seq):
            gather.hand_on(item)
        weights.ready()
        weights.finish()
        for item in range(seq):
            gather.ready(item)
        gather.finish()
        for p in range(pairs):
            here, there, back = mixed_copies(p)
            here.wait()
            there.wait_send()
            back.wait_recv()


def attend(cot_send, wi_send, q, k, v, local, seq):
    rows, mine = q.shape
    n_f = lax.axis_size("fsdp")
    _, _, half, width = cot_send.shape
    pairs = mine // 128
    by_pair = pl.BlockSpec((rows, 128), lambda p: (0, p))
    return pl.pallas_call(
        lambda *refs: attend_kernel(seq, local, pairs, *refs),
        grid=(pairs,),
        in_specs=[ANY, ANY, by_pair, by_pair, by_pair],
        out_specs=[
            pl.BlockSpec((2, rows, rows), lambda p: (p, 0, 0)),
            by_pair,
            by_pair,
            ANY,
            ANY,
            ANY,
        ],
        out_shape=[
            jax.ShapeDtypeStruct((2 * pairs, rows, rows), BF16),
            jax.ShapeDtypeStruct((rows, mine), F32),
            jax.ShapeDtypeStruct((rows, mine), F32),
            jax.ShapeDtypeStruct((2, pairs, rows, 128), BF16),
            jax.ShapeDtypeStruct((seq, 2, half, width), BF16),
            jax.ShapeDtypeStruct((n_f,) + wi_send.shape[1:], BF16),
        ],
        scratch_shapes=GATHER_SEMS(seq)
        + spread_sems(n_f)
        + [
            pltpu.VMEM((pairs, rows, 128), BF16),
            pltpu.VMEM((2, rows, 128), BF16),
            pltpu.VMEM((2, rows, 128), BF16),
            pltpu.VMEM((2, rows, 128), BF16),
            pltpu.SemaphoreType.DMA((pairs,)),
            pltpu.SemaphoreType.DMA((pairs,)),
            pltpu.SemaphoreType.DMA((pairs,)),
        ],
        compiler_params=pltpu.CompilerParams(
            collective_id=1, has_side_effects=True, vmem_limit_bytes=LIMIT
        ),
        name="attend",
    )(cot_send, wi_send, q, k, v)


def gelu_parts(u):
    x = jnp.abs(u) * (1.0 / math.sqrt(2.0))
    t = 1.0 / (1.0 + 0.3275911 * x)
    poly = t * (
        0.254829592
        + t * (-0.284496736 + t * (1.421413741 + t * (-1.453152027 + t * 1.061405429)))
    )
    expo = jnp.exp(-x * x)
    tail = 0.5 * poly * expo
    phi = jnp.where(u >= 0, 1.0 - tail, tail)
    return phi, u * expo * (1.0 / math.sqrt(2.0 * math.pi))


def dense_kernel(
    seq, x, mixed_in, cot_in, wo_in, wi_in, wu_send, vecs, ibias,
    out_back, gres_own, gm_out, gwo_out, gwi_out, ru_out, gvec_out, gib_out,
    xv, mixed, cot, wo, wi, wu, n2, hat2, inv2, resid, active, slope, out_own,
    pstage, precv, grecv, ugot, upart,
    psem, prsem, gsem, grsem, bsend, brecv, usend, urecv, wsend, wrecv, wlocal, lsem, xsem,
):
    f, z, m, c = where_am_i()
    other = (m * 2 + 1 - c, z)
    half = x.shape[2]
    chunk = 2 * half
    width = x.shape[3]
    mine = gm_out.shape[1]
    hidden = wi.shape[1]
    n_m = gwi_out.shape[0]
    share = gwi_out.shape[2]
    piece = upart.shape[1]
    rows = seq * chunk
    tile = 512

    def block(i):
        return pl.ds(i * chunk, chunk)

    def fetch_x(i):
        return pltpu.make_async_copy(x.at[i], xv.at[i % 2], xsem.at[i % 2])

    loads = [
        pltpu.make_async_copy(src, dst, lsem.at[k])
        for k, (src, dst) in enumerate(
            ((mixed_in, mixed), (wo_in, wo), (wi_in, wi), (cot_in, cot))
        )
    ]
    fetch_x(0).start()
    for item in loads:
        item.start()
    meet(all_peers(seq))
    weights = spreading(lambda to: wu_send, wu, (wsend, wrecv, wlocal), 2)
    weights.start()
    obias, gain, shift, ubias = vecs[4:5, :], vecs[5:6, :], vecs[6:7, :], vecs[7:8, :]
    back = Return(out_own, out_back, bsend, brecv, seq)
    gstage = active.at[:, :width]
    branch = active.at[:, width : 2 * width]
    gown = resid

    def p_copy(i):
        return remote(pstage.at[i, 1 - c], precv.at[i], psem.at[i], prsem.at[i], other)

    def g_copy(i):
        return remote(gstage.at[block(i)], grecv.at[block(i)], gsem.at[i], grsem.at[i], other)

    def mixed_rows(sl):
        return jnp.concatenate(
            [mixed[a, p, sl, :] for a in range(2) for p in range(mixed.shape[1])], axis=1
        )

    for item in loads[:3]:
        item.wait()
    for i in range(seq):
        sl = block(i)
        fetch_x(i).wait()
        if i + 1 < seq:
            fetch_x(i + 1).start()
        frames = xv[i % 2].reshape(chunk, width).astype(F32)
        res = frames + nn(mixed_rows(sl), wo[...]) + obias
        hat, inv = normalize(res)
        normed = (hat * gain + shift).astype(BF16)
        resid[sl, :] = res + ubias
        n2[sl, :] = normed
        hat2[sl, :] = hat
        inv2[sl, :] = jnp.broadcast_to(inv, (chunk, 128))
        for j in range(0, hidden, tile):
            cols = slice(j, j + tile)
            inner = nn(normed, wi[:, cols]) + ibias[:, cols]
            phi, bump = gelu_parts(inner)
            active[sl, cols] = (inner * phi).astype(BF16)
            slope[sl, cols] = (phi + bump).astype(BF16)
        if i == seq // 2:
            weights.relay()
    weights.ready()
    loads[3].wait()
    wuf = wu.at[...]

    def outer_weight():
        return wuf[...].reshape(hidden, width)

    for i in range(seq):
        sl = block(i)
        pout = nn(active[sl, :], outer_weight())
        resid[sl, :] += pout
        pstage[i] = pout.astype(BF16).reshape(2, half, width)
        p_copy(i).start()
    cots = cot[...].reshape(rows, width)
    outer = Scatter(lambda to: upart.at[to], ugot, usend, urecv)
    if piece % 128 == 0:
        for d in range(n_m):
            k = (m + 1 + d) % n_m
            at = pl.ds(pl.multiple_of(k * piece, 128), piece)
            upart[k] = tn(active[:, at], cots).astype(BF16)
            if d < n_m - 1:
                outer.copies[d].start()
    else:
        for k in range(n_m):
            upart[k] = tn(active[:, k * piece : (k + 1) * piece], cots).astype(BF16)
        outer.start()
    for i in range(seq):
        p_copy(i).wait_recv()
        out_own[i] = (
            resid[pl.ds(pl.multiple_of(i * chunk + c * half, 16), half), :]
            + precv[i].astype(F32)
        ).astype(BF16)
    back.start()
    gvec_out[0:1, :] = jnp.sum(cots.astype(F32), 0, keepdims=True)
    for i in range(seq):
        sl = block(i)
        g = cot[i].reshape(chunk, width)
        for j in range(0, hidden, piece):
            cols = slice(j, j + piece)
            gi = (nt(g, wu[j // piece]) * slope[sl, cols].astype(F32)).astype(BF16)
            slope[sl, cols] = gi
            line = jnp.sum(gi.astype(F32), 0, keepdims=True)
            if i == 0:
                gib_out[:, cols] = line
            else:
                gib_out[:, cols] += line
        gn2 = nt(slope[sl, :], wi[...])
        gown[sl, :] = gn2
        gstage[sl, :] = gn2.astype(BF16)
        g_copy(i).start()
    for j in range(0, hidden, tile):
        part = tn(n2[...], slope[:, j : j + tile])
        for k in range(n_m):
            for b in range(2):
                at = (2 * k + b) * share
                gwi_out[k, b, :, j : j + tile] = part[at : at + share, :].astype(BF16)
    wrows = pl.ds(pl.multiple_of(c * mine, 128), mine)
    for i in range(seq):
        sl = block(i)
        g_copy(i).wait_recv()
        gn2 = gown[sl, :] + grecv[sl, :].astype(F32)
        hat = hat2[sl, :]
        line = jnp.sum(gn2 * hat, 0, keepdims=True)
        flat = jnp.sum(gn2, 0, keepdims=True)
        g = cot[i].reshape(chunk, width).astype(F32)
        gres = g + norm_back(gn2, gain, hat, inv2[sl, 0:1])
        hat2[sl, :] = gres
        low = gres.astype(BF16)
        branch[sl, :] = low
        total = jnp.sum(low.astype(F32), 0, keepdims=True)
        if i == 0:
            lines, flats, totals = line, flat, total
        else:
            lines, flats, totals = lines + line, flats + flat, totals + total
        gm_out[sl, :] = nt(low, wo[wrows, :]).astype(BF16)
        gres_own[i] = hat2[pl.ds(pl.multiple_of(i * chunk + c * half, 16), half), :]
    gvec_out[1:2, :] = lines
    gvec_out[2:3, :] = flats
    gvec_out[3:4, :] = totals
    gvec_out[4:8, :] = jnp.zeros((4, width), F32)
    part = tn(
        mixed_rows(slice(None)),
        active[:, pl.ds(pl.multiple_of(width + c * mine, 128), mine)],
    )
    for k in range(n_m):
        for b in range(2):
            at = (2 * k + b) * share
            gwo_out[k, b] = part[at : at + share, :].astype(BF16)
    for i in range(seq):
        p_copy(i).wait_send()
        g_copy(i).wait_send()
    weights.finish()
    ru_out[...] = outer.total(upart[m]).astype(BF16)
    outer.finish()
    back.finish()


def dense(x, mixed, cot, wo, wi, wu_send, vecs, ibias):
    seq, _, half, width = x.shape
    rows = seq * 2 * half
    hidden = wi.shape[1]
    mine = width // 2
    n_f = lax.axis_size("fsdp")
    n_m = n_f // 2
    share = width // n_f
    piece = hidden // n_m
    return pl.pallas_call(
        lambda *refs: dense_kernel(seq, *refs),
        in_specs=[ANY] * 6 + [VMEM] * 2,
        out_specs=[ANY] + [VMEM] * 7,
        out_shape=[
            jax.ShapeDtypeStruct((2, 2, half, width), BF16),
            jax.ShapeDtypeStruct((seq, half, width), F32),
            jax.ShapeDtypeStruct((rows, mine), BF16),
            jax.ShapeDtypeStruct((n_m, 2, share, mine), BF16),
            jax.ShapeDtypeStruct((n_m, 2, share, hidden), BF16),
            jax.ShapeDtypeStruct((piece, width), BF16),
            jax.ShapeDtypeStruct((8, width), F32),
            jax.ShapeDtypeStruct((1, hidden), F32),
        ],
        scratch_shapes=[
            pltpu.VMEM((2, 2, half, width), BF16),
            pltpu.VMEM(mixed.shape, BF16),
            pltpu.VMEM(cot.shape, BF16),
            pltpu.VMEM(wo.shape, BF16),
            pltpu.VMEM(wi.shape, BF16),
            pltpu.VMEM((n_m, piece, width), BF16),
            pltpu.VMEM((rows, width), BF16),
            pltpu.VMEM((rows, width), F32),
            pltpu.VMEM((rows, 128), F32),
            pltpu.VMEM((rows, width), F32),
            pltpu.VMEM((rows, hidden), BF16),
            pltpu.VMEM((rows, hidden), BF16),
            pltpu.VMEM((seq, half, width), BF16),
            pltpu.VMEM((seq, 2, half, width), BF16),
            pltpu.VMEM((seq, half, width), BF16),
            pltpu.VMEM((rows, width), BF16),
            pltpu.VMEM((n_m - 1, piece, width), BF16),
            pltpu.VMEM((n_m, piece, width), BF16),
            pltpu.SemaphoreType.DMA((seq,)),
            pltpu.SemaphoreType.DMA((seq,)),
            pltpu.SemaphoreType.DMA((seq,)),
            pltpu.SemaphoreType.DMA((seq,)),
        ]
        + RETURN_SEMS(seq)
        + scatter_sems()
        + spread_sems(n_m)
        + [pltpu.SemaphoreType.DMA((4,)), pltpu.SemaphoreType.DMA((2,))],
        compiler_params=pltpu.CompilerParams(
            collective_id=2, has_side_effects=True, vmem_limit_bytes=LIMIT
        ),
        name="dense",
    )(x, mixed, cot, wo, wi, wu_send, vecs, ibias)


def attend_back_kernel(
    seq, pairs, gwi, gwo, ru, q, k, v, gm, o, linv, e,
    gq_out, gk_out, gv_out, ri_out, ro_out, gwu_out,
    asend, arecv, bsend, brecv, osend, orecv, zu, za, zb,
    uown, uspare, aown, aspare, bown, bspare, igot, ogot, oown, lsem,
    do, dot_, qt, va, km, dvt, dkt,
):
    pair = pl.program_id(0)
    rows = q.shape[0]
    m = lax.axis_index("fsdp") // 2
    inner = [
        Scatter(lambda to: gwi.at[to, 0], igot.at[0], asend, arecv),
        Scatter(lambda to: gwi.at[to, 1], igot.at[1], bsend, brecv),
    ]
    out = Scatter(lambda to: gwo.at[to], ogot, osend, orecv)
    outer = Across(uown, uspare, zu)
    halves = [Across(aown, aspare, za), Across(bown, bspare, zb)]
    loads = [
        pltpu.make_async_copy(src, dst, lsem.at[k])
        for k, (src, dst) in enumerate(
            ((ru, uown), (gwi.at[m, 0], aown), (gwi.at[m, 1], bown), (gwo.at[m], oown))
        )
    ]

    def sum_half(k):
        own = halves[k].own
        own[...] = inner[k].total(own[...]).astype(BF16)

    def at(step, place, action):
        def run():
            pl.when(pair == step)(action)

        events.setdefault(place, []).append(run)

    events = {}

    def begin():
        for item in loads:
            item.start()
        meet(all_peers(seq))
        inner[0].start()
        for item in loads:
            item.wait()
        outer.rise()

    def one():
        outer.risen()
        outer.cross()

    def two():
        inner[1].start()
        outer.crossed()
        outer.fall()

    def three():
        sum_half(0)
        halves[0].rise()

    def four():
        out.start()
        halves[0].risen()
        halves[0].cross()

    def five():
        sum_half(1)
        halves[1].rise()
        outer.fallen()
        gwu_out[...] = uown[...].astype(F32)

    at(0, 0, begin)
    at(0, 1, one)
    at(1, 0, two)
    at(1, 1, three)
    at(2, 0, four)
    at(2, 1, five)
    for run in events[0]:
        run()
    third = HD ** (-0.5)
    lane = lax.broadcasted_iota(jnp.int32, (1, 128), 1)
    low = lane < HD
    scaled = (gm[...].astype(F32) * linv[...]).astype(BF16).astype(F32)
    kf, vf = k[...].astype(F32), v[...].astype(F32)
    weighted = scaled * o[...]
    for a in range(2):
        mine = low if a == 0 else jnp.logical_not(low)
        delta = jnp.sum(jnp.where(mine, weighted, 0.0), -1, keepdims=True)
        high = delta.astype(BF16).astype(F32)
        middle = (delta - high).astype(BF16).astype(F32)
        last = delta - high - middle
        base = HD * (1 - a)
        extra = jnp.where(
            lane == base, high, jnp.where(lane == base + 1, middle, jnp.where(lane == base + 2, last, 0.0))
        )
        do[a] = jnp.where(mine, scaled, -extra).astype(BF16)
        va[a] = jnp.where(mine, vf, 1.0).astype(BF16)
        km[a] = jnp.where(mine, kf, 0.0).astype(BF16)
    dot_[...] = scaled.astype(BF16).T
    qt[...] = q[...].T
    steps = [(i, a) for i in range(rows // QB) for a in range(2)]

    def block(i):
        return slice(i * QB, (i + 1) * QB)

    def sub(a):
        return slice(a * HD, (a + 1) * HD)

    def pushed(t):
        i, a = steps[t]
        return nt(do[a, block(i), :], va[a])

    dqs = {}
    grads = pushed(0)
    for t, (i, a) in enumerate(steps):
        if t == len(steps) // 2:
            for run in events[1]:
                run()
        sl = block(i)
        p = e[a, sl, :]
        ds = (p.astype(F32) * grads).astype(BF16)
        grads = pushed(t + 1) if t + 1 < len(steps) else None
        dv = nn(dot_[sub(a), sl], p)
        dk = nn(qt[sub(a), sl], ds)
        dqs[a] = nn(ds, km[a])
        if i == 0:
            dvt[sub(a), :] = dv
            dkt[sub(a), :] = dk
        else:
            dvt[sub(a), :] += dv
            dkt[sub(a), :] += dk
        if a == 1:
            gq_out[sl, :] = ((dqs[0] + dqs[1]) * third).astype(BF16)
    gv_out[...] = dvt[...].astype(BF16).T
    gk_out[...] = (dkt[...] * third).astype(BF16).T

    @pl.when(pair == pairs - 1)
    def _():
        halves[0].crossed()
        ro_out[...] = out.total(oown[...]).astype(BF16)
        halves[1].risen()
        ri_out[0] = aown[...]
        ri_out[1] = bown[...]
        for item in inner + [out]:
            item.finish()


def attend_back(gwi, gwo, ru, q, k, v, gm, o, linv, e, seq):
    rows, mine = q.shape
    pairs = mine // 128
    n_m = gwi.shape[0]
    piece, width = ru.shape
    by_pair = pl.BlockSpec((rows, 128), lambda p: (0, p))
    return pl.pallas_call(
        lambda *refs: attend_back_kernel(seq, pairs, *refs),
        grid=(pairs,),
        in_specs=[ANY] * 3
        + [by_pair] * 6
        + [pl.BlockSpec((2, rows, rows), lambda p: (p, 0, 0))],
        out_specs=[by_pair] * 3
        + [
            pl.BlockSpec(gwi.shape[1:], lambda p: (0, 0, 0)),
            pl.BlockSpec(gwo.shape[1:], lambda p: (0, 0, 0)),
            pl.BlockSpec((piece, width), lambda p: (0, 0)),
        ],
        out_shape=[jax.ShapeDtypeStruct((rows, mine), BF16)] * 3
        + [
            jax.ShapeDtypeStruct(gwi.shape[1:], BF16),
            jax.ShapeDtypeStruct(gwo.shape[1:], BF16),
            jax.ShapeDtypeStruct((piece, width), F32),
        ],
        scratch_shapes=scatter_sems()
        + scatter_sems()
        + scatter_sems()
        + [ACROSS_SEMS] * 3
        + [
            pltpu.VMEM((piece, width), BF16),
            pltpu.VMEM((2, piece, width), BF16),
            pltpu.VMEM(gwi.shape[2:], BF16),
            pltpu.VMEM((2,) + gwi.shape[2:], BF16),
            pltpu.VMEM(gwi.shape[2:], BF16),
            pltpu.VMEM((2,) + gwi.shape[2:], BF16),
            pltpu.VMEM((2, n_m - 1) + gwi.shape[2:], BF16),
            pltpu.VMEM((n_m - 1,) + gwo.shape[1:], BF16),
            pltpu.VMEM(gwo.shape[1:], BF16),
            pltpu.SemaphoreType.DMA((4,)),
            pltpu.VMEM((2, rows, 128), BF16),
            pltpu.VMEM((128, rows), BF16),
            pltpu.VMEM((128, rows), BF16),
            pltpu.VMEM((2, rows, 128), BF16),
            pltpu.VMEM((2, rows, 128), BF16),
            pltpu.VMEM((128, rows), F32),
            pltpu.VMEM((128, rows), F32),
        ],
        compiler_params=pltpu.CompilerParams(
            collective_id=3, has_side_effects=True, vmem_limit_bytes=LIMIT
        ),
        name="attend_back",
    )(gwi, gwo, ru, q, k, v, gm, o, linv, e)


def project_back_kernel(
    seq, x_in, n1_in, gq_in, gk_in, gv_in, gres_in, wqkv_in, vecs, gvec, gib, ri_in, ro_in,
    gwq_out, gwk_out, gwv_out, gwo_out, gwi_out,
    fg_out, fs_out, qb_out, vb_out, ob_out, sg_out, ss_out, ub_out, ib_out, ig_back,
    x, n1, grads, gres, wqkv, gown, gstage, grecv, ig_own, qpart, qgot, vgot,
    ri, ispare, ito, ra, aspare, ato, vown, vspare, vto,
    gsem, grsem, bsend, brecv, qsend, qrecv, vsend, vrecv, zi, za, zv, pair_sems, lsem,
):
    f, z, m, c = where_am_i()
    other = (m * 2 + 1 - c, z)
    half = gres.shape[1]
    chunk = 2 * half
    width = gres.shape[2]
    rows = seq * chunk
    mine = width // 2
    n_m = qpart.shape[1]
    share = ri.shape[1]
    hidden = ri.shape[2]
    piece = hidden // n_m
    loads = [
        pltpu.make_async_copy(src, dst, lsem.at[k])
        for k, (src, dst) in enumerate(
            (
                (gq_in, grads.at[:, :mine]),
                (gk_in, grads.at[:, mine : 2 * mine]),
                (gv_in, grads.at[:, 2 * mine :]),
                (wqkv_in, wqkv),
                (ri_in, ri),
                (ro_in, ra.at[3]),
                (n1_in, n1),
                (gres_in, gres),
                (x_in.at[:, c], x),
            )
        )
    ]
    for item in loads:
        item.start()
    meet(all_peers(seq))
    gain = vecs[0:1, :]
    inner = [Across(ri.at[k], ispare.at[k], zi.at[k]) for k in range(2)]
    parts = [Across(ra.at[k], aspare.at[k], za.at[k]) for k in range(4)]
    vectors = Across(vown, vspare, zv)
    queries = [
        Scatter(lambda to, k=k: qpart.at[k, to], qgot.at[k], qsend.at[k], qrecv.at[k])
        for k in range(3)
    ]
    vspread = Scatter(lambda to: vown, vgot, vsend, vrecv)
    back = Return(ig_own, ig_back, bsend, brecv, seq)

    def g_copy(i):
        return remote(gstage.at[i, 1 - c], grecv.at[i], gsem.at[i], grsem.at[i], other)

    def pass_on(k, src, dst):
        return remote(src, dst, pair_sems.at[0, k], pair_sems.at[1, k], other)

    for item in loads[:6]:
        item.wait()
    inner[0].fall()
    inner[1].cross()
    parts[3].rise()
    for i in range(seq):
        gn1 = nt(grads[i * chunk : (i + 1) * chunk, :], wqkv[...])
        gown[i] = gn1.reshape(2, half, width)
        gstage[i] = gn1.astype(BF16).reshape(2, half, width)
        g_copy(i).start()
    for item in loads[6:]:
        item.wait()

    def weight(k):
        part = tn(n1[...], grads[:, k * mine : (k + 1) * mine])
        for j in range(n_m):
            for b in range(2):
                at = (2 * j + b) * share
                qpart[k, j, b] = part[at : at + share, :].astype(BF16)
        queries[k].start()

    weight(0)
    for k in range(seq):
        g_copy(k).wait_recv()
        gn1 = gown[k, c] + grecv[k].astype(F32)
        hat, inv = normalize(x[k].astype(F32))
        line = jnp.sum(gn1 * hat, 0, keepdims=True)
        flat = jnp.sum(gn1, 0, keepdims=True)
        if k == 0:
            gain_sum, shift_sum = line, flat
        else:
            gain_sum, shift_sum = gain_sum + line, shift_sum + flat
        ig_own[k] = (gres[k] + norm_back(gn1, gain, hat, inv)).astype(BF16)
        back.ships[k].start()
    vown[...] = jnp.zeros_like(vown)
    vown[0:1, :] = gain_sum
    vown[1:2, :] = shift_sum
    cols = pl.ds(pl.multiple_of(c * mine, 128), mine)
    vown[2:3, cols] = jnp.sum(grads[:, :mine].astype(F32), 0, keepdims=True)
    vown[3:4, cols] = jnp.sum(grads[:, 2 * mine :].astype(F32), 0, keepdims=True)
    for k, r in enumerate((3, 1, 2, 0)):
        vown[4 + k : 5 + k, :] = 0.5 * gvec[r : r + 1, :]
    lines = hidden // width
    for k in range(lines):
        vown[pl.ds(8 + lines * c + k, 1), :] = gib[:, k * width : (k + 1) * width]
    vspread.start()
    weight(1)
    parts[3].risen()
    parts[3].cross()
    weight(2)
    inner[1].crossed()
    inner[1].fall()
    total = vspread.total(vown[...])
    vspread.finish()
    vown[...] = total
    vectors.rise()
    parts[3].crossed()
    parts[3].fall()
    for k in range(3):
        ra[k] = queries[k].total(qpart[k, m]).astype(BF16)
        parts[k].rise()
    vectors.risen()
    vectors.cross()
    crosses = {}

    def hand_over(k, src, dst):
        crosses[k] = pass_on(k, src, dst)
        crosses[k].start()

    for k in range(2):
        inner[k].fallen()
        pl.when(c != k)(pass_on(k, ri.at[k], ito).start)
    for k in range(3):
        parts[k].risen()
        parts[k].cross()
    vectors.crossed()
    vectors.fall()
    parts[3].fallen()
    hand_over(5, ra.at[3, 1 - c], ato.at[3])
    for k in range(3):
        parts[k].crossed()
        parts[k].fall()
    vectors.fallen()
    hand_over(6, vown, vto)

    for k in range(2):
        pl.when(c == k)(pass_on(k, ri.at[1 - k], ito).wait_recv)
        pl.when(c != k)(pass_on(k, ri.at[k], ito).wait_send)
    if piece % 128:
        gwi_out[c] = ri[c].astype(F32)
        gwi_out[1 - c] = ito[...].astype(F32)
    else:
        for k in range(n_m):
            cols = slice(k * piece, (k + 1) * piece)
            here = pl.ds(pl.multiple_of((2 * k + c) * piece, 128), piece)
            there = pl.ds(pl.multiple_of((2 * k + 1 - c) * piece, 128), piece)
            gwi_out[:, here] = ri[c, :, cols].astype(F32)
            gwi_out[:, there] = ito[:, cols].astype(F32)
    for k in range(3):
        parts[k].fallen()
        hand_over(2 + k, ra.at[k, 1 - c], ato.at[k])
    here = pl.ds(pl.multiple_of(c * mine, 128), mine)
    there = pl.ds(pl.multiple_of((1 - c) * mine, 128), mine)
    for key, k, out in ((5, 3, gwo_out), (2, 0, gwq_out), (3, 1, gwk_out), (4, 2, gwv_out)):
        crosses[key].wait()
        out[:, here] = ra[k, c].astype(F32)
        out[:, there] = ato[k].astype(F32)
    crosses[6].wait()
    vto[...] = vown[...] + vto[...]
    turned = pltpu.roll(vto[0:8, :], (width - f * share) % width, 1)
    small = (fg_out, fs_out, qb_out, vb_out, ob_out, sg_out, ss_out, ub_out)
    for k, out in enumerate(small):
        out[...] = turned[k : k + 1, :share]
    per = width // piece
    line = jnp.broadcast_to(vto[pl.ds(8 + lines * c + m // per, 1), :], (8, width))
    ib_out[...] = pltpu.roll(line, (width - (m % per) * piece) % width, 1)[0:1, :piece]
    for k in range(seq):
        g_copy(k).wait_send()
    for k in range(3):
        queries[k].finish()
    back.finish()


def project_back(x, n1, gq, gk, gv, gres, wqkv, vecs, gvec, gib, ri, ro):
    seq, _, half, width = x.shape
    _, share, hidden = ri.shape
    rows, mine = gq.shape
    n_m = lax.axis_size("fsdp") // 2
    piece = hidden // n_m
    square = jax.ShapeDtypeStruct((share, width), F32)
    block = (2, share, mine)
    return pl.pallas_call(
        lambda *refs: project_back_kernel(seq, *refs),
        in_specs=[ANY] * 7 + [VMEM] * 3 + [ANY] * 2,
        out_specs=[VMEM] * 14 + [ANY],
        out_shape=[square] * 4
        + [
            jax.ShapeDtypeStruct(
                (2, share, hidden) if piece % 128 else (share, 2 * hidden), F32
            )
        ]
        + [jax.ShapeDtypeStruct((1, share), F32)] * 8
        + [
            jax.ShapeDtypeStruct((1, piece), F32),
            jax.ShapeDtypeStruct((2, 2, half, width), BF16),
        ],
        scratch_shapes=[
            pltpu.VMEM((seq, half, width), BF16),
            pltpu.VMEM((rows, width), BF16),
            pltpu.VMEM((rows, 3 * mine), BF16),
            pltpu.VMEM((seq, half, width), F32),
            pltpu.VMEM(wqkv.shape, BF16),
            pltpu.VMEM((seq, 2, half, width), F32),
            pltpu.VMEM((seq, 2, half, width), BF16),
            pltpu.VMEM((seq, half, width), BF16),
            pltpu.VMEM((seq, half, width), BF16),
            pltpu.VMEM((3, n_m) + block, BF16),
            pltpu.VMEM((3, n_m - 1) + block, BF16),
            pltpu.VMEM((n_m - 1, 16, width), F32),
            pltpu.VMEM((2, share, hidden), BF16),
            pltpu.VMEM((2, 2, share, hidden), BF16),
            pltpu.VMEM((share, hidden), BF16),
            pltpu.VMEM((4,) + block, BF16),
            pltpu.VMEM((4, 2) + block, BF16),
            pltpu.VMEM((4, share, mine), BF16),
            pltpu.VMEM((16, width), F32),
            pltpu.VMEM((2, 16, width), F32),
            pltpu.VMEM((16, width), F32),
            pltpu.SemaphoreType.DMA((seq,)),
            pltpu.SemaphoreType.DMA((seq,)),
        ]
        + RETURN_SEMS(seq)
        + [
            pltpu.SemaphoreType.DMA((3, n_m)),
            pltpu.SemaphoreType.DMA((3, n_m)),
            pltpu.SemaphoreType.DMA((n_m,)),
            pltpu.SemaphoreType.DMA((n_m,)),
            pltpu.SemaphoreType.DMA((2, 6)),
            pltpu.SemaphoreType.DMA((4, 6)),
            ACROSS_SEMS,
            pltpu.SemaphoreType.DMA((2, 7)),
            pltpu.SemaphoreType.DMA((9,)),
        ],
        compiler_params=pltpu.CompilerParams(
            collective_id=4, has_side_effects=True, vmem_limit_bytes=LIMIT
        ),
        name="project_back",
    )(x, n1, gq, gk, gv, gres, wqkv, vecs, gvec, gib, ri, ro)


def per_device(
    frames,
    cotangent,
    valid_slots,
    first_gain,
    first_shift,
    query_weight,
    query_bias,
    key_weight,
    value_weight,
    value_bias,
    output_weight,
    output_bias,
    second_gain,
    second_shift,
    inner_weight,
    inner_bias,
    outer_weight,
    outer_bias,
):
    seq = lax.axis_size("seq")
    n_f = lax.axis_size("fsdp")
    f = lax.axis_index("fsdp")
    m, c = f // 2, f % 2
    slots, local, width = frames.shape
    chunk = -(-local // 128) * 128
    half = chunk // 2
    mine = width // 2
    share = width // n_f
    piece = inner_bias.shape[0]
    hidden = piece * n_f // 2

    keep = valid_slots.astype(BF16)[:, None, None]
    pad = ((0, 0), (0, chunk - local), (0, 0))
    x_send = jnp.pad(frames, pad).reshape(slots, 2, half, width)
    cot_send = jnp.pad(cotangent * keep, pad).reshape(slots, 2, half, width)
    wi_send = inner_weight.reshape(share, n_f // 2, 2, piece).transpose(2, 0, 1, 3)
    wi_send = wi_send.reshape(2, share, hidden)
    vectors = (
        first_gain,
        first_shift,
        query_bias,
        value_bias,
        output_bias,
        second_gain,
        second_shift,
        outer_bias,
    )
    if share % 16 == 0 and piece % 128 == 0:
        wqkv_send = jnp.concatenate(
            [
                w.reshape(share, 2, mine).transpose(1, 0, 2)
                for w in (query_weight, key_weight, value_weight)
            ],
            axis=-1,
        )
        x, n1, q, k, v, wqkv, wo, vecs, ibias = project(
            x_send,
            wqkv_send,
            output_weight,
            [value[None] for value in vectors] + [inner_bias[None]],
            seq,
        )
        wqkv = wqkv.reshape(width, 3 * mine)
        wo = wo.reshape(width, width)
    else:

        def gathered(value, axis=0):
            return lax.all_gather(value, "fsdp", axis=axis, tiled=True)

        def my_columns(value):
            return lax.dynamic_slice_in_dim(value, c * mine, mine, axis=1)

        wqkv = jnp.concatenate(
            [my_columns(gathered(w)) for w in (query_weight, key_weight, value_weight)], axis=1
        )
        wo = gathered(output_weight)
        vecs = gathered(jnp.stack(vectors), 1).astype(F32)
        ibias = gathered(inner_bias).astype(F32).reshape(n_f // 2, 2, piece)
        ibias = lax.dynamic_index_in_dim(ibias, c, 1, keepdims=False).reshape(1, hidden)
        x, n1, q, k, v = project_plain(x_send, wqkv, vecs, seq)

    e, o, linv, mixed, cot, wi = attend(cot_send, wi_send, q, k, v, local, seq)
    wi = wi.reshape(width, hidden)
    out_back, gres, gm, gwo, gwi, ru, gvec, gib = dense(
        x, mixed, cot, wo, wi, outer_weight, vecs, ibias
    )
    gq, gk, gv, ri, ro, gwu = attend_back(gwi, gwo, ru, q, k, v, gm, o, linv, e, seq)
    gwq, gwk, gwv, gwo, gwi, fg, fs, qb, vb, ob, sg, ss, ub, ib, ig_back = project_back(
        x, n1, gq, gk, gv, gres, wqkv, vecs, gvec, gib, ri, ro
    )
    if gwi.ndim == 3:
        gwi = gwi.reshape(2, share, n_f // 2, piece).transpose(1, 2, 0, 3)
        gwi = gwi.reshape(share, 2 * hidden)
    keep32 = valid_slots.astype(F32)[:, None, None]
    outputs = (out_back.reshape(slots, chunk, width)[:, :local].astype(F32) * keep32).astype(BF16)
    input_grad = ig_back.reshape(slots, chunk, width)[:, :local]
    return (
        outputs,
        input_grad,
        fg[0],
        fs[0],
        gwq,
        qb[0],
        gwk,
        gwv,
        vb[0],
        gwo,
        ob[0],
        sg[0],
        ss[0],
        gwi,
        ib[0],
        gwu,
        ub[0],
    )


def solution(mesh):
    rows = P("fsdp", "seq", None)
    vector, matrix = P("fsdp"), P("fsdp", None)
    weights = (
        vector,
        vector,
        matrix,
        vector,
        matrix,
        matrix,
        vector,
        matrix,
        vector,
        vector,
        vector,
        matrix,
        vector,
        matrix,
        vector,
    )
    return jax.shard_map(
        per_device,
        mesh=mesh,
        in_specs=(rows, rows, vector) + weights,
        out_specs=(rows, rows) + weights,
        check_vma=False,
    )
```

time: 340 us -> 297 us (0.87)
  Pallas kernels: 306 us -> 267 us
    pallas_call x4, Pallas kernels: 262 us -> 224 us  [the longest x1 68.2 us: dense(): pl.pallas_call(lambda *refs: dense_kernel(seq, *refs), in_specs=[ANY] * 6...]
    unnamed x40 -> x55, local copies, waits for them, and re-layouts: 8.19 us -> 12.4 us
where the time goes in v3:
time: 297 us; the launch traced here: 294 us
  Pallas kernels  267 us (90%)
  local copies, waits for them, and re-layouts  20.9 us (7%)
  other arithmetic  5.15 us (2%)
    pallas_call x1, Pallas kernels, dense(): pl.pallas_call(lambda *refs: dense_kernel(seq, *refs), in_specs=[ANY] * 6...  68.2 us
    pallas_call x1, Pallas kernels, project_back(): pl.pallas_call(lambda *refs: project_back_kernel(seq, *refs), in_specs=[A...  63.1 us
    pallas_call x1, Pallas kernels, attend_back(): pl.pallas_call(lambda *refs: attend_back_kernel(seq, pairs, *refs), grid=...  58.7 us
    pallas_call x1, Pallas kernels, project(): pl.pallas_call(lambda *refs: project_kernel(seq, *refs), in_specs=[ANY] *...  42.2 us
    pallas_call x1, Pallas kernels, attend(): pl.pallas_call(lambda *refs: attend_kernel(seq, local, pairs, *refs), gri...  34.4 us
    unnamed x55, local copies, waits for them, and re-layouts  12.4 us

profile of v3, /device:TPU:0, one launch (start us, length us, event | category | flops | bytes accessed | tf_op | source)
XLA Modules:
  0.0 294.0 jit_solution(9833776430806325442)
XLA Ops:
  0.7 0.7 fusion
  1.4 1.2 broadcast_in_dim.37.refs_11_
  2.6 0.9 copy.61
  3.6 1.0 bitcast_bitcast_fusion
  4.6 0.8 pad_maximum_fusion.refs_1_
  6.1 1.0 reshape.78.refs_1_
  7.1 1.1 broadcast_multiply_fusion
  8.3 1.1 pad.8.clone
  9.4 0.6 copy-done.3
  10.1 1.1 pad.7.clone
  11.2 42.2 %project.1 = (bf16[4,2,192,768]{3,2,1,0:T(8,128)(2,1)}, bf16[1536,768]{1,0:T(8,128)(2,1)}, bf16[1536,384]{1,0:T(8,128)(2,1)}, bf16[1536,384]{1,0:T(8,128)(2,1)},...) custom-call(bf16[2,2,192,768]{3,2,1,0:T(8,128)(2,1)} %bitcast.43, ...), custom_call_target="tpu_custom_call" | custom-call | tf_op jit(solution)/shard_map/project/pallas_call | solution.py:502
  53.4 34.4 %attend.1 = (bf16[6,1536,1536]{2,1,0:T(8,128)(2,1)}, f32[1536,384]{1,0:T(8,128)}, f32[1536,384]{1,0:T(8,128)}, bf16[2,3,1536,128]{3,2,1,0:T(8,128)(2,1)}, bf16[4...) custom-call(bf16[2,2,192,768]{3,2,1,0:T(8,128)(2,1)} %bitcast.44, bf16[2,96,1536]{2,1,0:T(8,128)(2,1)} %reshape.78.refs_1_, ...), custom_call_target="tpu_custom_call" | custom-call | tf_op jit(solution)/shard_map/attend/pallas_call | solution.py:690
  87.8 68.2 %dense.1 = (bf16[2,2,192,768]{3,2,1,0:T(8,128)(2,1)}, f32[4,192,768]{2,1,0:T(8,128)}, bf16[1536,384]{1,0:T(8,128)(2,1)}, bf16[4,2,96,384]{3,2,1,0:T(8,128)(2,1)}...) custom-call(bf16[4,2,192,768]{3,2,1,0:T(8,128)(2,1)} %get-tuple-element.61., ...), custom_call_target="tpu_custom_call" | custom-call | tf_op jit(solution)/shard_map/dense/pallas_call | solution.py:925
  156.0 58.7 %attend_back.1 = (bf16[1536,384]{1,0:T(8,128)(2,1)}, bf16[1536,384]{1,0:T(8,128)(2,1)}, bf16[1536,384]{1,0:T(8,128)(2,1)}, bf16[2,96,1536]{2,1,0:T(8,128)(2,1)},...) custom-call(bf16[4,2,96,1536]{3,2,1,0:T(8,128)(2,1)} %get-tuple-element.73.refs_0_, ...), custom_call_target="tpu_custom_call" | custom-call | tf_op jit(solution)/shard_map/attend_back/pallas_call | solution.py:1125
  214.9 2.0 multiply_convert_fusion
  216.8 63.1 %project_back.1 = (f32[96,768]{1,0:T(8,128)}, f32[96,768]{1,0:T(8,128)}, f32[96,768]{1,0:T(8,128)}, f32[96,768]{1,0:T(8,128)}, f32[96,3072]{1,0:T(8,128)}, /*ind...) custom-call(bf16[4,2,192,768]{3,2,1,0:T(8,128)(2,1)} %get-tuple-elem, ...), custom_call_target="tpu_custom_call" | custom-call | tf_op jit(solution)/shard_map/project_back/pallas_call | solution.py:1359
  279.9 1.3 slice.9
  281.3 1.9 copy.49
  283.2 0.6 reduce
  283.8 0.5 copy.76
  284.3 0.5 copy.77
  284.9 0.7 copy.78
  285.6 0.5 copy.79
  286.1 0.7 copy.80
  286.8 0.7 copy.81
  287.5 0.5 copy.82
  288.1 0.7 copy.83
  288.8 0.5 copy.84
  289.3 0.5 copy.85
  290.3 1.0 copy.87
  291.3 0.7 copy-done
  292.0 1.0 copy.88
  (43 shorter events, 2.1 us)
Async XLA Ops:
  0.7 4.7 %copy-start.5 = (bf16[96,3072]{1,0:T(8,128)(2,1)S(1)}, bf16[96,3072]{1,0:T(8,128)(2,1)}, u32[]{:S(2)}) copy-start(bf16[96,3072]{1,0:T(8,128)(2,1)} %param.32) | copy-start | bytes 1769476
  5.8 1.3 copy-start.2
  8.3 1.7 copy-start.3
  156.0 58.7 %copy-start.4 = (bf16[2,2,192,768]{3,2,1,0:T(8,128)(2,1)S(1)}, bf16[2,2,192,768]{3,2,1,0:T(8,128)(2,1)}, u32[]{:S(2)}) copy-start(bf16[2,2,192,768]{3,2,1,0:T(8,128)(2,1)} %get-tuple-element.71) | copy-start | bytes 3538948
  281.3 2.0 copy-start.10
  281.3 2.6 copy-start.18
  281.3 3.1 %copy-start.17 = (f32[1,96]{1,0:T(1,128)S(1)}, f32[1,96]{1,0:T(1,128)}, u32[]{:S(2)}) copy-start(f32[1,96]{1,0:T(1,128)} %get-tuple-element.91) | copy-start | bytes 1156
  281.3 3.6 %copy-start.9 = (f32[96,768]{1,0:T(8,128)S(1)}, f32[96,768]{1,0:T(8,128)}, u32[]{:S(2)}) copy-start(f32[96,768]{1,0:T(8,128)} %get-tuple-element.130) | copy-start | bytes 884740
  281.3 4.3 %copy-start.16 = (f32[1,96]{1,0:T(1,128)S(1)}, f32[1,96]{1,0:T(1,128)}, u32[]{:S(2)}) copy-start(f32[1,96]{1,0:T(1,128)} %get-tuple-element.93) | copy-start | bytes 1156
  281.3 4.8 %copy-start.8 = (f32[96,768]{1,0:T(8,128)S(1)}, f32[96,768]{1,0:T(8,128)}, u32[]{:S(2)}) copy-start(f32[96,768]{1,0:T(8,128)} %get-tuple-element.132) | copy-start | bytes 884740
  281.3 5.5 %copy-start.7 = (f32[96,768]{1,0:T(8,128)S(1)}, f32[96,768]{1,0:T(8,128)}, u32[]{:S(2)}) copy-start(f32[96,768]{1,0:T(8,128)} %get-tuple-element.133) | copy-start | bytes 884740
  283.2 4.3 %copy-start.15 = (f32[1,96]{1,0:T(1,128)S(1)}, f32[1,96]{1,0:T(1,128)}, u32[]{:S(2)}) copy-start(f32[1,96]{1,0:T(1,128)} %get-tuple-element.96) | copy-start | bytes 1156
  283.2 4.8 %copy-start.6 = (f32[96,768]{1,0:T(8,128)S(1)}, f32[96,768]{1,0:T(8,128)}, u32[]{:S(2)}) copy-start(f32[96,768]{1,0:T(8,128)} %get-tuple-element.135) | copy-start | bytes 884740
  284.9 3.9 %copy-start.14 = (f32[1,96]{1,0:T(1,128)S(1)}, f32[1,96]{1,0:T(1,128)}, u32[]{:S(2)}) copy-start(f32[1,96]{1,0:T(1,128)} %get-tuple-element.98) | copy-start | bytes 1156
  284.9 4.4 %copy-start.13 = (f32[1,96]{1,0:T(1,128)S(1)}, f32[1,96]{1,0:T(1,128)}, u32[]{:S(2)}) copy-start(f32[1,96]{1,0:T(1,128)} %get-tuple-element.99) | copy-start | bytes 1156
  284.9 4.9 %copy-start.12 = (f32[1,96]{1,0:T(1,128)S(1)}, f32[1,96]{1,0:T(1,128)}, u32[]{:S(2)}) copy-start(f32[1,96]{1,0:T(1,128)} %get-tuple-element.100) | copy-start | bytes 1156
  284.9 5.5 %copy-start.1 = (f32[96,3072]{1,0:T(8,128)S(1)}, f32[96,3072]{1,0:T(8,128)}, u32[]{:S(2)}) copy-start(f32[96,3072]{1,0:T(8,128)} %get-tuple-element.139) | copy-start | bytes 3538948
  290.3 1.7 copy-start
  292.0 1.0 copy-start.11
